TPU v7x, 32 devices: a whole 2x2x4 slice. The times are simulated.
32 devices in a mesh: seq: 8 (over z, x), tensor: 4 (over y, core).
Axes of the slice: x: 2, y: 2, z: 4, core: 2. Of those that a mesh axis runs over, the one named last changes fastest.
Arguments:
- tokens: bfloat16 [4, 1024, 768], P(None, 'seq'), may hold values from -6 to 6
- lengths: int32 [4], replicated, may hold values from 513 to 1024, as said below
- query_weight: bfloat16 [768, 768], P(None, 'tensor'), may hold values from -0.875 to 0.875
- query_bias: float32 [768], P('tensor'), may hold values from -3 to 3
- key_weight: bfloat16 [768, 768], P(None, 'tensor'), may hold values from -0.875 to 0.875
- value_weight: bfloat16 [768, 768], P(None, 'tensor'), may hold values from -0.21875 to 0.21875
- value_bias: float32 [768], P('tensor'), may hold values from -2 to 2
- conv_kernel: float32 [12, 33], P('tensor'), may hold values from -0.6 to 0.6
- out_weight: bfloat16 [768, 768], P('tensor'), may hold values from -0.4375 to 0.4375
- out_bias: float32 [768], replicated, may hold values from -2 to 2
- first_gain: float32 [768], replicated, may hold values from 0.5 to 1.5
- first_shift: float32 [768], replicated, may hold values from -2 to 2
- up_weight: bfloat16 [768, 3072], P(None, 'tensor'), may hold values from -0.21875 to 0.21875
- up_bias: float32 [3072], P('tensor'), may hold values from -3 to 3
- down_weight: bfloat16 [3072, 768], P('tensor'), may hold values from -0.109375 to 0.109375
- down_bias: float32 [768], replicated, may hold values from -2 to 2
- second_gain: float32 [768], replicated, may hold values from 0.5 to 1.5
- second_shift: float32 [768], replicated, may hold values from -2 to 2
- out_grad: bfloat16 [4, 1024, 768], P(None, 'seq'), may hold values from -6 to 6
Outputs:
- output: bfloat16 [4, 1024, 768], P(None, 'seq')
- grad_tokens: float32 [4, 1024, 768], P(None, 'seq')
- grad_query_weight: float32 [768, 768], P('seq', 'tensor')
- grad_query_bias: float32 [768], P('tensor')
- grad_key_weight: float32 [768, 768], P('seq', 'tensor')
- grad_value_weight: float32 [768, 768], P('seq', 'tensor')
- grad_value_bias: float32 [768], P('tensor')
- grad_conv_kernel: float32 [12, 33], P('tensor')
- grad_out_weight: float32 [768, 768], P('tensor', 'seq')
- grad_out_bias: float32 [768], replicated
- grad_first_gain: float32 [768], replicated
- grad_first_shift: float32 [768], replicated
- grad_up_weight: float32 [768, 3072], P('seq', 'tensor')
- grad_up_bias: float32 [3072], P('tensor')
- grad_down_weight: float32 [3072, 768], P('tensor', 'seq')
- grad_down_bias: float32 [768], replicated
- grad_second_gain: float32 [768], replicated
- grad_second_shift: float32 [768], replicated
- proxy_norm: float32 [], replicated
Inputs may be any that keep to these rules, and one draw needn't show every extreme that they name: True lengths of the 4 sequences, each more than half of the bucket of 1024 tokens; in every draw one of them is 1024.
All inputs are finite; a program needn't handle non-finite values.
Results may differ from a plain program's by a relative error of at most 0.018.
The roundings to bfloat16 on the way count: a program that leaves them out, or rounds other values in their place, can miss the bound.
Values may be sent and summed in bfloat16 or wider, within the bound.
A program may use at most 192 MiB of HBM per device.

v0:
```python
import jax
import jax.numpy as jnp
from jax import lax
from jax.sharding import PartitionSpec as P

HEADS = 12
HEAD_DIM = 64
LAND = 64
CONV = 33
NS_ITERS = 6


highest = lax.Precision.HIGHEST
epsilon = 1e-05
negative = -1e30


def joined(x, axis, combine):
    everything = jax.tree.map(lambda part: lax.all_gather(part, axis), x)
    first = jax.tree.map(lambda part: part[0], everything)

    def hop(k, so_far):
        return combine(so_far, jax.tree.map(lambda part: part[k], everything))

    return lax.fori_loop(1, lax.axis_size(axis), hop, first)


def with_halo(block, sides, width):
    for axis, dim in sides:
        count = lax.axis_size(axis)
        forward = [(i, i + 1) for i in range(count - 1)]
        backward = [(target, source) for source, target in forward]
        low = lax.ppermute(
            lax.slice_in_dim(block, block.shape[dim] - width, None, axis=dim), axis, forward
        )
        high = lax.ppermute(lax.slice_in_dim(block, 0, width, axis=dim), axis, backward)
        block = jnp.concatenate([low, block, high], axis=dim)
    return block


def newton_inverse(kernel):
    identity = jnp.eye(kernel.shape[-1], dtype=jnp.float32)
    inverse = jnp.swapaxes(kernel, -1, -2) / jnp.sum(kernel * kernel, axis=(-2, -1), keepdims=True)
    for _ in range(NS_ITERS):
        product = jnp.matmul(kernel, inverse, precision=highest)
        inner_term = jnp.matmul(product, 7.0 * identity - product, precision=highest)
        inner_term = jnp.matmul(product, 15.0 * identity - inner_term, precision=highest)
        inverse = 0.25 * jnp.matmul(inverse, 13.0 * identity - inner_term, precision=highest)
    return inverse


def landmark_core(query_marks, key_marks):
    scores = jnp.einsum(
        "bhjd,bhid->bhji", query_marks, key_marks, precision=highest
    ) * HEAD_DIM ** (-0.5)
    kernel_two = jax.nn.softmax(scores, axis=-1)
    return (kernel_two, newton_inverse(kernel_two))


def normalize(summed, gain_vec, shift_vec):
    middle = jnp.mean(summed, axis=-1, keepdims=True)
    centred = summed - middle
    inverse_std = lax.rsqrt(jnp.mean(centred * centred, axis=-1, keepdims=True) + epsilon)
    normal = centred * inverse_std
    return (normal * gain_vec + shift_vec, normal, inverse_std)


def add_norm(partial_sum, residual, bias_vec, gain_vec, shift_vec):
    summed = lax.psum(partial_sum.astype(jnp.bfloat16), "tensor").astype(jnp.float32)
    return normalize(residual + summed + bias_vec, gain_vec, shift_vec)


def norm_back(grad_hidden, normal, inverse_std, gain_vec):
    grad_normal = grad_hidden * gain_vec
    grad_summed = inverse_std * (
        grad_normal
        - jnp.mean(grad_normal, axis=-1, keepdims=True)
        - normal * jnp.mean(grad_normal * normal, axis=-1, keepdims=True)
    )
    return (grad_summed, jnp.sum(grad_hidden * normal, axis=0), jnp.sum(grad_hidden, axis=0))


def combine_soft(earlier, later):
    top_score = jnp.maximum(earlier[0], later[0])
    weight_first = jnp.exp(earlier[0] - top_score)
    weight_second = jnp.exp(later[0] - top_score)
    return (
        top_score,
        earlier[1] * weight_first + later[1] * weight_second,
        earlier[2] * weight_first[..., None] + later[2] * weight_second[..., None],
    )


def per_device(
    tokens,
    lengths,
    query_weight,
    query_bias,
    key_weight,
    value_weight,
    value_bias,
    conv_kernel,
    out_weight,
    out_bias,
    first_gain,
    first_shift,
    up_weight,
    up_bias,
    down_weight,
    down_bias,
    second_gain,
    second_shift,
    out_grad,
):
    batch, tok_local, width = tokens.shape
    local_width = query_weight.shape[1]
    local_heads = conv_kernel.shape[0]
    head_dim = local_width // local_heads
    score_scale = HEAD_DIM ** (-0.5)
    rows = batch * tok_local
    half_width = CONV // 2
    f32 = jnp.float32
    bf16 = jnp.bfloat16
    position = lax.axis_index("seq") * tok_local + jnp.arange(tok_local, dtype=jnp.int32)
    inside = position[None, :] < lengths[:, None]
    living = inside.astype(f32)
    segment = position[None, :] * LAND // lengths[:, None]
    onehot = (
        (segment[:, :, None] == jnp.arange(LAND, dtype=jnp.int32)[None, None, :])
        & inside[:, :, None]
    ).astype(f32)
    marks_index = jnp.arange(LAND, dtype=jnp.int32)
    upper = ((marks_index[None, :] + 1) * lengths[:, None] + LAND - 1) // LAND
    lower = (marks_index[None, :] * lengths[:, None] + LAND - 1) // LAND
    counts = (upper - lower).astype(f32)
    flat = tokens.reshape(rows, width)
    flat_wide = flat.astype(f32)
    queries = (jnp.dot(flat, query_weight, preferred_element_type=f32) + query_bias).astype(bf16)
    key_vectors = jnp.dot(flat, key_weight, preferred_element_type=f32).astype(bf16)
    values = (
        (jnp.dot(flat, value_weight, preferred_element_type=f32) + value_bias)
        * living.reshape(rows, 1)
    ).astype(bf16)
    query_three = queries.reshape(batch, tok_local, local_width)
    key_three = key_vectors.reshape(batch, tok_local, local_width)
    value_three = values.reshape(batch, tok_local, local_width)
    onehot_low = onehot.astype(bf16)
    query_sum = jnp.einsum("btj,btf->bjf", onehot_low, query_three, preferred_element_type=f32)
    key_sum = jnp.einsum("btj,btf->bjf", onehot_low, key_three, preferred_element_type=f32)
    query_sum, key_sum = lax.psum((query_sum, key_sum), "seq")
    query_marks = (
        (query_sum / counts[:, :, None])
        .reshape(batch, LAND, local_heads, head_dim)
        .transpose(0, 2, 1, 3)
    )
    key_marks = (
        (key_sum / counts[:, :, None])
        .reshape(batch, LAND, local_heads, head_dim)
        .transpose(0, 2, 1, 3)
    )
    (kernel_two, inverse), core_back = jax.vjp(landmark_core, query_marks, key_marks)
    identity = jnp.eye(LAND, dtype=f32)
    deviation = identity - jnp.matmul(kernel_two, inverse, precision=highest)
    proxy_part = jnp.sum(jnp.sqrt(jnp.sum(deviation * deviation, axis=(-2, -1)))) / (batch * HEADS)
    query_heads = query_three.reshape(batch, tok_local, local_heads, head_dim).astype(f32)
    key_heads = key_three.reshape(batch, tok_local, local_heads, head_dim).astype(f32)
    value_heads = value_three.reshape(batch, tok_local, local_heads, head_dim).astype(f32)
    first_scores = (
        jnp.einsum("bthd,bhjd->bhtj", query_heads, key_marks, precision=highest) * score_scale
    )
    kernel_one = jax.nn.softmax(first_scores, axis=-1)
    third_scores = (
        jnp.einsum("bhjd,bthd->bhjt", query_marks, key_heads, precision=highest) * score_scale
    )
    key_alive = inside[:, None, None, :]
    third_scores = jnp.where(key_alive, third_scores, negative)
    local_top = jnp.max(third_scores, axis=-1)
    local_weights = jnp.where(key_alive, jnp.exp(third_scores - local_top[..., None]), 0.0)
    local_total = jnp.sum(local_weights, axis=-1)
    local_mix = jnp.einsum("bhjt,bthd->bhjd", local_weights, value_heads, precision=highest)
    top_score, total_weight, mixed = joined(
        (local_top, local_total, local_mix), "seq", combine_soft
    )
    third_out = mixed / total_weight[..., None]
    carried = jnp.matmul(inverse, third_out, precision=highest)
    nystrom = jnp.einsum("bhtj,bhjd->bthd", kernel_one, carried, precision=highest).reshape(
        batch, tok_local, local_width
    )
    padded_values = with_halo(value_three, (("seq", 1),), half_width)
    kernel_wide = jnp.repeat(conv_kernel, head_dim, axis=0)
    convolved = jnp.zeros((batch, tok_local, local_width), f32)
    for i in range(CONV):
        convolved = (
            convolved + padded_values[:, i : i + tok_local, :].astype(f32) * kernel_wide[:, i]
        )
    attention = (nystrom + convolved).astype(bf16).reshape(rows, local_width)
    out_part = jnp.dot(attention, out_weight, preferred_element_type=f32)
    hidden_one, normal_one, inverse_one = add_norm(
        out_part, flat_wide, out_bias, first_gain, first_shift
    )
    hidden_low = hidden_one.astype(bf16)
    up_value = jnp.dot(hidden_low, up_weight, preferred_element_type=f32) + up_bias
    activated, gelu_back = jax.vjp(lambda z: jax.nn.gelu(z, approximate=False), up_value)
    activated = activated.astype(bf16)
    down_part = jnp.dot(activated, down_weight, preferred_element_type=f32)
    hidden_two, normal_two, inverse_two = add_norm(
        down_part, hidden_one, down_bias, second_gain, second_shift
    )
    output = hidden_two.astype(bf16).reshape(batch, tok_local, width)
    grad_output = out_grad.reshape(rows, width).astype(f32)
    grad_second_total, grad_second_gain, grad_second_shift = norm_back(
        grad_output, normal_two, inverse_two, second_gain
    )
    down_in = grad_second_total.astype(bf16)
    grad_down_bias = jnp.sum(down_in.astype(f32), axis=0)
    grad_down_weight = jnp.einsum("rf,rd->fd", activated, down_in, preferred_element_type=f32)
    grad_activated = jnp.einsum("rd,fd->rf", down_in, down_weight, preferred_element_type=f32)
    up_in = gelu_back(grad_activated)[0].astype(bf16)
    grad_up_bias = jnp.sum(up_in.astype(f32), axis=0)
    grad_up_weight = jnp.einsum("rd,rf->df", hidden_low, up_in, preferred_element_type=f32)
    hidden_part = jnp.einsum("rf,df->rd", up_in, up_weight, preferred_element_type=f32)
    grad_hidden_one = (
        lax.psum(hidden_part.astype(jnp.bfloat16), "tensor").astype(jnp.float32) + grad_second_total
    )
    grad_first_total, grad_first_gain, grad_first_shift = norm_back(
        grad_hidden_one, normal_one, inverse_one, first_gain
    )
    out_in = grad_first_total.astype(bf16)
    grad_out_bias = jnp.sum(out_in.astype(f32), axis=0)
    grad_out_weight = jnp.einsum("rf,rd->fd", attention, out_in, preferred_element_type=f32)
    grad_attention = jnp.einsum(
        "rd,fd->rf", out_in, out_weight, preferred_element_type=f32
    ).reshape(batch, tok_local, local_width)
    padded_grad = with_halo(grad_attention.astype(jnp.bfloat16), (("seq", 1),), half_width).astype(
        grad_attention.dtype
    )
    grad_conv_values = jnp.zeros((batch, tok_local, local_width), f32)
    conv_columns = []
    for i in range(CONV):
        conv_columns.append(
            jnp.sum(
                grad_attention * padded_values[:, i : i + tok_local, :].astype(f32), axis=(0, 1)
            )
        )
        start_index = 2 * half_width - i
        grad_conv_values = (
            grad_conv_values
            + padded_grad[:, start_index : start_index + tok_local, :] * kernel_wide[:, i]
        )
    grad_conv_kernel = (
        jnp.stack(conv_columns, axis=0).reshape(CONV, local_heads, head_dim).sum(axis=-1).T
    )
    grad_nystrom = grad_attention.reshape(batch, tok_local, local_heads, head_dim)
    grad_kernel_one = jnp.einsum("bthd,bhjd->bhtj", grad_nystrom, carried, precision=highest)
    grad_carried_part = jnp.einsum("bhtj,bthd->bhjd", kernel_one, grad_nystrom, precision=highest)
    grad_first_scores = kernel_one * (
        grad_kernel_one - jnp.sum(kernel_one * grad_kernel_one, axis=-1, keepdims=True)
    )
    grad_query_one = (
        jnp.einsum("bhtj,bhjd->bthd", grad_first_scores, key_marks, precision=highest) * score_scale
    )
    grad_key_marks_part = (
        jnp.einsum("bhtj,bthd->bhjd", grad_first_scores, query_heads, precision=highest)
        * score_scale
    )
    grad_carried, grad_key_marks_one = lax.psum((grad_carried_part, grad_key_marks_part), "seq")
    grad_third_out = jnp.matmul(jnp.swapaxes(inverse, -1, -2), grad_carried, precision=highest)
    grad_inverse = jnp.matmul(grad_carried, jnp.swapaxes(third_out, -1, -2), precision=highest)
    grad_query_marks_two, grad_key_marks_two = core_back((jnp.zeros_like(kernel_two), grad_inverse))
    third_prob = local_weights * jnp.exp(local_top - top_score)[..., None] / total_weight[..., None]
    delta_term = jnp.sum(grad_third_out * third_out, axis=-1)
    grad_prob_value = jnp.einsum("bhjd,bthd->bhjt", grad_third_out, value_heads, precision=highest)
    grad_third_scores = third_prob * (grad_prob_value - delta_term[..., None])
    grad_value_three = jnp.einsum("bhjt,bhjd->bthd", third_prob, grad_third_out, precision=highest)
    grad_key_three = (
        jnp.einsum("bhjt,bhjd->bthd", grad_third_scores, query_marks, precision=highest)
        * score_scale
    )
    grad_query_marks_part = (
        jnp.einsum("bhjt,bthd->bhjd", grad_third_scores, key_heads, precision=highest) * score_scale
    )
    grad_query_marks_three = lax.psum(grad_query_marks_part, "seq")
    grad_query_marks = (grad_query_marks_two + grad_query_marks_three) / counts[:, None, :, None]
    grad_key_marks = (grad_key_marks_one + grad_key_marks_two) / counts[:, None, :, None]
    grad_query_marks = grad_query_marks.transpose(0, 2, 1, 3).reshape(batch, LAND, local_width)
    grad_key_marks = grad_key_marks.transpose(0, 2, 1, 3).reshape(batch, LAND, local_width)
    grad_query_seg = jnp.einsum("btj,bjf->btf", onehot, grad_query_marks, precision=highest)
    grad_key_seg = jnp.einsum("btj,bjf->btf", onehot, grad_key_marks, precision=highest)
    query_in = (
        (grad_query_one.reshape(batch, tok_local, local_width) + grad_query_seg)
        .astype(bf16)
        .reshape(rows, local_width)
    )
    key_in = (
        (grad_key_three.reshape(batch, tok_local, local_width) + grad_key_seg)
        .astype(bf16)
        .reshape(rows, local_width)
    )
    value_in = (grad_value_three.reshape(batch, tok_local, local_width) + grad_conv_values).astype(
        bf16
    )
    value_in = jnp.where(inside[:, :, None], value_in, jnp.zeros_like(value_in)).reshape(
        rows, local_width
    )
    grad_query_bias = jnp.sum(query_in.astype(f32), axis=0)
    grad_value_bias = jnp.sum(value_in.astype(f32), axis=0)
    grad_query_weight = jnp.einsum("rd,rf->df", flat, query_in, preferred_element_type=f32)
    grad_key_weight = jnp.einsum("rd,rf->df", flat, key_in, preferred_element_type=f32)
    grad_value_weight = jnp.einsum("rd,rf->df", flat, value_in, preferred_element_type=f32)
    input_part = (
        jnp.einsum("rf,df->rd", query_in, query_weight, preferred_element_type=f32)
        + jnp.einsum("rf,df->rd", key_in, key_weight, preferred_element_type=f32)
        + jnp.einsum("rf,df->rd", value_in, value_weight, preferred_element_type=f32)
    )
    input_sum, proxy_norm = (
        lax.psum(input_part.astype(jnp.bfloat16), "tensor").astype(jnp.float32),
        lax.psum(proxy_part.astype(jnp.bfloat16), "tensor").astype(jnp.float32),
    )
    grad_tokens = (grad_first_total + input_sum).reshape(batch, tok_local, width)
    (
        grad_query_weight,
        grad_key_weight,
        grad_value_weight,
        grad_out_weight,
        grad_up_weight,
        grad_down_weight,
    ) = (
        lax.psum_scatter(grad_query_weight, "seq", scatter_dimension=0, tiled=True),
        lax.psum_scatter(grad_key_weight, "seq", scatter_dimension=0, tiled=True),
        lax.psum_scatter(grad_value_weight, "seq", scatter_dimension=0, tiled=True),
        lax.psum_scatter(grad_out_weight, "seq", scatter_dimension=1, tiled=True),
        lax.psum_scatter(grad_up_weight, "seq", scatter_dimension=0, tiled=True),
        lax.psum_scatter(grad_down_weight, "seq", scatter_dimension=1, tiled=True),
    )
    (
        grad_query_bias,
        grad_value_bias,
        grad_conv_kernel,
        grad_out_bias,
        grad_first_gain,
        grad_first_shift,
        grad_up_bias,
        grad_down_bias,
        grad_second_gain,
        grad_second_shift,
    ) = lax.psum(
        (
            grad_query_bias,
            grad_value_bias,
            grad_conv_kernel,
            grad_out_bias,
            grad_first_gain,
            grad_first_shift,
            grad_up_bias,
            grad_down_bias,
            grad_second_gain,
            grad_second_shift,
        ),
        "seq",
    )
    return (
        output,
        grad_tokens,
        grad_query_weight,
        grad_query_bias,
        grad_key_weight,
        grad_value_weight,
        grad_value_bias,
        grad_conv_kernel,
        grad_out_weight,
        grad_out_bias,
        grad_first_gain,
        grad_first_shift,
        grad_up_weight,
        grad_up_bias,
        grad_down_weight,
        grad_down_bias,
        grad_second_gain,
        grad_second_shift,
        proxy_norm,
    )


def solution(mesh):
    return jax.shard_map(
        per_device,
        mesh=mesh,
        in_specs=(
            P(None, "seq", None),
            P(),
            P(None, "tensor"),
            P("tensor"),
            P(None, "tensor"),
            P(None, "tensor"),
            P("tensor"),
            P("tensor", None),
            P("tensor", None),
            P(),
            P(),
            P(),
            P(None, "tensor"),
            P("tensor"),
            P("tensor", None),
            P(),
            P(),
            P(),
            P(None, "seq", None),
        ),
        out_specs=(
            P(None, "seq", None),
            P(None, "seq", None),
            P("seq", "tensor"),
            P("tensor"),
            P("seq", "tensor"),
            P("seq", "tensor"),
            P("tensor"),
            P("tensor", None),
            P("tensor", "seq"),
            P(),
            P(),
            P(),
            P("seq", "tensor"),
            P("tensor"),
            P("tensor", "seq"),
            P(),
            P(),
            P(),
            P(),
        ),
        check_vma=False,
    )
```

profile of v0, /device:TPU:0, one launch (start us, length us, event | category | flops | bytes accessed | tf_op | source)
XLA Modules:
  0.0 1053.6 jit_solution(2662073800216182806)
XLA Ops:
  12.1 6.2 collective-permute-start
  26.4 68.7 %all-reduce.23.cloned.1.call-done = (f32[4,64,192]{2,1,0:T(8,128)}, f32[4,64,192]{2,1,0:T(8,128)}) async-done(((f32[4,64,192]{2,1,0:T(8,128)}, f32[4,64,192]{2,1,0:T(8,128)}), (f32[4,64,192]{2,1,0:T(8,128)}, f32[4,64,192]{2,1,0:T(8,128)})) %all-reduce.23.cloned.1.call-update) | async-done | bytes 393232 | tf_op jit(solution)/shard_map/psum | solution.py:150
  98.7 30.5 %all-gather = f32[32,3,64]{2,1,0:T(4,128)S(1)} all-gather(f32[4,3,64]{2,1,0:T(4,128)S(1)} %get-tuple-element.422), channel_id=2, replica_groups=mesh['seq'=8,'tensor'=4] {'seq'}, dimensions={0}, use_global_device_ids=true | all-gather | bytes 27648 | tf_op jit(solution)/shard_map/all_gather | solution.py:19
  130.9 30.6 %all-gather.1 = f32[32,3,64]{2,1,0:T(4,128)S(1)} all-gather(f32[4,3,64]{2,1,0:T(4,128)S(1)} %fusion.164), channel_id=3, replica_groups=mesh['seq'=8,'tensor'=4] {'seq'}, dimensions={0}, use_global_device_ids=true | all-gather | bytes 27648 | tf_op jit(solution)/shard_map/all_gather | solution.py:19
  187.9 2.9 all-gather.5.cloned.1.call-done
  191.8 19.1 %while.19 = (s32[]{:T(128)}, f32[4,3,64]{2,1,0:T(4,128)}, f32[4,3,64]{2,1,0:T(4,128)S(1)}, f32[4,3,64,64]{3,2,1,0:T(8,128)S(1)}, f32[8,4,3,64]{3,2,1,0:T(4,128)}...) while((s32[]{:T(128)}, f32[4,3,64]{2,1,0:T(4,128)}, ...), condition=%wide.region_8.9_spmd, body=%wide.region_7.8_spmd.sunk | while | flops 152069 | bytes 620695 | solution.py:25
  215.6 16.8 %fusion.156 = bf16[4,128,192]{1,0,2:T(4,128)(2,1)S(1)} fusion(bf16[4,128,192]{1,0,2:T(4,128)(2,1)S(1)} %copy-done.21, f32[4,128,192]{1,2,0:T(8,128)S(1)} %bitcast.375, f32[192]{0:T(256)S(1)} %bitcast.386, f32[192]{0:T(256)S(1)} %bitcast.388, f32[192]{0:T(256)S(1)} %bitcast.390, f32[192]{0:T(256)S(1)} %bitcast.392, f32[192]{0:T(256)S(1)} %bitcast.394, ...), kind=kLoop, calls=%fused_computation.415 | loop fusion | flops 14548992 | bytes 3982080 | tf_op jit(solution)/shard_map/convert_element_type | solution.py:196
  236.2 31.7 %all-reduce.11.cloned.1.call-done = bf16[512,768]{1,0:T(8,128)(2,1)} async-done(((bf16[512,768]{1,0:T(8,128)(2,1)}), bf16[512,768]{1,0:T(8,128)(2,1)}) %all-reduce.11.cloned.1.call-update) | async-done | bytes 786448 | tf_op jit(solution)/shard_map/psum | solution.py:69
  270.8 5.1 multiply_convert_fusion
  280.5 32.7 %all-reduce.13.cloned.1.call-done = bf16[512,768]{1,0:T(8,128)(2,1)} async-done(((bf16[512,768]{1,0:T(8,128)(2,1)}), bf16[512,768]{1,0:T(8,128)(2,1)}) %all-reduce.13.cloned.1.call-update) | async-done | bytes 786448 | tf_op jit(solution)/shard_map/psum | solution.py:69
  326.9 32.2 %all-reduce.15.cloned.1.call-done = bf16[512,768]{1,0:T(8,128)(2,1)} async-done(((bf16[512,768]{1,0:T(8,128)(2,1)}), bf16[512,768]{1,0:T(8,128)(2,1)}) %all-reduce.15.cloned.1.call-update) | async-done | bytes 786448 | tf_op jit(solution)/shard_map/psum | solution.py:223
  359.1 3.4 multiply_reduce_fusion
  370.9 2.9 multiply_reduce_fusion.8
  373.8 11.2 %fusion.119 = (f32[192]{0:T(256)}, f32[192]{0:T(256)}, f32[192]{0:T(256)}, f32[192]{0:T(256)}, f32[192]{0:T(256)}, /*index=5*/f32[192]{0:T(256)}, f32[192]{0:T(2...) fusion(f32[4,128,192]{1,0,2:T(4,128)S(1)} %reshape.656, ...), kind=kLoop, calls=%fused_computation.329 | loop fusion | flops 4813824 | bytes 3747840 | tf_op jit(solution)/shard_map/reduce_sum | solution.py:241
  385.3 3.5 collective-permute-start.2
  398.2 60.4 %all-reduce.17.cloned.1.call-done = f32[4,3,64,64]{3,2,1,0:T(8,128)} async-done(((f32[4,3,64,64]{3,2,1,0:T(8,128)}), f32[4,3,64,64]{3,2,1,0:T(8,128)}) %all-reduce.17.cloned.1.call-update) | async-done | bytes 196624 | tf_op jit(solution)/shard_map/psum | solution.py:266
  505.0 19.0 %convert_reduce_fusion.4 = (f32[192]{0:T(256)S(1)}, bf16[4,128,192]{1,0,2:T(4,128)(2,1)S(1)}) fusion(f32[192]{0:T(256)} %bitcast.385, f32[4,160,192]{1,0,2:T(4,128)S(1)} %maximum_convert_fusion, f32[192]{0:T(256)} %bitcast.387, f32[192]{0:T(256)} %bitcast.389, f32[192]{0:T(256)} %bitcast.391, f32[192]{0:T(256)} %bitcast.393, f32[192]{0:T(256)} %bitcast.395, ...), kind=kLoop, calls=%fused_computation.402 | loop fusion | flops 6881088 | bytes 13592576 | tf_op jit(solution)/shard_map/reduce_sum | solution.py:306
  524.2 2.9 multiply_reduce_fusion.7
  527.6 70.6 %all-reduce.21.cloned.1.call-done = (f32[4,3,64,64]{2,3,1,0:T(8,128)}, f32[4,3,64,64]{2,3,1,0:T(8,128)}) async-done(((f32[4,3,64,64]{2,3,1,0:T(8,128)}, f32[4,3,64,64]{2,3,1,0:T(8,128)}), (f32[4,3,64,64]{2,3,1,0:T(8,128)}, f32[4,3,64,64]{2,3,1,0:T(8,128)})) %all-reduce.21.cloned.1.call-update) | async-done | bytes 393232 | tf_op jit(solution)/shard_map/psum | solution.py:282
  604.4 2.9 convolution_bitcast_fusion
  615.1 3.4 fusion.252
  621.7 6.4 psum.159
  632.3 6.8 fusion.73
  639.7 9.8 fusion.94
  652.2 36.3 %all-reduce = (f32[192]{0:T(256)}, f32[192]{0:T(256)}, f32[3,33]{0,1:T(8,128)S(1)}, f32[768]{0:T(1024)}, f32[768]{0:T(1024)}, /*index=5*/f32[768]{0:T(1024)}, f3...) all-reduce(f32[192]{0:T(256)S(1)} %get-tuple-element.435, ...), channel_id=1, replica_groups=mesh['seq'=8,'tensor'=4] {'seq'}, use_global_device_ids=true, to_apply=%region_32.33 | all-reduce | flops 5859 | bytes 46872 | tf_op jit(solution)/shard_map/psum | solution.py:346
  689.1 2.9 convert_add_fusion
  692.0 12.3 %reduce-scatter.25.cloned.1.call-done = f32[96,192]{1,0:T(8,128)} async-done(((f32[768,192]{1,0:T(8,128)}), f32[96,192]{1,0:T(8,128)}) %reduce-scatter.25.cloned.1.call-update) | async-done | bytes 73744
  706.0 63.6 %reduce-scatter.23.cloned.1.call-done = f32[96,192]{1,0:T(8,128)} async-done(((f32[768,192]{1,0:T(8,128)}), f32[96,192]{1,0:T(8,128)}) %reduce-scatter.23.cloned.1.call-update) | async-done | bytes 73744
  769.6 65.7 %reduce-scatter.21.cloned.1.call-done = f32[96,192]{1,0:T(8,128)} async-done(((f32[768,192]{1,0:T(8,128)}), f32[96,192]{1,0:T(8,128)}) %reduce-scatter.21.cloned.1.call-update) | async-done | bytes 73744
  835.3 65.3 %reduce-scatter.19.cloned.1.call-done = f32[96,192]{1,0:T(8,128)} async-done(((f32[768,192]{1,0:T(8,128)}), f32[96,192]{1,0:T(8,128)}) %reduce-scatter.19.cloned.1.call-update) | async-done | bytes 73744
  900.6 72.5 %reduce-scatter.17.cloned.1.call-done = f32[768,96]{0,1:T(8,128)} async-done(((f32[768,768]{0,1:T(8,128)}), f32[768,96]{0,1:T(8,128)}) %reduce-scatter.17.cloned.1.call-update) | async-done | bytes 294928 | tf_op jit(solution)/shard_map/reduce_scatter | solution.py:333
  973.1 72.4 %reduce-scatter.15.cloned.1.call-done = f32[96,768]{1,0:T(8,128)} async-done(((f32[768,768]{1,0:T(8,128)}), f32[96,768]{1,0:T(8,128)}) %reduce-scatter.15.cloned.1.call-update) | async-done | bytes 294928 | tf_op jit(solution)/shard_map/reduce_scatter | solution.py:332
  (721 shorter events, 181.5 us)
Async XLA Ops:
  7.2 263.4 %copy-start = (bf16[768,768]{1,0:T(8,128)(2,1)S(1)}, bf16[768,768]{1,0:T(8,128)(2,1)}, u32[]{:S(2)}) copy-start(bf16[768,768]{1,0:T(8,128)(2,1)} %param.33) | copy-start | bytes 3538948
  7.2 87.8 %all-reduce.23.cloned.1.call-start = ((), (), s32[]{:S(2)}) async-start(), calls=%async_computation.19 | async-start | bytes 1048576 | tf_op jit(solution)/shard_map/psum | solution.py:150
  8.2 121.4 %copy-start.122 = (pred[4,128]{1,0:T(4,128)(4,1)}, pred[4,128]{1,0:T(4,128)(4,1)S(1)}, u32[]{:S(2)}) copy-start(pred[4,128]{1,0:T(4,128)(4,1)S(1)} %get-tuple-element.377) | copy-start | bytes 1540
  10.8 14.5 %collective-permute-start.1 = (bf16[4,16,192]{1,0,2:T(4,128)(2,1)}, bf16[4,16,192]{1,0,2:T(4,128)(2,1)}, u32[]{:S(2)}, u32[]{:S(2)}) collective-permute-start(bf16[4,16,192]{1,0,2:T(4,128)(2,1)} %get-tuple-element.384), channel_id=1, source_target_pairs={{4,0},{8,4},{12,8},{16,12},{20,16},{24,20},{28,24},{5,1},{9,5},{13... | collective-permute-start | bytes 73736 | tf_op jit(solution)/shard_map/ppermute | solution.py:36
  12.1 203.1 %collective-permute-start = (bf16[4,16,192]{1,0,2:T(4,128)(2,1)}, bf16[4,16,192]{1,0,2:T(4,128)(2,1)}, u32[]{:S(2)}, u32[]{:S(2)}) collective-permute-start(bf16[4,16,192]{1,0,2:T(4,128)(2,1)} %get-tuple-element.383), channel_id=1, source_target_pairs={{0,4},{4,8},{8,12},{12,16},{16,20},{20,24},{24,28},{1,5},{5,9},{9,... | collective-permute-start | bytes 73736 | tf_op jit(solution)/shard_map/ppermute | solution.py:33
  21.3 169.4 %all-gather.5.cloned.1.call-start = ((), (), s32[]{:S(2)}) async-start(), calls=%async_computation.13 | async-start | bytes 3538944 | tf_op jit(solution)/shard_map/all_gather | solution.py:19
  23.1 74.9 %copy-start.173 = (f32[4,64]{1,0:T(4,128)}, f32[4,64]{1,0:T(4,128)S(1)}, u32[]{:S(2)}) copy-start(f32[4,64]{1,0:T(4,128)S(1)} %fusion.242) | copy-start | bytes 3076
  23.7 142.0 %copy-start.38 = (f32[64,64]{1,0:T(8,128)}, f32[64,64]{1,0:T(8,128)S(1)}, u32[]{:S(2)}) copy-start(f32[64,64]{1,0:T(8,128)S(1)} %get-tuple-element.443) | copy-start | bytes 49156
  24.5 74.2 %copy-start.76 = (bf16[4,128,3,64]{1,0,3,2:T(4,128)(2,1)}, bf16[4,128,3,64]{1,0,3,2:T(4,128)(2,1)S(1)}, u32[]{:S(2)}) copy-start(bf16[4,128,3,64]{1,0,3,2:T(4,128)(2,1)S(1)} %reshape_reshape.12) | copy-start | bytes 589828
  24.6 105.0 %copy-start.101 = (bf16[4,128,3,64]{1,0,3,2:T(4,128)(2,1)}, bf16[4,128,3,64]{1,0,3,2:T(4,128)(2,1)S(1)}, u32[]{:S(2)}) copy-start(bf16[4,128,3,64]{1,0,3,2:T(4,128)(2,1)S(1)} %reshape_reshape.13) | copy-start | bytes 589828
  98.1 64.3 %copy-start.26 = (f32[4,64,192]{1,2,0:T(8,128)}, f32[4,64,192]{1,2,0:T(8,128)S(1)}, u32[]{:S(2)}) copy-start(f32[4,64,192]{1,2,0:T(8,128)S(1)} %copy.328) | copy-start | bytes 589828
  130.9 137.0 %all-reduce.11.cloned.1.call-start = ((), (), s32[]{:S(2)}) async-start(), calls=%async_computation.6 | async-start | bytes 1572864 | tf_op jit(solution)/shard_map/psum | solution.py:69
  234.5 78.8 %all-reduce.13.cloned.1.call-start = ((), (), s32[]{:S(2)}) async-start(), calls=%async_computation.7 | async-start | bytes 1572864 | tf_op jit(solution)/shard_map/psum | solution.py:69
  278.4 80.7 %all-reduce.15.cloned.1.call-start = ((), (), s32[]{:S(2)}) async-start(), calls=%async_computation.8 | async-start | bytes 1572864 | tf_op jit(solution)/shard_map/psum | solution.py:223
  324.3 134.2 %all-reduce.17.cloned.1.call-start = ((), (), s32[]{:S(2)}) async-start(), calls=%async_computation.9 | async-start | bytes 786432 | tf_op jit(solution)/shard_map/psum | solution.py:266
  326.9 35.6 %copy-start.118 = (f32[768]{0:T(1024)S(1)}, f32[768]{0:T(1024)}, u32[]{:S(2)}) copy-start(f32[768]{0:T(1024)} %param.31) | copy-start | bytes 9220
  326.9 35.6 %copy-start.131 = (f32[512]{0:T(512)S(1)}, f32[512]{0:T(512)}, u32[]{:S(2)}) copy-start(f32[512]{0:T(512)} %copy-done.130) | copy-start | bytes 6148
  385.1 213.1 %all-reduce.21.cloned.1.call-start = ((), (), s32[]{:S(2)}) async-start(), calls=%async_computation.18 | async-start | bytes 1572864 | tf_op jit(solution)/shard_map/psum | solution.py:282
  385.3 11.4 %collective-permute-start.2 = (bf16[4,16,192]{1,0,2:T(4,128)(2,1)S(1)}, bf16[4,16,192]{1,0,2:T(4,128)(2,1)S(1)}, u32[]{:S(2)}, u32[]{:S(2)}) collective-permute-start(bf16[4,16,192]{1,0,2:T(4,128)(2,1)S(1)} %get-tuple-element.381), channel_id=1, source_target_pairs={{0,4},{4,8},{8,12},{12,16},{16,20},{20,24},{24,28},{1,5},{5,9},{9,... | collective-permute-start | bytes 73736 | tf_op jit(solution)/shard_map/ppermute | solution.py:33
  388.9 8.8 collective-permute-start.3
  394.2 66.0 %copy-start.37 = (f32[4,3,64,64]{3,2,1,0:T(8,128)S(1)}, f32[4,3,64,64]{3,2,1,0:T(8,128)}, u32[]{:S(2)}) copy-start(f32[4,3,64,64]{3,2,1,0:T(8,128)} %copy-done.36) | copy-start | bytes 589828
  398.2 62.9 %copy-start.19 = (f32[4,3,64,64]{3,2,1,0:T(8,128)S(1)}, f32[4,3,64,64]{3,2,1,0:T(8,128)}, u32[]{:S(2)}) copy-start(f32[4,3,64,64]{3,2,1,0:T(8,128)} %copy-done.18) | copy-start | bytes 589828
  524.1 165.1 %all-reduce.19.cloned.1.call-start = ((), (), s32[]{:S(2)}) async-start(), calls=%async_computation.10 | async-start | bytes 1572864 | tf_op jit(solution)/shard_map/psum | solution.py:316
  524.2 74.0 %copy-start.58 = (f32[4,64,192]{1,2,0:T(8,128)S(1)}, f32[4,64,192]{1,2,0:T(8,128)}, u32[]{:S(2)}) copy-start(f32[4,64,192]{1,2,0:T(8,128)} %copy-done.55) | copy-start | bytes 589828
  524.2 74.0 %copy-start.174 = (f32[4,64]{1,0:T(4,128)S(1)}, f32[4,64]{1,0:T(4,128)}, u32[]{:S(2)}) copy-start(f32[4,64]{1,0:T(4,128)} %copy-done.173) | copy-start | bytes 3076
  604.3 100.0 %reduce-scatter.25.cloned.1.call-start = ((), (), s32[]{:S(2)}) async-start(), calls=%async_computation.17 | async-start | bytes 884736
  607.3 162.3 %reduce-scatter.23.cloned.1.call-start = ((), (), s32[]{:S(2)}) async-start(), calls=%async_computation.16 | async-start | bytes 884736
  609.0 226.3 %reduce-scatter.21.cloned.1.call-start = ((), (), s32[]{:S(2)}) async-start(), calls=%async_computation.15 | async-start | bytes 884736
  611.5 289.1 %reduce-scatter.19.cloned.1.call-start = ((), (), s32[]{:S(2)}) async-start(), calls=%async_computation.14 | async-start | bytes 884736
  615.1 358.0 %reduce-scatter.17.cloned.1.call-start = ((), (), s32[]{:S(2)}) async-start(), calls=%async_computation.12 | async-start | bytes 2654208 | tf_op jit(solution)/shard_map/reduce_scatter | solution.py:333
  618.5 427.0 %reduce-scatter.15.cloned.1.call-start = ((), (), s32[]{:S(2)}) async-start(), calls=%async_computation.11 | async-start | bytes 2654208 | tf_op jit(solution)/shard_map/reduce_scatter | solution.py:332
  688.5 357.0 %copy-start.1 = (bf16[768,768]{1,0:T(8,128)(2,1)S(1)}, bf16[768,768]{1,0:T(8,128)(2,1)}, u32[]{:S(2)}) copy-start(bf16[768,768]{1,0:T(8,128)(2,1)} %param.33) | copy-start | bytes 3538948
  (202 other events, 1237.9 us)
Sparse Core Ops, SparseCore 0:
  21.5 73.5 all-reduce.22
  131.0 59.6 all-gather.4
  234.6 33.2 all-reduce.10
  278.6 34.6 all-reduce.12
  324.4 34.6 all-reduce.14
  385.2 73.2 all-reduce.16
  524.2 73.9 all-reduce.20
  604.4 33.6 all-reduce.18
  641.8 62.5 reduce-scatter.24
  708.1 61.4 reduce-scatter.22
  773.8 61.4 reduce-scatter.20
  839.0 61.5 reduce-scatter.18
  905.1 67.9 reduce-scatter.16
  977.4 68.0 reduce-scatter.14
where the time goes:
time: 1060 us; the launch traced here: 1050 us
  waiting for transfers between devices  655 us (62%)
  matrix products  115 us (11%)
  other arithmetic  112 us (11%)
  blocking collectives  104 us (10%)
  local copies, waits for them, and re-layouts  33.8 us (3%)
  between operations  20.2 us (2%)
  starting transfers between devices  13.2 us (1%)
    unnamed x18, waiting for transfers between devices  207 us
    reduce_scatter x1, waiting for transfers between devices, per_device(): lax.psum_scatter(grad_down_weight, 'seq', scatter_dimension=1, tiled=True)  72.5 us
    reduce_scatter x1, waiting for transfers between devices, per_device(): lax.psum_scatter(grad_up_weight, 'seq', scatter_dimension=0, tiled=True)  72.4 us
    psum x1, waiting for transfers between devices, per_device(): grad_query_marks_three = lax.psum(grad_query_marks_part, 'seq')  70.6 us
    psum x1, waiting for transfers between devices, per_device(): query_sum, key_sum = lax.psum((query_sum, key_sum), 'seq')  68.7 us
    psum x2, waiting for transfers between devices, add_norm(): lax.psum(partial_sum.astype(jnp.bfloat16), 'tensor').astype(jnp.float32)  64.5 us
    all_gather x2, blocking collectives, joined(): everything = jax.tree.map(lambda part: lax.all_gather(part, axis), x)  61.1 us
    psum x1, waiting for transfers between devices, per_device(): lax.psum((grad_carried_part, grad_key_marks_part), 'seq')  60.4 us
  transfers between devices with their start and end apart: 18, of which 15 were waited for; matrix products, arithmetic and copies ran while one was open for 11% of the time, Pallas kernels for 0%

commit v1 on v0

--- a/solution.py
+++ b/solution.py
@@ -1,6 +1,10 @@
+import functools
+
 import jax
 import jax.numpy as jnp
 from jax import lax
+from jax.experimental import pallas as pl
+from jax.experimental.pallas import tpu as pltpu
 from jax.sharding import PartitionSpec as P
 
 HEADS = 12
@@ -91,7 +95,7 @@
     )
 
 
-def per_device(
+def general_plan(
     tokens,
     lengths,
     query_weight,
@@ -381,9 +385,578 @@
     )
 
 
+MESH = pl.DeviceIdType.MESH
+LANES = 2 * HEAD_DIM
+f32 = jnp.float32
+bf16 = jnp.bfloat16
+NN = (1, 0)
+NT = (1, 1)
+TN = (0, 0)
+
+
+def dot(a, b, dims=NN):
+    return lax.dot_general(
+        a, b, (((dims[0],), (dims[1],)), ((), ())), preferred_element_type=f32
+    )
+
+
+def split(x):
+    if x.dtype == bf16:
+        return (x,)
+    top = x.astype(bf16)
+    return (top, (x - top.astype(f32)).astype(bf16))
+
+
+def fine(a, b, dims=NN):
+    a, b = split(a), split(b)
+    total = dot(a[0], b[0], dims)
+    if len(b) > 1:
+        total = total + dot(a[0], b[1], dims)
+    if len(a) > 1:
+        total = total + dot(a[1], b[0], dims)
+    return total
+
+
+def iota(shape, dim):
+    return lax.broadcasted_iota(jnp.int32, shape, dim)
+
+
+def block_mask():
+    shape = (LANES, LANES)
+    return (iota(shape, 0) < HEAD_DIM) == (iota(shape, 1) < HEAD_DIM)
+
+
+def eye():
+    return jnp.where(iota((LANES, LANES), 0) == iota((LANES, LANES), 1), 1.0, 0.0).astype(f32)
+
+
+def block_sums(x, same_head):
+    ones = jnp.where(same_head, 1.0, 0.0).astype(bf16)
+    return jnp.where(same_head, fine(fine(ones, x), ones), 1.0)
+
+
+def taps_matrix(row, tok):
+    return pltpu.roll(jnp.broadcast_to(row, (tok, 2 * tok)), 0, 1, stride=1, stride_axis=0)
+
+
+def taps_row(taps, head, tok):
+    row = taps[pl.ds(head, 1), :]
+    return jnp.concatenate([row, jnp.zeros((1, 2 * tok - CONV), f32)], axis=1)
+
+
+def conv_block(matrices, window):
+    first = fine(matrices[0], window)
+    second = fine(matrices[1], window)
+    return jnp.where(iota(first.shape, 1) < HEAD_DIM, first, second)
+
+
+def greet(n, me, tensor):
+    barrier = pltpu.get_barrier_semaphore()
+    for d in range(1, n):
+        pl.semaphore_signal(
+            barrier, inc=1, device_id=(lax.rem(me + d, n), tensor), device_id_type=MESH
+        )
+    return barrier
+
+
+def paired(y):
+    return y[:, :LANES], jnp.concatenate(
+        [y[:, LANES : LANES + HEAD_DIM], y[:, HEAD_DIM:LANES]], axis=1
+    )
+
+
+def remote(src, dst, send, recv, device):
+    return pltpu.make_async_remote_copy(
+        src_ref=src, dst_ref=dst, send_sem=send, recv_sem=recv, device_id=device,
+        device_id_type=MESH,
+    )
+
+
+def member_rows(length, total):
+    j = iota((LANES, total), 0) % LAND
+    t = iota((LANES, total), 1)
+    inside = (t * LAND >= j * length) & (t * LAND < (j + 1) * length) & (t < length)
+    return jnp.where(inside, 1.0, 0.0).astype(bf16)
+
+
+def member_columns(length, total):
+    j = iota((total, LANES), 1) % LAND
+    t = iota((total, LANES), 0)
+    inside = (t * LAND >= j * length) & (t * LAND < (j + 1) * length) & (t < length)
+    return jnp.where(inside, 1.0, 0.0).astype(bf16)
+
+
+def segment_counts(length):
+    j = iota((LANES, LANES), 0) % LAND
+    upper = ((j + 1) * length + LAND - 1) // LAND
+    lower = (j * length + LAND - 1) // LAND
+    return (upper - lower).astype(f32)
+
+
+def forward_kernel(
+    n, lengths, x, wq, qb, wk, wv, vb, taps,
+    attn, qs, ks, vs, k1, p3, newton, mats, proxy,
+    stage, out_stage, send, recv, out_send, out_recv,
+):
+    me = lax.axis_index("seq")
+    tensor = lax.axis_index("tensor")
+    rows = x.shape[0]
+    batch = n // 2
+    tok = rows // batch
+    total = n * tok
+    half = CONV // 2
+    own, side = me // 2, me % 2
+    scale = HEAD_DIM ** (-0.5)
+    barrier = greet(n, me, tensor)
+
+    copies = []
+    owned = (ks, qs, vs)
+    offsets = (0, 0, half)
+    vs[0:half] = jnp.zeros((half, LANES), bf16)
+    vs[half + total : total + tok] = jnp.zeros((tok - half, LANES), bf16)
+    for i in range(3):
+        y = dot(x[...], (wk, wq, wv)[i][...])
+        if i == 1:
+            y = y + qb[...]
+        if i == 2:
+            y = y + vb[...]
+            pieces = []
+            position = me * tok + iota((tok, y.shape[1]), 0)
+            for b in range(batch):
+                part = y[b * tok : (b + 1) * tok]
+                pieces.append(jnp.where(position < lengths[b], part, 0.0))
+            y = jnp.concatenate(pieces, axis=0)
+        low = y.astype(bf16)
+        stage[i, 0], stage[i, 1] = paired(low)
+        if i == 0:
+            pl.semaphore_wait(barrier, n - 1)
+        here = pl.ds(pl.multiple_of(offsets[i] + me * tok, 16), tok)
+        for d in range(1, n):
+            peer = lax.rem(me + d, n)
+            copy = remote(
+                stage.at[i, peer % 2, pl.ds(pl.multiple_of((peer // 2) * tok, tok), tok)],
+                owned[i].at[here],
+                send.at[i, d - 1],
+                recv.at[i, d - 1],
+                (peer, tensor),
+            )
+            copy.start()
+            copies.append(copy)
+        owned[i][here] = stage[i, side, pl.ds(pl.multiple_of(own * tok, tok), tok)]
+
+    length = lengths[own]
+    same_head = block_mask()
+    identity = eye()
+    ones = jnp.where(same_head, 1.0, 0.0).astype(bf16)
+    members = member_rows(length, total)
+    counts = segment_counts(length)
+    for copy in copies[: n - 1]:
+        copy.wait_recv()
+    keys = ks[...]
+    key_marks = jnp.where(same_head, dot(members, keys) / counts, 0.0)
+    for copy in copies[n - 1 : 2 * (n - 1)]:
+        copy.wait_recv()
+    queries = qs[...]
+    query_marks = jnp.where(same_head, dot(members, queries) / counts, 0.0)
+
+    scores = jnp.where(same_head, fine(query_marks, key_marks, NT) * scale, negative)
+    weights = jnp.exp(scores - jnp.max(scores, axis=1, keepdims=True))
+    kernel_two = weights / jnp.sum(weights, axis=1, keepdims=True)
+    inverse = jnp.where(
+        same_head, kernel_two.T / block_sums(kernel_two * kernel_two, same_head), 0.0
+    )
+    for step in range(NS_ITERS):
+        product = fine(kernel_two, inverse)
+        inner_one = fine(product, 7.0 * identity - product)
+        inner_two = fine(product, 15.0 * identity - inner_one)
+        newton[4 * step] = inverse
+        newton[4 * step + 1] = product
+        newton[4 * step + 2] = inner_one
+        newton[4 * step + 3] = inner_two
+        inverse = 0.25 * fine(inverse, 13.0 * identity - inner_two)
+
+    deviation = identity - fine(kernel_two, inverse)
+    norms = jnp.sqrt(block_sums(deviation * deviation, same_head))
+    proxy[...] = norms
+
+    first_scores = fine(queries, key_marks, NT) * scale
+    left = iota(first_scores.shape, 1) < HEAD_DIM
+    top_left = jnp.max(jnp.where(left, first_scores, negative), axis=1, keepdims=True)
+    top_right = jnp.max(jnp.where(left, negative, first_scores), axis=1, keepdims=True)
+    weights = jnp.exp(first_scores - jnp.where(left, top_left, top_right))
+    kernel_one = weights / fine(weights, ones)
+    k1[...] = kernel_one
+
+    third_scores = fine(keys, query_marks, NT) * scale
+    alive = iota(third_scores.shape, 0) < length
+    third_scores = jnp.where(alive, third_scores, negative)
+    weights = jnp.exp(third_scores - jnp.max(third_scores, axis=0, keepdims=True))
+    weights = jnp.where(alive, weights, 0.0)
+    third_prob = weights / jnp.sum(weights, axis=0, keepdims=True)
+    p3[...] = third_prob
+
+    for copy in copies[2 * (n - 1) :]:
+        copy.wait_recv()
+    values = vs[half : half + total]
+    third_out = jnp.where(same_head, fine(third_prob, values, TN), 0.0)
+    carried = fine(inverse, third_out)
+    mats[0] = query_marks
+    mats[1] = key_marks
+    mats[2] = kernel_two
+    mats[3] = inverse
+    mats[4] = third_out
+    mats[5] = carried
+
+    matrices = [taps_matrix(taps_row(taps, h, tok), tok) for h in (2 * side, 1)]
+    there = pl.ds(pl.multiple_of(own * tok, tok), tok)
+    for d in range(1, n + 1):
+        peer = lax.rem(me + d, n)
+        start = pl.multiple_of(peer * tok, tok)
+        nystrom = fine(k1[pl.ds(start, tok)], carried)
+        convolved = conv_block(matrices, vs[pl.ds(start, 2 * tok)])
+        low = (nystrom + convolved).astype(bf16)
+        if d == n:
+            attn[side, there] = low
+        else:
+            out_stage[d - 1] = low
+            copy = remote(
+                out_stage.at[d - 1],
+                attn.at[side, there],
+                out_send.at[d - 1],
+                out_recv.at[d - 1],
+                (peer, tensor),
+            )
+            copy.start()
+            copies.append(copy)
+    for copy in copies[: 3 * (n - 1)]:
+        copy.wait_send()
+    for copy in copies[3 * (n - 1) :]:
+        copy.wait()
+
+
+def backward_kernel(
+    n, lengths, out_in, out_weight, taps, qs, ks, vs, k1, p3, newton, mats,
+    rin, conv_grad,
+    stage, gs, out_stage, send, recv, out_send, out_recv,
+):
+    me = lax.axis_index("seq")
+    tensor = lax.axis_index("tensor")
+    rows = out_in.shape[0]
+    batch = n // 2
+    tok = rows // batch
+    total = n * tok
+    half = CONV // 2
+    own, side = me // 2, me % 2
+    scale = HEAD_DIM ** (-0.5)
+    barrier = greet(n, me, tensor)
+
+    gs[0:half] = jnp.zeros((half, LANES), bf16)
+    gs[half + total : total + tok] = jnp.zeros((tok - half, LANES), bf16)
+    grad = dot(out_in[...], out_weight[...], NT).astype(bf16)
+    stage[0], stage[1] = paired(grad)
+    pl.semaphore_wait(barrier, n - 1)
+    here = pl.ds(pl.multiple_of(half + me * tok, 16), tok)
+    copies = []
+    for d in range(1, n):
+        peer = lax.rem(me + d, n)
+        copy = remote(
+            stage.at[peer % 2, pl.ds(pl.multiple_of((peer // 2) * tok, tok), tok)],
+            gs.at[here],
+            send.at[d - 1],
+            recv.at[d - 1],
+            (peer, tensor),
+        )
+        copy.start()
+        copies.append(copy)
+    gs[here] = stage[side, pl.ds(pl.multiple_of(own * tok, tok), tok)]
+
+    length = lengths[own]
+    same_head = block_mask()
+    identity = eye()
+    ones = jnp.where(same_head, 1.0, 0.0).astype(bf16)
+    members = member_columns(length, total)
+    counts = segment_counts(length)
+    query_marks, key_marks, kernel_two, inverse, third_out, carried = [mats[i] for i in range(6)]
+    matrices = [taps_matrix(taps_row(taps, h, tok), tok) for h in (2 * side, 1)]
+    flip = jnp.where(
+        iota((2 * tok, 2 * tok), 0) + iota((2 * tok, 2 * tok), 1) == CONV - 1, 1.0, 0.0
+    ).astype(bf16)
+    reverse = [
+        taps_matrix(
+            fine(jnp.broadcast_to(taps_row(taps, h, tok), (8, 2 * tok)), flip)[0:1], tok
+        )
+        for h in (2 * side, 1)
+    ]
+    queries, keys, values = qs[...], ks[...], vs[half : half + total]
+    for copy in copies:
+        copy.wait_recv()
+
+    grad = gs[half : half + total]
+    kernel_one = k1[...]
+    grad_carried = jnp.where(same_head, fine(kernel_one, grad, TN), 0.0)
+    grad_third = fine(inverse, grad_carried, TN)
+    grad_inverse = fine(grad_carried, third_out, NT)
+
+    third_prob = p3[...]
+    grad_values = fine(third_prob, grad_third)
+    alive = iota((tok, LANES), 0)
+    outs = []
+
+    return_blocks = {}
+    full = []
+    for m in range(n):
+        block = grad_values[m * tok : (m + 1) * tok] + conv_block(
+            reverse, gs[m * tok : (m + 2) * tok]
+        )
+        full.append(jnp.where(alive + m * tok < length, block, 0.0))
+    return_blocks[2] = jnp.concatenate(full, axis=0)
+
+    kernel_back = jnp.zeros((LANES, LANES), f32)
+    grad_state = grad_inverse
+    for step in reversed(range(NS_ITERS)):
+        state, product, inner_one, inner_two = [newton[4 * step + i] for i in range(4)]
+        grad_next = 0.25 * fine(grad_state, 13.0 * identity - inner_two, NT)
+        grad_two = -0.25 * fine(state, grad_state, TN)
+        grad_product = fine(grad_two, 15.0 * identity - inner_one, NT)
+        grad_one = -fine(product, grad_two, TN)
+        grad_product = (
+            grad_product
+            + fine(grad_one, 7.0 * identity - product, NT)
+            - fine(product, grad_one, TN)
+        )
+        grad_state = grad_next + fine(kernel_two, grad_product, TN)
+        kernel_back = kernel_back + fine(grad_product, state, NT)
+    squares = block_sums(kernel_two * kernel_two, same_head)
+    spread = jnp.where(same_head, block_sums(grad_state * newton[0], same_head), 0.0)
+    kernel_back = kernel_back + (grad_state.T - 2.0 * kernel_two * spread) / squares
+    grad_scores = scale * kernel_two * (
+        kernel_back - jnp.sum(kernel_two * kernel_back, axis=1, keepdims=True)
+    )
+    query_two = fine(grad_scores, key_marks)
+    key_two = fine(grad_scores, query_marks, TN)
+
+    grad_one = fine(grad, carried, NT)
+    both = kernel_one * grad_one
+    first_scores = scale * (both - kernel_one * fine(both, ones))
+    key_one = jnp.where(same_head, fine(first_scores, queries, TN), 0.0)
+    delta = fine(jnp.ones((8, LANES), bf16), grad_third * third_out, NT)[0:1]
+    third_scores = scale * third_prob * (fine(values, grad_third, NT) - delta)
+    query_three = jnp.where(same_head, fine(third_scores, keys, TN), 0.0)
+    return_blocks[0] = fine(third_scores, query_marks) + fine(
+        members, (key_one + key_two) / counts
+    )
+    return_blocks[1] = fine(first_scores, key_marks) + fine(
+        members, (query_two + query_three) / counts
+    )
+    for i in (2, 0, 1):
+        low = return_blocks[i].astype(bf16)
+        for m in range(n):
+            out_stage[i, m] = low[m * tok : (m + 1) * tok]
+        there = pl.ds(pl.multiple_of(own * tok, tok), tok)
+        for d in range(1, n):
+            peer = lax.rem(me + d, n)
+            copy = remote(
+                out_stage.at[i, peer],
+                rin.at[i, side, there],
+                out_send.at[i, d - 1],
+                out_recv.at[i, d - 1],
+                (peer, tensor),
+            )
+            copy.start()
+            outs.append(copy)
+        rin[i, side, there] = out_stage[i, me]
+
+    position = iota((tok, tok), 0) + iota((tok, tok), 1)
+    upside = jnp.where(position == tok - 1, 1.0, 0.0).astype(bf16)
+    lane = iota((tok, LANES), 1)
+    for h in range(2):
+        mine = (lane < HEAD_DIM) if h == 0 else (lane >= HEAD_DIM)
+        table = jnp.zeros((tok, 2 * tok), f32)
+        for m in range(n):
+            block = gs[half + m * tok : half + (m + 1) * tok]
+            block = jnp.where(mine, block, jnp.zeros_like(block))
+            table = table + dot(block, vs[m * tok : (m + 2) * tok], NT)
+        table = pltpu.roll(fine(upside, table), 0, 1, stride=1, stride_axis=0)
+        row = jnp.sum(table, axis=0, keepdims=True)
+        row = pltpu.roll(jnp.broadcast_to(row, (8, 2 * tok)), tok + 1, 1)
+        conv_grad[h] = row
+    for copy in copies:
+        copy.wait_send()
+    for copy in outs:
+        copy.wait()
+
+
+def whole(shape, dtype):
+    return jax.ShapeDtypeStruct(shape, dtype)
+
+
+VMEM = pl.BlockSpec(memory_space=pltpu.VMEM)
+SMEM = pl.BlockSpec(memory_space=pltpu.SMEM)
+
+
+def attention_forward(n, lengths, flat, wq, qb, wk, wv, vb, taps):
+    rows = flat.shape[0]
+    tok = rows // (n // 2)
+    total = n * tok
+    return pl.pallas_call(
+        functools.partial(forward_kernel, n),
+        out_shape=(
+            whole((2, rows, LANES), bf16),
+            whole((total, LANES), bf16),
+            whole((total, LANES), bf16),
+            whole((total + tok, LANES), bf16),
+            whole((total, LANES), f32),
+            whole((total, LANES), f32),
+            whole((4 * NS_ITERS, LANES, LANES), f32),
+            whole((6, LANES, LANES), f32),
+            whole((LANES, LANES), f32),
+        ),
+        in_specs=[SMEM] + [VMEM] * 7,
+        out_specs=(VMEM,) * 9,
+        scratch_shapes=[
+            pltpu.VMEM((3, 2, rows, LANES), bf16),
+            pltpu.VMEM((n - 1, tok, LANES), bf16),
+            pltpu.SemaphoreType.DMA((3, n - 1)),
+            pltpu.SemaphoreType.DMA((3, n - 1)),
+            pltpu.SemaphoreType.DMA((n - 1,)),
+            pltpu.SemaphoreType.DMA((n - 1,)),
+        ],
+        compiler_params=pltpu.CompilerParams(
+            collective_id=0, has_side_effects=True, vmem_limit_bytes=48 * 2**20
+        ),
+        name="attention_forward",
+    )(lengths, flat, wq, qb, wk, wv, vb, taps)
+
+
+def attention_backward(n, lengths, out_in, out_weight, taps, saved):
+    rows = out_in.shape[0]
+    tok = rows // (n // 2)
+    total = n * tok
+    return pl.pallas_call(
+        functools.partial(backward_kernel, n),
+        out_shape=(whole((3, 2, rows, LANES), bf16), whole((2, 8, 2 * tok), f32)),
+        in_specs=[SMEM] + [VMEM] * 10,
+        out_specs=(VMEM,) * 2,
+        scratch_shapes=[
+            pltpu.VMEM((2, rows, LANES), bf16),
+            pltpu.VMEM((total + tok, LANES), bf16),
+            pltpu.VMEM((3, n, tok, LANES), bf16),
+            pltpu.SemaphoreType.DMA((n - 1,)),
+            pltpu.SemaphoreType.DMA((n - 1,)),
+            pltpu.SemaphoreType.DMA((3, n - 1)),
+            pltpu.SemaphoreType.DMA((3, n - 1)),
+        ],
+        compiler_params=pltpu.CompilerParams(
+            collective_id=1, has_side_effects=True, vmem_limit_bytes=48 * 2**20
+        ),
+        name="attention_backward",
+    )(lengths, out_in, out_weight, taps, *saved)
+
+
+def gathered_plan(
+    n, tokens, lengths, query_weight, query_bias, key_weight, value_weight, value_bias,
+    conv_kernel, out_weight, out_bias, first_gain, first_shift, up_weight, up_bias, down_weight,
+    down_bias, second_gain, second_shift, out_grad,
+):
+    batch, tok, width = tokens.shape
+    rows = batch * tok
+    flat = tokens.reshape(rows, width)
+    flat_wide = flat.astype(f32)
+    attn, *saved, proxy = attention_forward(
+        n, lengths, flat, query_weight, query_bias[None], key_weight, value_weight,
+        value_bias[None], conv_kernel,
+    )
+    side = lax.axis_index("seq") % 2
+    proxy_part = jnp.where(side == 0, proxy[0, 0] + proxy[-1, -1], proxy[0, 0]) / (batch * HEADS)
+    attention = jnp.concatenate([attn[0], attn[1, :, :HEAD_DIM]], axis=1)
+    out_part = jnp.dot(attention, out_weight, preferred_element_type=f32)
+    hidden_one, normal_one, inverse_one = add_norm(
+        out_part, flat_wide, out_bias, first_gain, first_shift
+    )
+    hidden_low = hidden_one.astype(bf16)
+    up_value = jnp.dot(hidden_low, up_weight, preferred_element_type=f32) + up_bias
+    activated, gelu_back = jax.vjp(lambda z: jax.nn.gelu(z, approximate=False), up_value)
+    activated = activated.astype(bf16)
+    down_part = jnp.dot(activated, down_weight, preferred_element_type=f32)
+    hidden_two, normal_two, inverse_two = add_norm(
+        down_part, hidden_one, down_bias, second_gain, second_shift
+    )
+    output = hidden_two.astype(bf16).reshape(batch, tok, width)
+    grad_output = out_grad.reshape(rows, width).astype(f32)
+    grad_second_total, grad_second_gain, grad_second_shift = norm_back(
+        grad_output, normal_two, inverse_two, second_gain
+    )
+    down_in = grad_second_total.astype(bf16)
+    grad_down_bias = jnp.sum(down_in.astype(f32), axis=0)
+    grad_down_weight = jnp.einsum("rf,rd->fd", activated, down_in, preferred_element_type=f32)
+    grad_activated = jnp.einsum("rd,fd->rf", down_in, down_weight, preferred_element_type=f32)
+    up_in = gelu_back(grad_activated)[0].astype(bf16)
+    grad_up_bias = jnp.sum(up_in.astype(f32), axis=0)
+    grad_up_weight = jnp.einsum("rd,rf->df", hidden_low, up_in, preferred_element_type=f32)
+    hidden_part = jnp.einsum("rf,df->rd", up_in, up_weight, preferred_element_type=f32)
+    grad_hidden_one = (
+        lax.psum(hidden_part.astype(bf16), "tensor").astype(f32) + grad_second_total
+    )
+    grad_first_total, grad_first_gain, grad_first_shift = norm_back(
+        grad_hidden_one, normal_one, inverse_one, first_gain
+    )
+    out_in = grad_first_total.astype(bf16)
+    grad_out_bias = jnp.sum(out_in.astype(f32), axis=0)
+    grad_out_weight = jnp.einsum("rf,rd->fd", attention, out_in, preferred_element_type=f32)
+    rin, conv_grad = attention_backward(n, lengths, out_in, out_weight, conv_kernel, saved)
+    first, second = conv_grad[0, 0, :CONV], conv_grad[1, 0, :CONV]
+    nothing = jnp.zeros_like(first)
+    grad_conv_kernel = jnp.where(
+        side == 0, jnp.stack([first, second, nothing]), jnp.stack([nothing, nothing, first])
+    )
+    key_in, query_in, value_in = [
+        jnp.concatenate([rin[i, 0], rin[i, 1, :, :HEAD_DIM]], axis=1) for i in range(3)
+    ]
+    grad_query_bias = jnp.sum(query_in.astype(f32), axis=0)
+    grad_value_bias = jnp.sum(value_in.astype(f32), axis=0)
+    grad_query_weight = jnp.einsum("rd,rf->df", flat, query_in, preferred_element_type=f32)
+    grad_key_weight = jnp.einsum("rd,rf->df", flat, key_in, preferred_element_type=f32)
+    grad_value_weight = jnp.einsum("rd,rf->df", flat, value_in, preferred_element_type=f32)
+    input_part = (
+        jnp.einsum("rf,df->rd", query_in, query_weight, preferred_element_type=f32)
+        + jnp.einsum("rf,df->rd", key_in, key_weight, preferred_element_type=f32)
+        + jnp.einsum("rf,df->rd", value_in, value_weight, preferred_element_type=f32)
+    )
+    input_sum = lax.psum(input_part.astype(bf16), "tensor").astype(f32)
+    proxy_norm = lax.psum(proxy_part, ("seq", "tensor"))
+    grad_tokens = (grad_first_total + input_sum).reshape(batch, tok, width)
+    scattered = [
+        lax.psum_scatter(g, "seq", scatter_dimension=dim, tiled=True)
+        for g, dim in (
+            (grad_query_weight, 0), (grad_key_weight, 0), (grad_value_weight, 0),
+            (grad_out_weight, 1), (grad_up_weight, 0), (grad_down_weight, 1),
+        )
+    ]
+    summed = lax.psum(
+        (
+            grad_query_bias, grad_value_bias, grad_conv_kernel, grad_out_bias, grad_first_gain,
+            grad_first_shift, grad_up_bias, grad_down_bias, grad_second_gain, grad_second_shift,
+        ),
+        "seq",
+    )
+    return (
+        output, grad_tokens, scattered[0], summed[0], scattered[1], scattered[2], summed[1],
+        summed[2], scattered[3], summed[3], summed[4], summed[5], scattered[4], summed[6],
+        scattered[5], summed[7], summed[8], summed[9], proxy_norm,
+    )
+
+
+def per_device(seq, tensor, *args):
+    batch, tok, _ = args[0].shape
+    local_heads = args[7].shape[0]
+    if seq == 2 * batch and local_heads == 3 and tok % 128 == 0:
+        return gathered_plan(seq, *args)
+    return general_plan(*args)
+
+
 def solution(mesh):
     return jax.shard_map(
-        per_device,
+        functools.partial(per_device, mesh.shape["seq"], mesh.shape["tensor"]),
         mesh=mesh,
         in_specs=(
             P(None, "seq", None),

time: 1060 us -> 677 us (0.64)
  waiting for transfers between devices: 655 us -> 445 us
  other arithmetic: 112 us -> 16 us
  matrix products: 115 us -> 25.5 us
  Pallas kernels: 0 us -> 70.5 us
  blocking collectives: 104 us -> 78.2 us
  starting transfers between devices: 13.2 us -> 0.82 us
  local copies, waits for them, and re-layouts: 33.8 us -> 23 us
    psum x5 -> x2, waiting for transfers between devices: 232 us -> 34.8 us  [the longest x1 34.8 us: gathered_plan(): lax.psum(hidden_part.astype(bf16), 'tensor').astype(f32) + grad_second_total]
    dot_general x112 -> x13, matrix products: 113 us -> 23.1 us  [the longest x1 5.13 us: gathered_plan(): jnp.dot(hidden_low, up_weight, preferred_element_type=f32) + up_bias]
    pallas_call x0 -> x2, Pallas kernels: none -> 70.5 us  [the longest x1 35.7 us: attention_forward(): pl.pallas_call(functools.partial(forward_kernel, n), out_shape=(whole((2,...]
    all_gather x2 -> x0, blocking collectives: 61.1 us -> none  [joined(): everything = jax.tree.map(lambda part: lax.all_gather(part, axis), x)]
    reduce_sum x10 -> x3, other arithmetic: 51 us -> 2.44 us  [the longest x1 2.23 us: gathered_plan(): grad_out_bias = jnp.sum(out_in.astype(f32), axis=0)]
    psum x2, blocking collectives: 42.7 us -> 78.2 us  [the longest x1 41 us: gathered_plan(): proxy_norm = lax.psum(proxy_part, ('seq', 'tensor'))]
    add x17 -> x1, other arithmetic: 21.9 us -> 2.92 us  [gathered_plan(): grad_tokens = (grad_first_total + input_sum).reshape(batch, tok, width)]
    convert_element_type x5 -> x0, other arithmetic: 18.3 us -> none  [the longest x1 16.8 us: per_device(): attention = (nystrom + convolved).astype(bf16).reshape(rows, local_width)]
  transfers between devices with their start and end apart: 18 -> 10, of which waited for: 15 -> 9; matrix products, arithmetic and copies ran while one was open for 11% -> 3% of each run, Pallas kernels for 0% -> 0%
where the time goes in v1:
time: 677 us; the launch traced here: 676 us
  waiting for transfers between devices  445 us (66%)
  blocking collectives  78.2 us (12%)
  Pallas kernels  70.5 us (10%)
  matrix products  25.5 us (4%)
  local copies, waits for them, and re-layouts  23 us (3%)
  between operations  16.7 us (2%)
  other arithmetic  16 us (2%)
    unnamed x14, waiting for transfers between devices  197 us
    reduce_scatter x2, waiting for transfers between devices, gathered_plan(): lax.psum_scatter(g, 'seq', scatter_dimension=dim, tiled=True)  144 us
    psum x2, waiting for transfers between devices, add_norm(): lax.psum(partial_sum.astype(jnp.bfloat16), 'tensor').astype(jnp.float32)  69.7 us
    psum x1, blocking collectives, gathered_plan(): proxy_norm = lax.psum(proxy_part, ('seq', 'tensor'))  41 us
    psum x1, blocking collectives, gathered_plan(): lax.psum((grad_query_bias, grad_value_bias, grad_conv_kernel, grad_out_bi...  37.3 us
    pallas_call x1, Pallas kernels, attention_forward(): pl.pallas_call(functools.partial(forward_kernel, n), out_shape=(whole((2,...  35.7 us
    psum x1, waiting for transfers between devices, gathered_plan(): lax.psum(hidden_part.astype(bf16), 'tensor').astype(f32) + grad_second_total  34.8 us
    pallas_call x1, Pallas kernels, attention_backward(): pl.pallas_call(functools.partial(backward_kernel, n), out_shape=(whole((3...  34.8 us
  transfers between devices with their start and end apart: 10, of which 9 were waited for; matrix products, arithmetic and copies ran while one was open for 3% of the time, Pallas kernels for 0%

profile of v1, /device:TPU:0, one launch (start us, length us, event | category | flops | bytes accessed | tf_op | source)
XLA Modules:
  0.0 676.1 jit_solution(1116790850322478480)
XLA Ops:
  7.3 1.3 copy.44.wq
  9.7 1.2 copy.46.wv
  10.9 35.7 %attention_forward.1 = (bf16[2,512,128]{2,1,0:T(8,128)(2,1)S(1)}, bf16[1024,128]{1,0:T(8,128)(2,1)S(1)}, bf16[1024,128]{1,0:T(8,128)(2,1)S(1)}, bf16[1152,128]{1...) custom-call(s32[4]{0:T(128)S(1)} %copy-done.18, ...), custom_call_target="tpu_custom_call" | custom-call | tf_op jit(solution)/shard_map/attention_forward/pallas_call | solution.py:801
  53.7 1.2 convolution_convert_fusion.2
  55.0 35.4 %all-reduce.7.cloned.1.call-done = bf16[512,768]{1,0:T(8,128)(2,1)} async-done(((bf16[512,768]{1,0:T(8,128)(2,1)}), bf16[512,768]{1,0:T(8,128)(2,1)}) %all-reduce.7.cloned.1.call-update) | async-done | bytes 786448 | tf_op jit(solution)/shard_map/psum | solution.py:73
  90.4 1.5 fusion.14
  93.2 5.1 multiply_convert_fusion
  99.2 1.7 convolution_convert_fusion.1
  101.5 34.2 %all-reduce.9.cloned.1.call-done = bf16[512,768]{1,0:T(8,128)(2,1)} async-done(((bf16[512,768]{1,0:T(8,128)(2,1)}), bf16[512,768]{1,0:T(8,128)(2,1)}) %all-reduce.9.cloned.1.call-update) | async-done | bytes 786448 | tf_op jit(solution)/shard_map/psum | solution.py:73
  135.8 2.0 fusion.35
  138.9 1.5 fusion.4
  141.5 1.8 convert_reduce_fusion.2
  144.2 1.7 convolution_convert_fusion
  146.0 34.8 %all-reduce.11.cloned.1.call-done = bf16[512,768]{1,0:T(8,128)(2,1)} async-done(((bf16[512,768]{1,0:T(8,128)(2,1)}), bf16[512,768]{1,0:T(8,128)(2,1)}) %all-reduce.11.cloned.1.call-update) | async-done | bytes 786448 | tf_op jit(solution)/shard_map/psum | solution.py:898
  180.8 3.3 multiply_reduce_fusion
  184.5 2.2 convert_reduce_fusion.3
  187.1 34.8 %attention_backward.1 = (bf16[3,2,512,128]{3,2,1,0:T(8,128)(2,1)S(1)}, f32[2,8,256]{2,1,0:T(8,128)S(1)}) custom-call(s32[4]{0:T(128)S(1)} %copy-done.18, bf16[512,768]{1,0:T(8,128)(2,1)S(1)} %get-tuple-element.99.out_in, bf16[192,768]{1,0:T(8,128)(2,1)S(1)} %copy-done.4, f32[3,33]{1,0:T(4,128)S(1)} %copy-done.17, bf16[1024,128]{1,0:T(8,128)(2,1)S(1)} %copy-done.14, ...), custom_call_target="tpu_custom_call" | custom-call | tf_op jit(solution)/shard_map/attention_backward/pallas_call | solution.py:835
  224.2 1.3 add_convert_fusion
  225.6 2.3 convolution_bitcast_fusion
  228.1 1.3 convolution_bitcast_fusion.2
  234.1 3.9 fusion.15
  239.1 3.7 fusion.28
  245.3 41.0 %psum.119 = f32[]{:T(128)} all-reduce(f32[]{:T(128)S(6)} %div.38), channel_id=1, replica_groups=mesh['seq'=8,'tensor'=4] {'seq','tensor'}, use_global_device_ids=true, to_apply=%region_37.38 | all-reduce | flops 1 | bytes 8 | tf_op jit(solution)/shard_map/psum | solution.py:926
  286.6 37.3 %all-reduce.1 = (f32[192]{0:T(256)}, f32[192]{0:T(256)}, f32[3,33]{1,0:T(4,128)}, f32[768]{0:T(1024)}, f32[768]{0:T(1024)}, /*index=5*/f32[768]{0:T(1024)}, f32[...) all-reduce(f32[192]{0:T(256)S(1)} %convert_reduce_fusion.5, ...), channel_id=1, replica_groups=mesh['seq'=8,'tensor'=4] {'seq'}, use_global_device_ids=true, to_apply=%region_14.15 | all-reduce | flops 5859 | bytes 46872 | tf_op jit(solution)/shard_map/psum | solution.py:935
  323.9 2.9 convert_add_fusion
  326.8 1.5 reduce-scatter.25.cloned.1.call-done
  328.3 1.6 copy.57
  330.0 64.0 %reduce-scatter.21.cloned.1.call-done = f32[96,192]{1,0:T(8,128)} async-done(((f32[768,192]{1,0:T(8,128)}), f32[96,192]{1,0:T(8,128)}) %reduce-scatter.21.cloned.1.call-update) | async-done | bytes 73744
  393.9 65.4 %reduce-scatter.23.cloned.1.call-done = f32[96,192]{1,0:T(8,128)} async-done(((f32[768,192]{1,0:T(8,128)}), f32[96,192]{1,0:T(8,128)}) %reduce-scatter.23.cloned.1.call-update) | async-done | bytes 73744
  459.4 65.8 %reduce-scatter.19.cloned.1.call-done = f32[96,192]{1,0:T(8,128)} async-done(((f32[768,192]{1,0:T(8,128)}), f32[96,192]{1,0:T(8,128)}) %reduce-scatter.19.cloned.1.call-update) | async-done | bytes 73744
  525.2 72.1 %reduce-scatter.15.cloned.1.call-done = f32[96,768]{1,0:T(8,128)} async-done(((f32[768,768]{1,0:T(8,128)}), f32[96,768]{1,0:T(8,128)}) %reduce-scatter.15.cloned.1.call-update) | async-done | bytes 294928 | tf_op jit(solution)/shard_map/reduce_scatter | solution.py:929
  597.3 72.0 %reduce-scatter.17.cloned.1.call-done = f32[768,96]{0,1:T(8,128)} async-done(((f32[768,768]{0,1:T(8,128)}), f32[768,96]{0,1:T(8,128)}) %reduce-scatter.17.cloned.1.call-update) | async-done | bytes 294928 | tf_op jit(solution)/shard_map/reduce_scatter | solution.py:929
  (161 shorter events, 23.8 us)
Async XLA Ops:
  7.2 85.7 %copy-start = (bf16[768,768]{1,0:T(8,128)(2,1)S(1)}, bf16[768,768]{1,0:T(8,128)(2,1)}, u32[]{:S(2)}) copy-start(bf16[768,768]{1,0:T(8,128)(2,1)} %param.31) | copy-start | bytes 3538948
  7.2 3.7 copy-start.1
  7.2 3.7 copy-start.17
  7.2 3.7 copy-start.18
  7.2 3.7 copy-start.20
  7.2 3.7 copy-start.19
  7.3 83.2 %all-reduce.7.cloned.1.call-start = ((), (), s32[]{:S(2)}) async-start(), calls=%async_computation.6 | async-start | bytes 1572864 | tf_op jit(solution)/shard_map/psum | solution.py:73
  9.7 44.0 %copy-start.4 = (bf16[192,768]{1,0:T(8,128)(2,1)S(1)}, bf16[192,768]{1,0:T(8,128)(2,1)}, u32[]{:S(2)}) copy-start(bf16[192,768]{1,0:T(8,128)(2,1)} %out_weight.1) | copy-start | bytes 884740
  52.3 38.1 %copy-start.42 = (f32[768]{0:T(1024)S(1)}, f32[768]{0:T(1024)}, u32[]{:S(2)}) copy-start(f32[768]{0:T(1024)} %param.28) | copy-start | bytes 9220
  54.9 80.8 %all-reduce.9.cloned.1.call-start = ((), (), s32[]{:S(2)}) async-start(), calls=%async_computation.7 | async-start | bytes 1572864 | tf_op jit(solution)/shard_map/psum | solution.py:73
  93.2 5.1 copy-start.21
  93.2 6.0 copy-start.50
  100.9 34.9 %copy-start.49 = (f32[768]{0:T(1024)S(1)}, f32[768]{0:T(1024)}, u32[]{:S(2)}) copy-start(f32[768]{0:T(1024)} %param.34) | copy-start | bytes 9220
  100.9 79.8 %all-reduce.11.cloned.1.call-start = ((), (), s32[]{:S(2)}) async-start(), calls=%async_computation.8 | async-start | bytes 1572864 | tf_op jit(solution)/shard_map/psum | solution.py:898
  138.9 2.6 copy-start.54
  140.4 2.9 copy-start.23
  145.9 178.0 %all-reduce.13.cloned.1.call-start = ((), (), s32[]{:S(2)}) async-start(), calls=%async_computation.9 | async-start | bytes 1572864 | tf_op jit(solution)/shard_map/psum | solution.py:925
  180.7 3.3 copy-start.22
  180.7 3.5 copy-start.24
  180.7 3.7 copy-start.27
  184.5 2.4 copy-start.12
  184.5 2.5 copy-start.14
  184.5 2.6 copy-start.16
  225.6 102.8 %reduce-scatter.25.cloned.1.call-start = ((), (), s32[]{:S(2)}) async-start(), calls=%async_computation.15 | async-start | bytes 884736
  228.0 2.6 copy-start.29
  228.0 165.9 %reduce-scatter.21.cloned.1.call-start = ((), (), s32[]{:S(2)}) async-start(), calls=%async_computation.13 | async-start | bytes 884736
  230.6 228.8 %reduce-scatter.23.cloned.1.call-start = ((), (), s32[]{:S(2)}) async-start(), calls=%async_computation.14 | async-start | bytes 884736
  232.2 293.0 %reduce-scatter.19.cloned.1.call-start = ((), (), s32[]{:S(2)}) async-start(), calls=%async_computation.12 | async-start | bytes 884736
  233.8 363.5 %reduce-scatter.15.cloned.1.call-start = ((), (), s32[]{:S(2)}) async-start(), calls=%async_computation.10 | async-start | bytes 2654208 | tf_op jit(solution)/shard_map/reduce_scatter | solution.py:929
  237.9 431.3 %reduce-scatter.17.cloned.1.call-start = ((), (), s32[]{:S(2)}) async-start(), calls=%async_computation.11 | async-start | bytes 2654208 | tf_op jit(solution)/shard_map/reduce_scatter | solution.py:929
  242.7 43.9 %copy-start.44 = (f32[768]{0:T(1024)S(1)}, f32[768]{0:T(1024)}, u32[]{:S(2)}) copy-start(f32[768]{0:T(1024)} %get-tuple-element.98) | copy-start | bytes 9220
  242.7 43.9 %copy-start.48 = (f32[768]{0:T(1024)S(1)}, f32[768]{0:T(1024)}, u32[]{:S(2)}) copy-start(f32[768]{0:T(1024)} %get-tuple-element.118) | copy-start | bytes 9220
  (33 other events, 42.7 us)
Sparse Core Ops, SparseCore 0:
  55.1 35.3 all-reduce.6
  101.0 34.6 all-reduce.8
  146.0 34.6 all-reduce.10
  225.7 36.9 all-reduce.12
  265.8 62.5 reduce-scatter.24
  332.4 61.4 reduce-scatter.20
  397.8 61.4 reduce-scatter.22
  463.6 61.5 reduce-scatter.18
  529.2 67.9 reduce-scatter.14
  601.2 68.0 reduce-scatter.16

commit v2 on v1

--- a/solution.py
+++ b/solution.py
@@ -450,13 +450,20 @@
     return jnp.where(iota(first.shape, 1) < HEAD_DIM, first, second)
 
 
-def greet(n, me, tensor):
+def greet(devices):
     barrier = pltpu.get_barrier_semaphore()
-    for d in range(1, n):
-        pl.semaphore_signal(
-            barrier, inc=1, device_id=(lax.rem(me + d, n), tensor), device_id_type=MESH
-        )
+    for device in devices:
+        pl.semaphore_signal(barrier, inc=1, device_id=device, device_id_type=MESH)
     return barrier
+
+
+def around(n, me, tensor):
+    return [(lax.rem(me + d, n), tensor) for d in range(1, n)]
+
+
+def others(me, tensor):
+    core = tensor + 1 - 2 * (tensor % 2)
+    return [(me, core), (me, lax.rem(tensor + 2, 4)), (me, lax.rem(core + 2, 4))]
 
 
 def paired(y):
@@ -494,9 +501,9 @@
 
 
 def forward_kernel(
-    n, lengths, x, wq, qb, wk, wv, vb, taps,
-    attn, qs, ks, vs, k1, p3, newton, mats, proxy,
-    stage, out_stage, send, recv, out_send, out_recv,
+    n, lengths, x, wq, qb, wk, wv, vb, taps, out_weight,
+    attn, qs, ks, vs, k1, p3, newton, mats, proxy, out_whole,
+    stage, out_stage, send, recv, out_send, out_recv, whole_send, whole_recv,
 ):
     me = lax.axis_index("seq")
     tensor = lax.axis_index("tensor")
@@ -507,15 +514,19 @@
     half = CONV // 2
     own, side = me // 2, me % 2
     scale = HEAD_DIM ** (-0.5)
-    barrier = greet(n, me, tensor)
+    barrier = greet(around(n, me, tensor) + others(me, tensor))
 
     copies = []
     owned = (ks, qs, vs)
+    width = out_weight.shape[0]
+    for t in range(4):
+        out_whole[t, width:] = jnp.zeros((2 * LANES - width, x.shape[1]), bf16)
+    out_whole[tensor, :width] = out_weight[...]
     offsets = (0, 0, half)
     vs[0:half] = jnp.zeros((half, LANES), bf16)
     vs[half + total : total + tok] = jnp.zeros((tok - half, LANES), bf16)
     for i in range(3):
-        y = dot(x[...], (wk, wq, wv)[i][...])
+        y = dot(x[...], (wk, wq, wv)[i][...], NT)
         if i == 1:
             y = y + qb[...]
         if i == 2:
@@ -529,7 +540,7 @@
         low = y.astype(bf16)
         stage[i, 0], stage[i, 1] = paired(low)
         if i == 0:
-            pl.semaphore_wait(barrier, n - 1)
+            pl.semaphore_wait(barrier, n + 2)
         here = pl.ds(pl.multiple_of(offsets[i] + me * tok, 16), tok)
         for d in range(1, n):
             peer = lax.rem(me + d, n)
@@ -543,6 +554,15 @@
             copy.start()
             copies.append(copy)
         owned[i][here] = stage[i, side, pl.ds(pl.multiple_of(own * tok, tok), tok)]
+
+    shares = []
+    for i, device in enumerate(others(me, tensor)):
+        copy = remote(
+            out_weight, out_whole.at[tensor, pl.ds(0, width)], whole_send.at[i], whole_recv.at[i],
+            device,
+        )
+        copy.start()
+        shares.append(copy)
 
     length = lengths[own]
     same_head = block_mask()
@@ -577,7 +597,9 @@
 
     deviation = identity - fine(kernel_two, inverse)
     norms = jnp.sqrt(block_sums(deviation * deviation, same_head))
-    proxy[...] = norms
+    first, second = norms[0:1, 0:1], norms[LANES - 1 :, LANES - 1 :]
+    norm_sum = jnp.where(side == 0, first + second, first) / (batch * HEADS)
+    proxy[...] = jnp.broadcast_to(norm_sum, proxy.shape)
 
     first_scores = fine(queries, key_marks, NT) * scale
     left = iota(first_scores.shape, 1) < HEAD_DIM
@@ -630,45 +652,315 @@
             copies.append(copy)
     for copy in copies[: 3 * (n - 1)]:
         copy.wait_send()
-    for copy in copies[3 * (n - 1) :]:
+    for copy in copies[3 * (n - 1) :] + shares:
         copy.wait()
 
 
-def backward_kernel(
-    n, lengths, out_in, out_weight, taps, qs, ks, vs, k1, p3, newton, mats,
-    rin, conv_grad,
-    stage, gs, out_stage, send, recv, out_send, out_recv,
+def normal_of(summed):
+    middle = jnp.mean(summed, axis=-1, keepdims=True)
+    centred = summed - middle
+    inverse_std = lax.rsqrt(jnp.mean(centred * centred, axis=-1, keepdims=True) + epsilon)
+    return centred * inverse_std, inverse_std
+
+
+def before_norm(grad, normal, inverse_std, gain):
+    grad_normal = grad * gain
+    return inverse_std * (
+        grad_normal
+        - jnp.mean(grad_normal, axis=-1, keepdims=True)
+        - normal * jnp.mean(grad_normal * normal, axis=-1, keepdims=True)
+    )
+
+
+def block_rows(t, tok):
+    return pl.ds(pl.multiple_of(t * tok, tok), tok)
+
+
+def gather_and_sum(phase, me, tensor, held, work, ring, filler):
+    tok = held.shape[0] // 4
+    ag_send, ag_recv, sum_send, sum_recv, core_out, core_in, y_out, y_in = ring
+    core, across, far = others(me, tensor)
+    mine = held.at[block_rows(tensor, tok)]
+    to_y = remote(mine, mine, ag_send.at[phase, 0], ag_recv.at[phase, 0], across)
+    to_y.start()
+    to_core = remote(mine, mine, ag_send.at[phase, 1], ag_recv.at[phase, 1], core)
+    to_core.start()
+    total = work(tensor)
+    to_core.wait_recv()
+    core_out[phase, 0] = work(core[1]).astype(bf16)
+    near = remote(
+        core_out.at[phase, 0], core_in.at[phase, 0], sum_send.at[phase, 0], sum_recv.at[phase, 0],
+        core,
+    )
+    near.start()
+    to_y.wait_recv()
+    other = held.at[block_rows(across[1], tok)]
+    pass_on = remote(other, other, ag_send.at[phase, 2], ag_recv.at[phase, 2], core)
+    pass_on.start()
+    part = work(across[1])
+    pass_on.wait_recv()
+    core_out[phase, 1] = work(far[1]).astype(bf16)
+    middle = remote(
+        core_out.at[phase, 1], core_in.at[phase, 1], sum_send.at[phase, 1], sum_recv.at[phase, 1],
+        core,
+    )
+    middle.start()
+    middle.wait_recv()
+    y_out[phase] = (part + core_in[phase, 1].astype(f32)).astype(bf16)
+    last = remote(
+        y_out.at[phase], y_in.at[phase], sum_send.at[phase, 2], sum_recv.at[phase, 2], across
+    )
+    last.start()
+    filler()
+    near.wait_recv()
+    last.wait_recv()
+    total = total + core_in[phase, 0].astype(f32) + y_in[phase].astype(f32)
+    return total, [to_y, to_core, pass_on, near, middle, last]
+
+
+def middle_kernel(
+    attn, x, out_whole, out_bias, gain_one, shift_one, up_weight, up_bias, down_weight, down_bias,
+    gain_two, shift_two, out_grad,
+    grad_attn, grad_first, out_in, out_rows, grad_up, grad_down, sums,
+    heads_in, heads_out, hidden, slope, active, down_in, up_in,
+    core_out, core_in, y_out, y_in,
+    a2a_send, a2a_recv, ag_send, ag_recv, sum_send, sum_recv,
 ):
     me = lax.axis_index("seq")
     tensor = lax.axis_index("tensor")
-    rows = out_in.shape[0]
+    rows = x.shape[0]
+    tok = rows // 4
+    peers = others(me, tensor)
+    ring = (ag_send, ag_recv, sum_send, sum_recv, core_out, core_in, y_out, y_in)
+    barrier = greet(peers)
+    pl.semaphore_wait(barrier, 3)
+    mine = block_rows(tensor, tok)
+    pending = []
+    for i in (2, 1, 0):
+        copy = remote(
+            attn.at[:, block_rows(peers[i][1], tok)], heads_in.at[tensor], a2a_send.at[0, i],
+            a2a_recv.at[0, i], peers[i],
+        )
+        copy.start()
+        pending.append(copy)
+    heads_in[tensor] = attn[:, mine]
+    for copy in pending:
+        copy.wait_recv()
+    branch = jnp.zeros((tok, x.shape[1]), f32)
+    for t in range(4):
+        branch = branch + dot(heads_in[t, 0], out_whole[t, :LANES])
+        branch = branch + dot(heads_in[t, 1], out_whole[t, LANES:])
+    first_total = x[mine].astype(f32) + (branch + out_bias[...])
+    normal_one, inverse_one = normal_of(first_total)
+    hidden_one = normal_one * gain_one[...] + shift_one[...]
+    hidden[mine] = hidden_one.astype(bf16)
+
+    def up(t):
+        at = block_rows(t, tok)
+        value = dot(hidden[at], up_weight[...]) + up_bias[...]
+        half = 0.5 * (1.0 + lax.erf(value * (0.5**0.5)))
+        density = jnp.exp(-0.5 * value * value) * (0.5 / jnp.pi) ** 0.5
+        slope[at] = half + value * density
+        low = (value * half).astype(bf16)
+        active[at] = low
+        return dot(low, down_weight[...])
+
+    down_sum, copies = gather_and_sum(0, me, tensor, hidden, up, ring, lambda: None)
+    pending += copies
+    second_total = hidden_one + (down_sum + down_bias[...])
+    normal_two, inverse_two = normal_of(second_total)
+    out_rows[...] = (normal_two * gain_two[...] + shift_two[...]).astype(bf16)
+    grad_out = out_grad[mine].astype(f32)
+    grad_second = before_norm(grad_out, normal_two, inverse_two, gain_two[...])
+    low = grad_second.astype(bf16)
+    down_in[mine] = low
+
+    def total_of(v):
+        return jnp.sum(v, axis=0, keepdims=True)
+
+    def down(t):
+        at = block_rows(t, tok)
+        low = (dot(down_in[at], down_weight[...], NT) * slope[at]).astype(bf16)
+        up_in[at] = low
+        return dot(low, up_weight[...], NT)
+
+    def fill():
+        sums[0:1] = total_of(grad_out * normal_two)
+        sums[1:2] = total_of(grad_out)
+        sums[2:3] = total_of(low.astype(f32))
+        grad_down[...] = dot(down_in[...], active[...], TN).astype(bf16)
+
+    up_sum, copies = gather_and_sum(1, me, tensor, down_in, down, ring, fill)
+    pending += copies
+    grad_hidden = grad_second + up_sum
+    grad_total = before_norm(grad_hidden, normal_one, inverse_one, gain_one[...])
+    grad_first[...] = grad_total
+    low_out = grad_total.astype(bf16)
+    out_in[...] = low_out
+    sent = []
+    for i in (2, 1, 0):
+        t = peers[i][1]
+        heads_out[i, 0] = dot(low_out, out_whole[t, :LANES], NT).astype(bf16)
+        heads_out[i, 1] = turn(dot(low_out, out_whole[t, LANES:], NT), heads_out[i, 0])
+        copy = remote(
+            heads_out.at[i], grad_attn.at[:, mine], a2a_send.at[1, i], a2a_recv.at[1, i], peers[i]
+        )
+        copy.start()
+        sent.append(copy)
+    own_first = dot(low_out, out_whole[tensor, :LANES], NT).astype(bf16)
+    grad_attn[0, mine] = own_first
+    grad_attn[1, mine] = turn(dot(low_out, out_whole[tensor, LANES:], NT), own_first)
+    sums[3:4] = total_of(grad_hidden * normal_one)
+    sums[4:5] = total_of(grad_hidden)
+    sums[5:6] = total_of(low_out.astype(f32))
+    sums[6:7] = dot(jnp.ones((8, rows), bf16), up_in[...])[0:1]
+    sums[7:8] = jnp.zeros_like(sums[7:8])
+    grad_up[...] = dot(hidden[...], up_in[...], TN).astype(bf16)
+    for copy in pending:
+        copy.wait_send()
+    for copy in sent:
+        copy.wait()
+
+
+def turn(second, first):
+    low = second.astype(bf16)
+    return jnp.where(iota(low.shape, 1) < HEAD_DIM, low, first)
+
+
+class Scatter:
+    def __init__(self, index, me, tensor, source, buffers, send, recv):
+        self.index, self.source = index, source
+        self.x_in, self.held, self.z_in, self.pair, self.last_in = buffers
+        self.block = source.shape[0] // 8
+        self.x, self.z = me % 2, me // 2
+        z = self.z
+        self.partners = (
+            (me + 1 - 2 * self.x, tensor),
+            (2 * (z + 1 - 2 * (z % 2)) + self.x, tensor),
+            (2 * lax.rem(z + 2, 4) + self.x, tensor),
+        )
+        self.send, self.recv = send, recv
+        self.copies = []
+
+    def rows(self, z, x):
+        return pl.ds(pl.multiple_of((2 * z + x) * self.block, 16), self.block)
+
+    def copy(self, src, dst, k, partner):
+        copy = remote(
+            src, dst, self.send.at[self.index, k], self.recv.at[self.index, k],
+            self.partners[partner],
+        )
+        copy.start()
+        self.copies.append(copy)
+
+    def first(self):
+        for z in range(4):
+            self.copy(self.source.at[self.rows(z, 1 - self.x)], self.x_in.at[z], z, 0)
+
+    def second(self):
+        odd = self.z % 2
+        for z in range(4):
+            self.copies[z].wait_recv()
+        for z in range(4):
+            both = self.source[self.rows(z, self.x)].astype(f32) + self.x_in[z].astype(f32)
+            self.held[z] = both.astype(bf16)
+        for k in range(2):
+            self.copy(self.held.at[2 * k + 1 - odd], self.z_in.at[k], 4 + k, 1)
+
+    def third(self):
+        odd = self.z % 2
+        for k in range(2):
+            self.copies[4 + k].wait_recv()
+        for k in range(2):
+            both = self.held[2 * k + odd].astype(f32) + self.z_in[k].astype(f32)
+            self.pair[k] = both.astype(bf16)
+        self.copy(self.pair.at[1 - self.z // 2], self.last_in, 6, 2)
+
+    def last(self):
+        self.copies[6].wait_recv()
+        return self.pair[self.z // 2].astype(f32) + self.last_in[...].astype(f32)
+
+    def finish(self):
+        for copy in self.copies:
+            copy.wait_send()
+
+
+def scatter_buffers(width, block):
+    return [
+        pltpu.VMEM((4, block, width), bf16),
+        pltpu.VMEM((4, block, width), bf16),
+        pltpu.VMEM((2, block, width), bf16),
+        pltpu.VMEM((2, block, width), bf16),
+        pltpu.VMEM((block, width), bf16),
+    ]
+
+
+def backward_kernel(
+    n, lengths, grad_attn, taps, qs, ks, vs, k1, p3, newton, mats, proxy, attn, x, wq, wk, wv,
+    grad_first, out_in, out_rows, grad_up, grad_down, sums,
+    grad_tokens, output, grad_query, grad_key, grad_value, grad_out, up_result, down_result,
+    early_result, late_result,
+    gs, out_stage, rin, out_whole, early, early_tensor, early_seq, late_seq, source_out,
+    source_heads, tokens_low, tokens_whole, core_out, core_in, y_out, y_in, *rest,
+):
+    buffers, sems = rest[:20], rest[20:]
+    (send, recv, out_send, out_recv, share_send, share_recv, sum_send, sum_recv, small_send,
+     small_recv, job_send, job_recv) = sems
+    me = lax.axis_index("seq")
+    tensor = lax.axis_index("tensor")
+    rows, width = x.shape
     batch = n // 2
     tok = rows // batch
     total = n * tok
     half = CONV // 2
     own, side = me // 2, me % 2
     scale = HEAD_DIM ** (-0.5)
-    barrier = greet(n, me, tensor)
+    ring_peers = around(n, me, tensor)
+    peers = others(me, tensor)
+    core, across, far = peers
+    mine = block_rows(tensor, tok)
+    barrier = greet(ring_peers + peers)
+    jobs = [
+        Scatter(i, me, tensor, source, buffers[5 * i : 5 * i + 5], job_send, job_recv)
+        for i, source in enumerate((grad_down, grad_up, source_out, source_heads))
+    ]
 
     gs[0:half] = jnp.zeros((half, LANES), bf16)
     gs[half + total : total + tok] = jnp.zeros((tok - half, LANES), bf16)
-    grad = dot(out_in[...], out_weight[...], NT).astype(bf16)
-    stage[0], stage[1] = paired(grad)
-    pl.semaphore_wait(barrier, n - 1)
+    output[mine] = out_rows[...]
+    out_whole[mine] = out_in[...]
+    early[0:7] = sums[0:7]
+    early[7:8] = jnp.broadcast_to(proxy[0:1, 0:1], (1, width))
+    early_tensor[tensor] = early[...]
+    pl.semaphore_wait(barrier, n + 2)
+
     here = pl.ds(pl.multiple_of(half + me * tok, 16), tok)
     copies = []
     for d in range(1, n):
         peer = lax.rem(me + d, n)
         copy = remote(
-            stage.at[peer % 2, pl.ds(pl.multiple_of((peer // 2) * tok, tok), tok)],
-            gs.at[here],
-            send.at[d - 1],
-            recv.at[d - 1],
-            (peer, tensor),
+            grad_attn.at[peer % 2, block_rows(peer // 2, tok)], gs.at[here], send.at[d - 1],
+            recv.at[d - 1], (peer, tensor),
         )
         copy.start()
         copies.append(copy)
-    gs[here] = stage[side, pl.ds(pl.multiple_of(own * tok, tok), tok)]
+    gs[here] = grad_attn[side, block_rows(own, tok)]
+    shares = []
+    for i, held in enumerate((out_whole, output)):
+        for j, device in enumerate((across, core)):
+            copy = remote(
+                held.at[mine], held.at[mine], share_send.at[i, j], share_recv.at[i, j], device
+            )
+            copy.start()
+            shares.append(copy)
+    for i, device in enumerate(peers):
+        copy = remote(
+            early, early_tensor.at[tensor], small_send.at[0, i], small_recv.at[0, i], device
+        )
+        copy.start()
+        shares.append(copy)
+    jobs[0].first()
+    jobs[1].first()
 
     length = lengths[own]
     same_head = block_mask()
@@ -677,7 +969,6 @@
     members = member_columns(length, total)
     counts = segment_counts(length)
     query_marks, key_marks, kernel_two, inverse, third_out, carried = [mats[i] for i in range(6)]
-    matrices = [taps_matrix(taps_row(taps, h, tok), tok) for h in (2 * side, 1)]
     flip = jnp.where(
         iota((2 * tok, 2 * tok), 0) + iota((2 * tok, 2 * tok), 1) == CONV - 1, 1.0, 0.0
     ).astype(bf16)
@@ -688,28 +979,43 @@
         for h in (2 * side, 1)
     ]
     queries, keys, values = qs[...], ks[...], vs[half : half + total]
+    there = block_rows(own, tok)
+    outs = []
+
+    def give(i, block):
+        low = block.astype(bf16)
+        for m in range(n):
+            out_stage[i, m] = low[m * tok : (m + 1) * tok]
+        for d in range(1, n):
+            peer = lax.rem(me + d, n)
+            copy = remote(
+                out_stage.at[i, peer], rin.at[i, side, there], out_send.at[i, d - 1],
+                out_recv.at[i, d - 1], (peer, tensor),
+            )
+            copy.start()
+            outs.append(copy)
+        rin[i, side, there] = out_stage[i, me]
+
     for copy in copies:
         copy.wait_recv()
-
     grad = gs[half : half + total]
     kernel_one = k1[...]
     grad_carried = jnp.where(same_head, fine(kernel_one, grad, TN), 0.0)
     grad_third = fine(inverse, grad_carried, TN)
     grad_inverse = fine(grad_carried, third_out, NT)
-
     third_prob = p3[...]
-    grad_values = fine(third_prob, grad_third)
-    alive = iota((tok, LANES), 0)
-    outs = []
-
-    return_blocks = {}
-    full = []
-    for m in range(n):
-        block = grad_values[m * tok : (m + 1) * tok] + conv_block(
-            reverse, gs[m * tok : (m + 2) * tok]
-        )
-        full.append(jnp.where(alive + m * tok < length, block, 0.0))
-    return_blocks[2] = jnp.concatenate(full, axis=0)
+    convolved = jnp.concatenate(
+        [conv_block(reverse, gs[m * tok : (m + 2) * tok]) for m in range(n)], axis=0
+    )
+    grad_values = fine(third_prob, grad_third) + convolved
+    give(2, jnp.where(iota(grad_values.shape, 0) < length, grad_values, 0.0))
+
+    for i, held in enumerate((out_whole, output)):
+        shares[2 * i].wait_recv()
+        block = held.at[block_rows(across[1], tok)]
+        copy = remote(block, block, share_send.at[i, 2], share_recv.at[i, 2], core)
+        copy.start()
+        shares.append(copy)
 
     kernel_back = jnp.zeros((LANES, LANES), f32)
     grad_state = grad_inverse
@@ -742,48 +1048,143 @@
     delta = fine(jnp.ones((8, LANES), bf16), grad_third * third_out, NT)[0:1]
     third_scores = scale * third_prob * (fine(values, grad_third, NT) - delta)
     query_three = jnp.where(same_head, fine(third_scores, keys, TN), 0.0)
-    return_blocks[0] = fine(third_scores, query_marks) + fine(
-        members, (key_one + key_two) / counts
-    )
-    return_blocks[1] = fine(first_scores, key_marks) + fine(
-        members, (query_two + query_three) / counts
-    )
-    for i in (2, 0, 1):
-        low = return_blocks[i].astype(bf16)
-        for m in range(n):
-            out_stage[i, m] = low[m * tok : (m + 1) * tok]
-        there = pl.ds(pl.multiple_of(own * tok, tok), tok)
-        for d in range(1, n):
-            peer = lax.rem(me + d, n)
-            copy = remote(
-                out_stage.at[i, peer],
-                rin.at[i, side, there],
-                out_send.at[i, d - 1],
-                out_recv.at[i, d - 1],
-                (peer, tensor),
-            )
-            copy.start()
-            outs.append(copy)
-        rin[i, side, there] = out_stage[i, me]
+    give(
+        0, fine(third_scores, query_marks) + fine(members, (key_one + key_two) / counts)
+    )
+    give(
+        1, fine(first_scores, key_marks) + fine(members, (query_two + query_three) / counts)
+    )
+
+    jobs[0].second()
+    jobs[1].second()
+    for copy in shares[4:7]:
+        copy.wait_recv()
+    by_tensor = early_tensor[0] + early_tensor[1] + early_tensor[2] + early_tensor[3]
+    early_seq[me] = jnp.where(iota(by_tensor.shape, 0) == 6, early[...], by_tensor)
+    for d, device in enumerate(ring_peers):
+        copy = remote(
+            early_seq.at[me], early_seq.at[me], small_send.at[1, d], small_recv.at[1, d], device
+        )
+        copy.start()
+        shares.append(copy)
+
+    shares[1].wait_recv()
+    shares[7].wait_recv()
+    attention = jnp.concatenate([attn[0], attn[1, :, :HEAD_DIM]], axis=1)
+    source_out[...] = dot(out_whole[...], attention, TN).astype(bf16)
+    jobs[2].first()
 
     position = iota((tok, tok), 0) + iota((tok, tok), 1)
     upside = jnp.where(position == tok - 1, 1.0, 0.0).astype(bf16)
     lane = iota((tok, LANES), 1)
+    conv_rows = []
     for h in range(2):
-        mine = (lane < HEAD_DIM) if h == 0 else (lane >= HEAD_DIM)
+        inner = (lane < HEAD_DIM) if h == 0 else (lane >= HEAD_DIM)
         table = jnp.zeros((tok, 2 * tok), f32)
         for m in range(n):
             block = gs[half + m * tok : half + (m + 1) * tok]
-            block = jnp.where(mine, block, jnp.zeros_like(block))
+            block = jnp.where(inner, block, jnp.zeros_like(block))
             table = table + dot(block, vs[m * tok : (m + 2) * tok], NT)
         table = pltpu.roll(fine(upside, table), 0, 1, stride=1, stride_axis=0)
         row = jnp.sum(table, axis=0, keepdims=True)
         row = pltpu.roll(jnp.broadcast_to(row, (8, 2 * tok)), tok + 1, 1)
-        conv_grad[h] = row
-    for copy in copies:
+        conv_rows.append(row[0:1, :LANES])
+    whole_weight = jnp.concatenate(
+        [w[:LANES] for w in (wk, wq, wv)] + [w[LANES:] for w in (wk, wq, wv)], axis=0
+    )
+    jobs[0].third()
+    jobs[1].third()
+
+    for copy in outs:
+        copy.wait_recv()
+    low = jnp.concatenate(
+        [rin[i, 0] for i in range(3)] + [rin[i, 1, :, :HEAD_DIM] for i in range(3)], axis=1
+    )
+    source_heads[...] = dot(x[...], low, TN).astype(bf16)
+    jobs[3].first()
+
+    tokens_low[...] = low
+
+    def input_part(t):
+        return dot(tokens_low[block_rows(t, tok)], whole_weight)
+
+    def pass_sum(k, value, device):
+        core_out[k] = value.astype(bf16)
+        copy = remote(core_out.at[k], core_in.at[k], sum_send.at[k], sum_recv.at[k], device)
+        copy.start()
+        shares.append(copy)
+        return copy
+
+    middle = pass_sum(1, input_part(far[1]), core)
+    near = pass_sum(0, input_part(core[1]), core)
+    part = input_part(across[1])
+    middle.wait_recv()
+    y_out[...] = (part + core_in[1].astype(f32)).astype(bf16)
+    final = remote(y_out, y_in, sum_send.at[2], sum_recv.at[2], across)
+    final.start()
+    shares.append(final)
+    result = input_part(tensor) + grad_first[...]
+
+    head_sums = dot(jnp.ones((8, rows), bf16), low)[0:1]
+    late = late_seq.at[me]
+    late[...] = jnp.zeros(late.shape, f32)
+    inner = HEAD_DIM
+    late[0:1, 0:LANES] = head_sums[:, LANES : 2 * LANES]
+    late[0:1, LANES : LANES + inner] = head_sums[:, 3 * LANES + inner : 4 * LANES]
+    late[1:2, 0:LANES] = head_sums[:, 2 * LANES : 3 * LANES]
+    late[1:2, LANES : LANES + inner] = head_sums[:, 4 * LANES : 4 * LANES + inner]
+    even = side == 0
+    late[2:3, 0:LANES] = jnp.where(even, conv_rows[0], 0.0)
+    late[3:4, 0:LANES] = jnp.where(even, conv_rows[1], 0.0)
+    late[4:5, 0:LANES] = jnp.where(even, 0.0, conv_rows[0])
+    for d, device in enumerate(ring_peers):
+        copy = remote(late, late, small_send.at[2, d], small_recv.at[2, d], device)
+        copy.start()
+        shares.append(copy)
+
+    jobs[2].second()
+    down_result[...] = jobs[0].last().T
+    up_result[...] = jobs[1].last()
+
+    near.wait_recv()
+    final.wait_recv()
+    result = result + core_in[0].astype(f32) + y_in[...].astype(f32)
+    tokens_whole[mine] = result.astype(bf16)
+    ends = []
+    for j, device in enumerate((across, core)):
+        copy = remote(
+            tokens_whole.at[mine], tokens_whole.at[mine], share_send.at[2, j], share_recv.at[2, j],
+            device,
+        )
+        copy.start()
+        ends.append(copy)
+    jobs[3].second()
+    jobs[2].third()
+    ends[0].wait_recv()
+    block = tokens_whole.at[block_rows(across[1], tok)]
+    copy = remote(block, block, share_send.at[2, 2], share_recv.at[2, 2], core)
+    copy.start()
+    jobs[3].third()
+    grad_out[...] = jobs[2].last().T
+    for k, device in enumerate(ring_peers):
+        shares[9 + k].wait_recv()
+    early_result[...] = functools.reduce(lambda a, b: a + b, [early_seq[i] for i in range(n)])
+    for k, device in enumerate(ring_peers):
+        shares[9 + n - 1 + 3 + k].wait_recv()
+    late_result[...] = functools.reduce(lambda a, b: a + b, [late_seq[i] for i in range(n)])
+    ends[1].wait_recv()
+    copy.wait_recv()
+    grad_tokens[...] = tokens_whole[...].astype(f32)
+    heads = jobs[3].last()
+    for i, ref in enumerate((grad_key, grad_query, grad_value)):
+        ref[:, :LANES] = heads[:, i * LANES : (i + 1) * LANES]
+        ref[:, LANES:] = heads[:, 3 * LANES + i * inner : 3 * LANES + (i + 1) * inner]
+    shares[3].wait_recv()
+    shares[8].wait_recv()
+    for copy in copies + outs + shares + ends + [copy]:
         copy.wait_send()
-    for copy in outs:
-        copy.wait()
+    for job in jobs:
+        job.finish()
 
 
 def whole(shape, dtype):
@@ -794,8 +1195,18 @@
 SMEM = pl.BlockSpec(memory_space=pltpu.SMEM)
 
 
-def attention_forward(n, lengths, flat, wq, qb, wk, wv, vb, taps):
-    rows = flat.shape[0]
+def limits(collective):
+    return pltpu.CompilerParams(
+        collective_id=collective, has_side_effects=True, vmem_limit_bytes=56 * 2**20
+    )
+
+
+def dma(*shape):
+    return pltpu.SemaphoreType.DMA(shape)
+
+
+def attention_forward(n, lengths, flat, wq, qb, wk, wv, vb, taps, out_weight):
+    rows, width = flat.shape
     tok = rows // (n // 2)
     total = n * tok
     return pl.pallas_call(
@@ -809,48 +1220,106 @@
             whole((total, LANES), f32),
             whole((4 * NS_ITERS, LANES, LANES), f32),
             whole((6, LANES, LANES), f32),
-            whole((LANES, LANES), f32),
+            whole((1, LANES), f32),
+            whole((4, 2 * LANES, width), bf16),
         ),
-        in_specs=[SMEM] + [VMEM] * 7,
-        out_specs=(VMEM,) * 9,
+        in_specs=[SMEM] + [VMEM] * 8,
+        out_specs=(VMEM,) * 10,
         scratch_shapes=[
             pltpu.VMEM((3, 2, rows, LANES), bf16),
             pltpu.VMEM((n - 1, tok, LANES), bf16),
-            pltpu.SemaphoreType.DMA((3, n - 1)),
-            pltpu.SemaphoreType.DMA((3, n - 1)),
-            pltpu.SemaphoreType.DMA((n - 1,)),
-            pltpu.SemaphoreType.DMA((n - 1,)),
+            dma(3, n - 1), dma(3, n - 1), dma(n - 1), dma(n - 1), dma(3), dma(3),
         ],
-        compiler_params=pltpu.CompilerParams(
-            collective_id=0, has_side_effects=True, vmem_limit_bytes=48 * 2**20
+        compiler_params=limits(0),
+        name="attention_forward",
+    )(lengths, flat, wq, qb, wk, wv, vb, taps, out_weight)
+
+
+def middle(attn, flat, out_whole, *params):
+    rows, width = flat.shape
+    hidden = params[3].shape[1]
+    tok = rows // 4
+    return pl.pallas_call(
+        middle_kernel,
+        out_shape=(
+            whole((2, rows, LANES), bf16),
+            whole((tok, width), f32),
+            whole((tok, width), bf16),
+            whole((tok, width), bf16),
+            whole((width, hidden), bf16),
+            whole((width, hidden), bf16),
+            whole((8, width), f32),
         ),
-        name="attention_forward",
-    )(lengths, flat, wq, qb, wk, wv, vb, taps)
-
-
-def attention_backward(n, lengths, out_in, out_weight, taps, saved):
-    rows = out_in.shape[0]
-    tok = rows // (n // 2)
+        in_specs=[VMEM] * 13,
+        out_specs=(VMEM,) * 7,
+        scratch_shapes=[
+            pltpu.VMEM((4, 2, tok, LANES), bf16),
+            pltpu.VMEM((3, 2, tok, LANES), bf16),
+            pltpu.VMEM((rows, width), bf16),
+            pltpu.VMEM((rows, hidden), f32),
+            pltpu.VMEM((rows, hidden), bf16),
+            pltpu.VMEM((rows, width), bf16),
+            pltpu.VMEM((rows, hidden), bf16),
+            pltpu.VMEM((2, 2, tok, width), bf16),
+            pltpu.VMEM((2, 2, tok, width), bf16),
+            pltpu.VMEM((2, tok, width), bf16),
+            pltpu.VMEM((2, tok, width), bf16),
+            dma(2, 3), dma(2, 3), dma(2, 3), dma(2, 3), dma(2, 3), dma(2, 3),
+        ],
+        compiler_params=limits(1),
+        name="middle",
+    )(attn, flat, out_whole, *params)
+
+
+def attention_backward(n, *args):
+    rows, width = args[12].shape
+    tok = rows // 4
     total = n * tok
+    block = width // n
+    local = 3 * HEAD_DIM
+    hidden = args[20].shape[1]
     return pl.pallas_call(
         functools.partial(backward_kernel, n),
-        out_shape=(whole((3, 2, rows, LANES), bf16), whole((2, 8, 2 * tok), f32)),
-        in_specs=[SMEM] + [VMEM] * 10,
-        out_specs=(VMEM,) * 2,
+        out_shape=(
+            whole((rows, width), f32),
+            whole((rows, width), bf16),
+            whole((block, local), f32),
+            whole((block, local), f32),
+            whole((block, local), f32),
+            whole((local, block), f32),
+            whole((block, hidden), f32),
+            whole((hidden, block), f32),
+            whole((8, width), f32),
+            whole((8, width), f32),
+        ),
+        in_specs=[SMEM] + [VMEM] * (len(args) - 1),
+        out_specs=(VMEM,) * 10,
         scratch_shapes=[
-            pltpu.VMEM((2, rows, LANES), bf16),
             pltpu.VMEM((total + tok, LANES), bf16),
             pltpu.VMEM((3, n, tok, LANES), bf16),
-            pltpu.SemaphoreType.DMA((n - 1,)),
-            pltpu.SemaphoreType.DMA((n - 1,)),
-            pltpu.SemaphoreType.DMA((3, n - 1)),
-            pltpu.SemaphoreType.DMA((3, n - 1)),
+            pltpu.VMEM((3, 2, rows, LANES), bf16),
+            pltpu.VMEM((rows, width), bf16),
+            pltpu.VMEM((8, width), f32),
+            pltpu.VMEM((4, 8, width), f32),
+            pltpu.VMEM((n, 8, width), f32),
+            pltpu.VMEM((n, 8, width), f32),
+            pltpu.VMEM((width, local), bf16),
+            pltpu.VMEM((width, 3 * local), bf16),
+            pltpu.VMEM((rows, 3 * local), bf16),
+            pltpu.VMEM((rows, width), bf16),
+            pltpu.VMEM((2, tok, width), bf16),
+            pltpu.VMEM((2, tok, width), bf16),
+            pltpu.VMEM((tok, width), bf16),
+            pltpu.VMEM((tok, width), bf16),
+        ]
+        + [b for w in (hidden, hidden, local, 3 * local) for b in scatter_buffers(w, block)]
+        + [
+            dma(n - 1), dma(n - 1), dma(3, n - 1), dma(3, n - 1), dma(3, 3), dma(3, 3), dma(3),
+            dma(3), dma(3, n - 1), dma(3, n - 1), dma(4, 7), dma(4, 7),
         ],
-        compiler_params=pltpu.CompilerParams(
-            collective_id=1, has_side_effects=True, vmem_limit_bytes=48 * 2**20
-        ),
+        compiler_params=limits(2),
         name="attention_backward",
-    )(lengths, out_in, out_weight, taps, *saved)
+    )(*args)
 
 
 def gathered_plan(
@@ -861,95 +1330,47 @@
     batch, tok, width = tokens.shape
     rows = batch * tok
     flat = tokens.reshape(rows, width)
-    flat_wide = flat.astype(f32)
-    attn, *saved, proxy = attention_forward(
-        n, lengths, flat, query_weight, query_bias[None], key_weight, value_weight,
-        value_bias[None], conv_kernel,
-    )
-    side = lax.axis_index("seq") % 2
-    proxy_part = jnp.where(side == 0, proxy[0, 0] + proxy[-1, -1], proxy[0, 0]) / (batch * HEADS)
-    attention = jnp.concatenate([attn[0], attn[1, :, :HEAD_DIM]], axis=1)
-    out_part = jnp.dot(attention, out_weight, preferred_element_type=f32)
-    hidden_one, normal_one, inverse_one = add_norm(
-        out_part, flat_wide, out_bias, first_gain, first_shift
-    )
-    hidden_low = hidden_one.astype(bf16)
-    up_value = jnp.dot(hidden_low, up_weight, preferred_element_type=f32) + up_bias
-    activated, gelu_back = jax.vjp(lambda z: jax.nn.gelu(z, approximate=False), up_value)
-    activated = activated.astype(bf16)
-    down_part = jnp.dot(activated, down_weight, preferred_element_type=f32)
-    hidden_two, normal_two, inverse_two = add_norm(
-        down_part, hidden_one, down_bias, second_gain, second_shift
-    )
-    output = hidden_two.astype(bf16).reshape(batch, tok, width)
-    grad_output = out_grad.reshape(rows, width).astype(f32)
-    grad_second_total, grad_second_gain, grad_second_shift = norm_back(
-        grad_output, normal_two, inverse_two, second_gain
-    )
-    down_in = grad_second_total.astype(bf16)
-    grad_down_bias = jnp.sum(down_in.astype(f32), axis=0)
-    grad_down_weight = jnp.einsum("rf,rd->fd", activated, down_in, preferred_element_type=f32)
-    grad_activated = jnp.einsum("rd,fd->rf", down_in, down_weight, preferred_element_type=f32)
-    up_in = gelu_back(grad_activated)[0].astype(bf16)
-    grad_up_bias = jnp.sum(up_in.astype(f32), axis=0)
-    grad_up_weight = jnp.einsum("rd,rf->df", hidden_low, up_in, preferred_element_type=f32)
-    hidden_part = jnp.einsum("rf,df->rd", up_in, up_weight, preferred_element_type=f32)
-    grad_hidden_one = (
-        lax.psum(hidden_part.astype(bf16), "tensor").astype(f32) + grad_second_total
-    )
-    grad_first_total, grad_first_gain, grad_first_shift = norm_back(
-        grad_hidden_one, normal_one, inverse_one, first_gain
-    )
-    out_in = grad_first_total.astype(bf16)
-    grad_out_bias = jnp.sum(out_in.astype(f32), axis=0)
-    grad_out_weight = jnp.einsum("rf,rd->fd", attention, out_in, preferred_element_type=f32)
-    rin, conv_grad = attention_backward(n, lengths, out_in, out_weight, conv_kernel, saved)
-    first, second = conv_grad[0, 0, :CONV], conv_grad[1, 0, :CONV]
-    nothing = jnp.zeros_like(first)
-    grad_conv_kernel = jnp.where(
-        side == 0, jnp.stack([first, second, nothing]), jnp.stack([nothing, nothing, first])
-    )
-    key_in, query_in, value_in = [
-        jnp.concatenate([rin[i, 0], rin[i, 1, :, :HEAD_DIM]], axis=1) for i in range(3)
-    ]
-    grad_query_bias = jnp.sum(query_in.astype(f32), axis=0)
-    grad_value_bias = jnp.sum(value_in.astype(f32), axis=0)
-    grad_query_weight = jnp.einsum("rd,rf->df", flat, query_in, preferred_element_type=f32)
-    grad_key_weight = jnp.einsum("rd,rf->df", flat, key_in, preferred_element_type=f32)
-    grad_value_weight = jnp.einsum("rd,rf->df", flat, value_in, preferred_element_type=f32)
-    input_part = (
-        jnp.einsum("rf,df->rd", query_in, query_weight, preferred_element_type=f32)
-        + jnp.einsum("rf,df->rd", key_in, key_weight, preferred_element_type=f32)
-        + jnp.einsum("rf,df->rd", value_in, value_weight, preferred_element_type=f32)
-    )
-    input_sum = lax.psum(input_part.astype(bf16), "tensor").astype(f32)
-    proxy_norm = lax.psum(proxy_part, ("seq", "tensor"))
-    grad_tokens = (grad_first_total + input_sum).reshape(batch, tok, width)
-    scattered = [
-        lax.psum_scatter(g, "seq", scatter_dimension=dim, tiled=True)
-        for g, dim in (
-            (grad_query_weight, 0), (grad_key_weight, 0), (grad_value_weight, 0),
-            (grad_out_weight, 1), (grad_up_weight, 0), (grad_down_weight, 1),
-        )
-    ]
-    summed = lax.psum(
-        (
-            grad_query_bias, grad_value_bias, grad_conv_kernel, grad_out_bias, grad_first_gain,
-            grad_first_shift, grad_up_bias, grad_down_bias, grad_second_gain, grad_second_shift,
-        ),
-        "seq",
-    )
+    wq, wk, wv = query_weight.T, key_weight.T, value_weight.T
+    attn, *saved, out_whole = attention_forward(
+        n, lengths, flat, wq, query_bias[None], wk, wv, value_bias[None], conv_kernel, out_weight
+    )
+    grad_attn, *results = middle(
+        attn, flat, out_whole, out_bias[None], first_gain[None], first_shift[None], up_weight,
+        up_bias[None], down_weight, down_bias[None], second_gain[None], second_shift[None],
+        out_grad.reshape(rows, width),
+    )
+    (grad_tokens, output, grad_query, grad_key, grad_value, grad_out, grad_up, grad_down, early,
+     late) = attention_backward(
+        n, lengths, grad_attn, conv_kernel, *saved, attn, flat, wq, wk, wv, *results
+    )
+    local = wq.shape[0]
     return (
-        output, grad_tokens, scattered[0], summed[0], scattered[1], scattered[2], summed[1],
-        summed[2], scattered[3], summed[3], summed[4], summed[5], scattered[4], summed[6],
-        scattered[5], summed[7], summed[8], summed[9], proxy_norm,
+        output.reshape(tokens.shape),
+        grad_tokens.reshape(tokens.shape),
+        grad_query,
+        late[0, :local],
+        grad_key,
+        grad_value,
+        late[1, :local],
+        late[2:5, :CONV],
+        grad_out,
+        early[5],
+        early[3],
+        early[4],
+        grad_up,
+        early[6],
+        grad_down,
+        early[2],
+        early[0],
+        early[1],
+        early[7, 0],
     )
 
 
 def per_device(seq, tensor, *args):
-    batch, tok, _ = args[0].shape
-    local_heads = args[7].shape[0]
-    if seq == 2 * batch and local_heads == 3 and tok % 128 == 0:
+    batch, tok, width = args[0].shape
+    heads = args[7].shape[0]
+    if seq == 8 and tensor == 4 and batch == 4 and heads == 3 and tok == 128:
         return gathered_plan(seq, *args)
     return general_plan(*args)
 

time: 677 us -> 193 us (0.29)
  waiting for transfers between devices: 445 us -> 0 us
  Pallas kernels: 70.5 us -> 169 us
  blocking collectives: 78.2 us -> 0 us
  matrix products: 25.5 us -> 0 us
  other arithmetic: 16 us -> 0 us
  between operations: 16.7 us -> 0.72 us
    unnamed x14 -> x0, waiting for transfers between devices: 197 us -> none
    reduce_scatter x2 -> x0, waiting for transfers between devices: 144 us -> none  [gathered_plan(): lax.psum_scatter(g, 'seq', scatter_dimension=dim, tiled=True)]
    psum x4 -> x0, waiting for transfers between devices: 104 us -> none  [the longest x2 69.7 us: add_norm(): lax.psum(partial_sum.astype(jnp.bfloat16), 'tensor').astype(jnp.float32)]
    pallas_call x1 -> x2, Pallas kernels: 34.8 us -> 130 us  [the longest x1 82.6 us: attention_backward(): pl.pallas_call(functools.partial(backward_kernel, n), out_shape=(whole((r...]
    psum x2 -> x0, blocking collectives: 78.2 us -> none  [the longest x1 41 us: gathered_plan(): proxy_norm = lax.psum(proxy_part, ('seq', 'tensor'))]
    dot_general x13 -> x0, matrix products: 23.1 us -> none  [the longest x1 5.13 us: gathered_plan(): jnp.dot(hidden_low, up_weight, preferred_element_type=f32) + up_bias]
    unnamed x117 -> x20, local copies, waits for them, and re-layouts: 22.3 us -> 8.37 us
    reduce_sum x10 -> x0, other arithmetic: 11.2 us -> none  [the longest x2 4.01 us: norm_back(): jnp.sum(grad_hidden * normal, axis=0)]
  transfers between devices with their start and end apart: 10 -> 0, of which waited for: 9 -> 0; matrix products, arithmetic and copies ran while one was open for 3% -> 0% of each run, Pallas kernels for 0% -> 0%
where the time goes in v2:
time: 193 us
  Pallas kernels  169 us (88%)
  local copies, waits for them, and re-layouts  22.8 us (12%)
    pallas_call x1, Pallas kernels, attention_backward(): pl.pallas_call(functools.partial(backward_kernel, n), out_shape=(whole((r...  82.6 us
    pallas_call x1, Pallas kernels, middle(): pl.pallas_call(middle_kernel, out_shape=(whole((2, rows, LANES), bf16), w...  47.3 us
    pallas_call x1, Pallas kernels, attention_forward(): pl.pallas_call(functools.partial(forward_kernel, n), out_shape=(whole((2,...  39.1 us
    unnamed x20, local copies, waits for them, and re-layouts  8.37 us

profile of v2, /device:TPU:0, one launch (start us, length us, event | category | flops | bytes accessed | tf_op | source)
XLA Modules:
  0.0 192.6 jit_solution(15032848293087488164)
XLA Ops:
  0.7 1.3 broadcast_in_dim.29.out_bias
  1.9 1.3 broadcast_in_dim.30.gain_one
  3.2 1.3 broadcast_in_dim.31.shift_one
  4.5 1.3 broadcast_in_dim.32.up_bias
  5.7 1.3 broadcast_in_dim.33.down_bias
  7.0 1.3 broadcast_in_dim.34.gain_two
  8.3 1.3 broadcast_in_dim.35.shift_two
  9.5 39.1 %attention_forward.1 = (bf16[2,512,128]{2,1,0:T(8,128)(2,1)}, bf16[1024,128]{1,0:T(8,128)(2,1)}, bf16[1024,128]{1,0:T(8,128)(2,1)}, bf16[1152,128]{1,0:T(8,128)(...) custom-call(s32[4]{0:T(128)} %lengths.3, ...), custom_call_target="tpu_custom_call" | custom-call | tf_op jit(solution)/shard_map/attention_forward/pallas_call | solution.py:1212
  48.7 47.3 %middle.1 = (bf16[2,512,128]{2,1,0:T(8,128)(2,1)}, f32[128,768]{1,0:T(8,128)}, bf16[128,768]{1,0:T(8,128)(2,1)}, bf16[128,768]{1,0:T(8,128)(2,1)}, bf16[768,768]...) custom-call(bf16[2,512,128]{2,1,0:T(8,128)(2,1)} %get-tuple-element.46.attn, bf16[512,768]{1,0:T(8,128)(2,1)} %bitcast.13, ...), custom_call_target="tpu_custom_call" | custom-call | tf_op jit(solution)/shard_map/middle/pallas_call | solution.py:1242
  96.0 82.6 %attention_backward.1 = (f32[512,768]{1,0:T(8,128)}, bf16[512,768]{1,0:T(8,128)(2,1)}, f32[96,192]{1,0:T(8,128)}, f32[96,192]{1,0:T(8,128)}, f32[96,192]{1,0:T(8...) custom-call(s32[4]{0:T(128)} %lengths.3, ...), custom_call_target="tpu_custom_call" | custom-call | tf_op jit(solution)/shard_map/attention_backward/pallas_call | solution.py:1281
  178.6 0.0 copy-start
  178.6 1.3 slice.43
  179.9 1.2 slice.35
  181.1 1.3 fusion
  182.5 1.7 slice_reduce_fusion
  184.2 1.9 copy.38
  186.0 2.1 %copy.46 = bf16[4,128,768]{2,1,0:T(8,128)(2,1)} copy(bf16[4,128,768]{2,1,0:T(8,128)(2,1)} %bitcast.22) | data formatting | bytes 1572864
  188.1 0.0 copy-done
  188.1 0.0 copy-start.5
  188.1 0.0 copy-start.2
  188.1 0.0 copy-start.1
  188.1 1.1 copy.47
  189.3 0.0 copy-done.5
  189.3 0.6 copy.48
  189.9 0.0 copy-done.4
  189.9 0.6 copy.49
  190.6 0.0 copy-done.3
  190.6 0.6 copy.50
  191.2 0.0 copy-done.2
  191.2 0.6 copy.51
  191.8 0.0 copy-done.1
  191.8 0.7 copy.52
  (2 shorter events, 0.0 us)
Async XLA Ops:
  178.6 9.5 %copy-start = (f32[512,768]{1,0:T(8,128)S(1)}, f32[512,768]{1,0:T(8,128)}, u32[]{:S(2)}) copy-start(f32[512,768]{1,0:T(8,128)} %get-tuple-element.64) | copy-start | bytes 4718596
  188.1 1.2 copy-start.5
  188.1 1.8 copy-start.4
  188.1 2.5 %copy-start.3 = (f32[96,192]{1,0:T(8,128)S(1)}, f32[96,192]{1,0:T(8,128)}, u32[]{:S(2)}) copy-start(f32[96,192]{1,0:T(8,128)} %get-tuple-element.125) | copy-start | bytes 221188
  188.1 3.1 %copy-start.2 = (f32[192,96]{1,0:T(8,128)S(1)}, f32[192,96]{1,0:T(8,128)}, u32[]{:S(2)}) copy-start(f32[192,96]{1,0:T(8,128)} %get-tuple-element.128) | copy-start | bytes 221188
  188.1 3.7 %copy-start.1 = (f32[96,768]{1,0:T(8,128)S(1)}, f32[96,768]{1,0:T(8,128)}, u32[]{:S(2)}) copy-start(f32[96,768]{1,0:T(8,128)} %get-tuple-element.132) | copy-start | bytes 884740

commit v3 on v0

--- a/solution.py
+++ b/solution.py
@@ -1,6 +1,10 @@
+import functools
+
 import jax
 import jax.numpy as jnp
 from jax import lax
+from jax.experimental import pallas as pl
+from jax.experimental.pallas import tpu as pltpu
 from jax.sharding import PartitionSpec as P
 
 HEADS = 12
@@ -91,7 +95,7 @@
     )
 
 
-def per_device(
+def general_plan(
     tokens,
     lengths,
     query_weight,
@@ -381,9 +385,1033 @@
     )
 
 
+MESH = pl.DeviceIdType.MESH
+LANES = 2 * HEAD_DIM
+f32 = jnp.float32
+bf16 = jnp.bfloat16
+NN = (1, 0)
+NT = (1, 1)
+TN = (0, 0)
+
+
+def dot(a, b, dims=NN):
+    return lax.dot_general(
+        a, b, (((dims[0],), (dims[1],)), ((), ())), preferred_element_type=f32
+    )
+
+
+def split(x):
+    if x.dtype == bf16:
+        return (x,)
+    top = x.astype(bf16)
+    return (top, (x - top.astype(f32)).astype(bf16))
+
+
+def fine(a, b, dims=NN):
+    a, b = split(a), split(b)
+    total = dot(a[0], b[0], dims)
+    if len(b) > 1:
+        total = total + dot(a[0], b[1], dims)
+    if len(a) > 1:
+        total = total + dot(a[1], b[0], dims)
+    return total
+
+
+def iota(shape, dim):
+    return lax.broadcasted_iota(jnp.int32, shape, dim)
+
+
+def block_mask():
+    shape = (LANES, LANES)
+    return (iota(shape, 0) < HEAD_DIM) == (iota(shape, 1) < HEAD_DIM)
+
+
+def eye():
+    return jnp.where(iota((LANES, LANES), 0) == iota((LANES, LANES), 1), 1.0, 0.0).astype(f32)
+
+
+def block_sums(x, same_head):
+    ones = jnp.where(same_head, 1.0, 0.0).astype(bf16)
+    return jnp.where(same_head, fine(fine(ones, x), ones), 1.0)
+
+
+def taps_matrix(row, tok):
+    return pltpu.roll(jnp.broadcast_to(row, (tok, 2 * tok)), 0, 1, stride=1, stride_axis=0)
+
+
+def taps_row(taps, head, tok):
+    row = taps[pl.ds(head, 1), :]
+    return jnp.concatenate([row, jnp.zeros((1, 2 * tok - CONV), f32)], axis=1)
+
+
+def conv_block(matrices, window):
+    first = fine(matrices[0], window)
+    second = fine(matrices[1], window)
+    return jnp.where(iota(first.shape, 1) < HEAD_DIM, first, second)
+
+
+def greet(devices):
+    barrier = pltpu.get_barrier_semaphore()
+    for device in devices:
+        pl.semaphore_signal(barrier, inc=1, device_id=device, device_id_type=MESH)
+    return barrier
+
+
+def around(n, me, tensor):
+    return [(lax.rem(me + d, n), tensor) for d in range(1, n)]
+
+
+def others(me, tensor):
+    core = tensor + 1 - 2 * (tensor % 2)
+    return [(me, core), (me, lax.rem(tensor + 2, 4)), (me, lax.rem(core + 2, 4))]
+
+
+def paired(y):
+    return y[:, :LANES], jnp.concatenate(
+        [y[:, LANES : LANES + HEAD_DIM], y[:, HEAD_DIM:LANES]], axis=1
+    )
+
+
+def remote(src, dst, send, recv, device):
+    return pltpu.make_async_remote_copy(
+        src_ref=src, dst_ref=dst, send_sem=send, recv_sem=recv, device_id=device,
+        device_id_type=MESH,
+    )
+
+
+def member_rows(length, total):
+    j = iota((LANES, total), 0) % LAND
+    t = iota((LANES, total), 1)
+    inside = (t * LAND >= j * length) & (t * LAND < (j + 1) * length) & (t < length)
+    return jnp.where(inside, 1.0, 0.0).astype(bf16)
+
+
+def member_columns(length, total):
+    j = iota((total, LANES), 1) % LAND
+    t = iota((total, LANES), 0)
+    inside = (t * LAND >= j * length) & (t * LAND < (j + 1) * length) & (t < length)
+    return jnp.where(inside, 1.0, 0.0).astype(bf16)
+
+
+def segment_counts(length):
+    j = iota((LANES, LANES), 0) % LAND
+    upper = ((j + 1) * length + LAND - 1) // LAND
+    lower = (j * length + LAND - 1) // LAND
+    return (upper - lower).astype(f32)
+
+
+def normal_of(summed):
+    middle = jnp.mean(summed, axis=-1, keepdims=True)
+    centred = summed - middle
+    inverse_std = lax.rsqrt(jnp.mean(centred * centred, axis=-1, keepdims=True) + epsilon)
+    return centred * inverse_std, inverse_std
+
+
+def before_norm(grad, normal, inverse_std, gain):
+    grad_normal = grad * gain
+    return inverse_std * (
+        grad_normal
+        - jnp.mean(grad_normal, axis=-1, keepdims=True)
+        - normal * jnp.mean(grad_normal * normal, axis=-1, keepdims=True)
+    )
+
+
+def block_rows(t, tok):
+    return pl.ds(pl.multiple_of(t * tok, tok), tok)
+
+
+def gather_and_sum(phase, me, tensor, held, work, ring, filler):
+    tok = held.shape[0] // 4
+    ag_send, ag_recv, sum_send, sum_recv, core_out, core_in, y_out, y_in = ring
+    core, across, far = others(me, tensor)
+    mine = held.at[block_rows(tensor, tok)]
+    to_y = remote(mine, mine, ag_send.at[phase, 0], ag_recv.at[phase, 0], across)
+    to_y.start()
+    to_core = remote(mine, mine, ag_send.at[phase, 1], ag_recv.at[phase, 1], core)
+    to_core.start()
+    total = work(tensor)
+    to_core.wait_recv()
+    core_out[phase, 0] = work(core[1]).astype(bf16)
+    near = remote(
+        core_out.at[phase, 0], core_in.at[phase, 0], sum_send.at[phase, 0], sum_recv.at[phase, 0],
+        core,
+    )
+    near.start()
+    to_y.wait_recv()
+    other = held.at[block_rows(across[1], tok)]
+    pass_on = remote(other, other, ag_send.at[phase, 2], ag_recv.at[phase, 2], core)
+    pass_on.start()
+    part = work(across[1])
+    pass_on.wait_recv()
+    core_out[phase, 1] = work(far[1]).astype(bf16)
+    middle = remote(
+        core_out.at[phase, 1], core_in.at[phase, 1], sum_send.at[phase, 1], sum_recv.at[phase, 1],
+        core,
+    )
+    middle.start()
+    middle.wait_recv()
+    y_out[phase] = (part + core_in[phase, 1].astype(f32)).astype(bf16)
+    last = remote(
+        y_out.at[phase], y_in.at[phase], sum_send.at[phase, 2], sum_recv.at[phase, 2], across
+    )
+    last.start()
+    filler()
+    near.wait_recv()
+    last.wait_recv()
+    total = total + core_in[phase, 0].astype(f32) + y_in[phase].astype(f32)
+    return total, [to_y, to_core, pass_on, near, middle, last]
+
+
+class Scatter:
+    def __init__(self, index, me, tensor, source, buffers, send, recv, order=(0, 1, 2)):
+        self.index, self.source = index, source
+        self.first_in, self.held, self.second_in, self.pair, self.last_in = buffers
+        self.block = source.shape[0] // 8
+        self.weights = [2**bit for bit in order]
+        self.bits = [(me // weight) % 2 for weight in self.weights]
+        self.partners = [
+            (me + weight * (1 - 2 * bit), tensor) for weight, bit in zip(self.weights, self.bits)
+        ]
+        self.send, self.recv = send, recv
+        self.copies = []
+
+    def rows(self, slot, bit):
+        index = (slot // 2) * self.weights[2] + (slot % 2) * self.weights[1] + bit * self.weights[0]
+        return pl.ds(pl.multiple_of(index * self.block, 16), self.block)
+
+    def copy(self, src, dst, k, stage):
+        copy = remote(
+            src, dst, self.send.at[self.index, k], self.recv.at[self.index, k],
+            self.partners[stage],
+        )
+        copy.start()
+        self.copies.append(copy)
+
+    def first(self, slots=range(4)):
+        for slot in slots:
+            self.copy(self.source.at[self.rows(slot, 1 - self.bits[0])], self.first_in.at[slot], slot, 0)
+
+    def second(self):
+        for slot in range(4):
+            self.copies[slot].wait_recv()
+        for slot in range(4):
+            both = self.source[self.rows(slot, self.bits[0])].astype(f32)
+            self.held[slot] = (both + self.first_in[slot].astype(f32)).astype(bf16)
+        for k in range(2):
+            self.copy(self.held.at[2 * k + 1 - self.bits[1]], self.second_in.at[k], 4 + k, 1)
+
+    def third(self):
+        for k in range(2):
+            self.copies[4 + k].wait_recv()
+        for k in range(2):
+            both = self.held[2 * k + self.bits[1]].astype(f32) + self.second_in[k].astype(f32)
+            self.pair[k] = both.astype(bf16)
+        self.copy(self.pair.at[1 - self.bits[2]], self.last_in, 6, 2)
+
+    def last(self):
+        kept, come = self.swapped()
+        return kept.astype(f32) + come.astype(f32)
+
+    def swapped(self):
+        self.copies[6].wait_recv()
+        return self.pair[self.bits[2]], self.last_in[...]
+
+    def finish(self):
+        for copy in self.copies:
+            copy.wait_send()
+
+
+def scatter_buffers(width, block):
+    return [
+        pltpu.VMEM((4, block, width), bf16),
+        pltpu.VMEM((4, block, width), bf16),
+        pltpu.VMEM((2, block, width), bf16),
+        pltpu.VMEM((2, block, width), bf16),
+        pltpu.VMEM((block, width), bf16),
+    ]
+
+
+def total_of(v):
+    return jnp.sum(v, axis=0, keepdims=True)
+
+
+def turn(second, first):
+    low = second.astype(bf16)
+    return jnp.where(iota(low.shape, 1) < HEAD_DIM, low, first)
+
+
+JOBS = 5
+RESULTS = 19
+
+
+def layer_kernel(
+    n, lengths, x_far, wq_far, qb, wk_far, wv_far, vb, taps, out_far, out_bias, gain_one,
+    shift_one, up_far, up_bias, down_far, down_bias, gain_two, shift_two, grad_far,
+    *rest,
+):
+    results, rest = rest[:RESULTS], rest[RESULTS:]
+    ready, rest = rest[:RESULTS], rest[RESULTS:]
+    layer_body(
+        n, lengths, x_far, wq_far, qb, wk_far, wv_far, vb, taps, out_far, out_bias, gain_one,
+        shift_one, up_far, up_bias, down_far, down_bias, gain_two, shift_two, grad_far, results,
+        ready, *rest,
+    )
+
+
+def layer_body(
+    n, lengths, x_far, wq_far, qb, wk_far, wv_far, vb, taps, out_far, out_bias, gain_one,
+    shift_one, up_far, up_bias, down_far, down_bias, gain_two, shift_two, grad_far, results, ready,
+    x, wk, wq, wv, up_weight, down_weight, out_grad, out_whole,
+    stage, ks, qs, vs, k1, p3, newton, out_stage, attn,
+    heads_in, heads_out, grad_attn, hidden, slope, active, down_in, up_in,
+    core_out, core_in, y_out, y_in,
+    gs, back_stage, back_single, come_pair, come_single, weight_in, out_in, early, early_tensor, tokens_own, tokens_low, source_up,
+    source_down, source_out, source_v, source_kq, early_seq, late_seq, tokens_whole,
+    *rest,
+):
+    buffers, sems = rest[: 5 * JOBS], rest[5 * JOBS :]
+    (load, send, recv, out_send, out_recv, whole_send, whole_recv, a2a_send, a2a_recv, ag_send,
+     ag_recv, sum_send, sum_recv, grad_send, grad_recv, back_send, back_recv, share_send,
+     share_recv, small_send, small_recv, job_send, job_recv, own_send, own_recv, store) = sems
+    (output, grad_tokens, grad_query, query_bias, grad_key, grad_value, value_bias, conv, grad_out,
+     out_bias_grad, first_gain, first_shift, grad_up, up_bias_grad, grad_down, down_bias_grad,
+     second_gain, second_shift, proxy) = ready
+    stores = []
+
+    def done(*numbers):
+        for i in numbers:
+            copy = pltpu.make_async_copy(ready[i], results[i], store.at[i])
+            copy.start()
+            stores.append(copy)
+
+    me = lax.axis_index("seq")
+    tensor = lax.axis_index("tensor")
+    rows, width = x.shape
+    batch = n // 2
+    tok = rows // batch
+    total = n * tok
+    half = CONV // 2
+    own, side = me // 2, me % 2
+    scale = HEAD_DIM ** (-0.5)
+    ring_peers = around(n, me, tensor)
+    peers = others(me, tensor)
+    core, across, far = peers
+    mine = block_rows(tensor, tok)
+    local = wk.shape[0]
+    barrier = greet(ring_peers + peers)
+    loads = []
+    for i, (source, target) in enumerate((
+        (x_far, x), (wk_far, wk), (wq_far, wq), (wv_far, wv),
+        (out_far, out_whole.at[tensor, pl.ds(0, local)]), (up_far, up_weight),
+        (down_far, down_weight), (grad_far, out_grad),
+    )):
+        copy = pltpu.make_async_copy(source, target, load.at[i])
+        copy.start()
+        loads.append(copy)
+    jobs = [
+        Scatter(i, me, tensor, source, buffers[5 * i : 5 * i + 5], job_send, job_recv, order)
+        for i, (source, order) in enumerate((
+            (source_down, (0, 1, 2)), (source_up, (0, 1, 2)), (source_out, (0, 1, 2)),
+            (source_v, (1, 2, 0)), (source_kq, (1, 2, 0)),
+        ))
+    ]
+    job_down, job_up, job_out, job_v, job_kq = jobs
+    sent = []
+
+    owned = (ks, qs, vs)
+    offsets = (0, 0, half)
+    for padded in (vs, gs):
+        padded[0:half] = jnp.zeros((half, LANES), bf16)
+        padded[half + total : total + tok] = jnp.zeros((tok - half, LANES), bf16)
+    for t in range(4):
+        out_whole[t, local:] = jnp.zeros((2 * LANES - local, width), bf16)
+
+    arrivals = [[], [], []]
+
+    def spread(i):
+        here = pl.ds(pl.multiple_of(offsets[i] + me * tok, 16), tok)
+        for d in range(1, n):
+            peer = lax.rem(me + d, n)
+            copy = remote(
+                stage.at[i, peer % 2, block_rows(peer // 2, tok)], owned[i].at[here],
+                send.at[i, d - 1], recv.at[i, d - 1], (peer, tensor),
+            )
+            copy.start()
+            arrivals[i].append(copy)
+            if i != 1:
+                sent.append(copy)
+        owned[i][here] = stage[i, side, block_rows(own, tok)]
+
+    loads[0].wait()
+    loads[1].wait()
+    y = dot(x[...], wk[...], NT)
+    stage[0, 0], stage[0, 1] = paired(y.astype(bf16))
+    pl.semaphore_wait(barrier, n + 2)
+    spread(0)
+    loads[2].wait()
+    y = dot(x[...], wq[...], NT) + qb[...].reshape(1, local)
+    stage[1, 0], stage[1, 1] = paired(y.astype(bf16))
+    spread(1)
+    loads[3].wait()
+    y = dot(x[...], wv[...], NT) + vb[...].reshape(1, local)
+    position = me * tok + iota((tok, local), 0)
+    y = jnp.concatenate(
+        [
+            jnp.where(position < lengths[b], y[b * tok : (b + 1) * tok], 0.0)
+            for b in range(batch)
+        ],
+        axis=0,
+    )
+    stage[2, 0], stage[2, 1] = paired(y.astype(bf16))
+    loads[4].wait()
+    whole_parts = []
+    for i, device in enumerate(peers):
+        part = out_whole.at[tensor, pl.ds(0, local)]
+        copy = remote(part, part, whole_send.at[i], whole_recv.at[i], device)
+        copy.start()
+        whole_parts.append(copy)
+
+    length = lengths[own]
+    same_head = block_mask()
+    identity = eye()
+    ones = jnp.where(same_head, 1.0, 0.0).astype(bf16)
+    members = member_rows(length, total)
+    counts = segment_counts(length)
+    matrices = [taps_matrix(taps_row(taps, h, tok), tok) for h in (2 * side, 1)]
+    flip = jnp.where(
+        iota((2 * tok, 2 * tok), 0) + iota((2 * tok, 2 * tok), 1) == CONV - 1, 1.0, 0.0
+    ).astype(bf16)
+    reverse = [
+        taps_matrix(
+            fine(jnp.broadcast_to(taps_row(taps, h, tok), (8, 2 * tok)), flip)[0:1], tok
+        )
+        for h in (2 * side, 1)
+    ]
+    even = side == 0
+    for i, w in enumerate((wk, wq, wv)):
+        pair, single = w[:LANES], w[LANES:]
+        weight_in[i * LANES : (i + 1) * LANES] = jnp.where(
+            even, pair, jnp.concatenate([single, pair[HEAD_DIM:]], axis=0)
+        )
+        start = 3 * LANES + i * HEAD_DIM
+        weight_in[start : start + HEAD_DIM] = jnp.where(even, single, pair[:HEAD_DIM])
+    for copy in arrivals[0]:
+        copy.wait_recv()
+    keys = ks[...]
+    key_marks = jnp.where(same_head, dot(members, keys) / counts, 0.0)
+    for copy in arrivals[1]:
+        copy.wait_send()
+    spread(2)
+    for copy in arrivals[1]:
+        copy.wait_recv()
+    queries = qs[...]
+    query_marks = jnp.where(same_head, dot(members, queries) / counts, 0.0)
+    scores = jnp.where(same_head, fine(query_marks, key_marks, NT) * scale, negative)
+    weights = jnp.exp(scores - jnp.max(scores, axis=1, keepdims=True))
+    kernel_two = weights / jnp.sum(weights, axis=1, keepdims=True)
+    inverse = jnp.where(
+        same_head, kernel_two.T / block_sums(kernel_two * kernel_two, same_head), 0.0
+    )
+    for step in range(NS_ITERS):
+        product = fine(kernel_two, inverse)
+        inner_one = fine(product, 7.0 * identity - product)
+        inner_two = fine(product, 15.0 * identity - inner_one)
+        newton[4 * step] = inverse
+        newton[4 * step + 1] = product
+        newton[4 * step + 2] = inner_one
+        newton[4 * step + 3] = inner_two
+        inverse = 0.25 * fine(inverse, 13.0 * identity - inner_two)
+
+    deviation = identity - fine(kernel_two, inverse)
+    norms = jnp.sqrt(block_sums(deviation * deviation, same_head))
+    first, second = norms[0:1, 0:1], norms[LANES - 1 :, LANES - 1 :]
+    norm_sum = jnp.where(side == 0, first + second, first) / (batch * HEADS)
+    early[7:8] = jnp.broadcast_to(norm_sum, (1, width))
+
+    first_scores = fine(queries, key_marks, NT) * scale
+    left = iota(first_scores.shape, 1) < HEAD_DIM
+    top_left = jnp.max(jnp.where(left, first_scores, negative), axis=1, keepdims=True)
+    top_right = jnp.max(jnp.where(left, negative, first_scores), axis=1, keepdims=True)
+    weights = jnp.exp(first_scores - jnp.where(left, top_left, top_right))
+    k1[...] = weights / fine(weights, ones)
+
+    third_scores = fine(keys, query_marks, NT) * scale
+    alive = iota(third_scores.shape, 0) < length
+    third_scores = jnp.where(alive, third_scores, negative)
+    weights = jnp.exp(third_scores - jnp.max(third_scores, axis=0, keepdims=True))
+    weights = jnp.where(alive, weights, 0.0)
+    third_prob = weights / jnp.sum(weights, axis=0, keepdims=True)
+    p3[...] = third_prob
+
+    for copy in arrivals[2]:
+        copy.wait_recv()
+    values = vs[half : half + total]
+    third_out = jnp.where(same_head, fine(third_prob, values, TN), 0.0)
+    carried = fine(inverse, third_out)
+
+    there = block_rows(own, tok)
+    attn_parts = []
+    for d in range(1, n + 1):
+        peer = lax.rem(me + d, n)
+        start = pl.multiple_of(peer * tok, tok)
+        nystrom = fine(k1[pl.ds(start, tok)], carried)
+        convolved = conv_block(matrices, vs[pl.ds(start, 2 * tok)])
+        low = (nystrom + convolved).astype(bf16)
+        if d == n:
+            attn[side, there] = low
+        else:
+            out_stage[d - 1] = low
+            copy = remote(
+                out_stage.at[d - 1], attn.at[side, there], out_send.at[d - 1], out_recv.at[d - 1],
+                (peer, tensor),
+            )
+            copy.start()
+            attn_parts.append(copy)
+    for copy in whole_parts + attn_parts:
+        copy.wait_recv()
+    sent += whole_parts + attn_parts
+
+    parts = []
+    for i in (2, 1, 0):
+        copy = remote(
+            attn.at[:, block_rows(peers[i][1], tok)], heads_in.at[tensor], a2a_send.at[0, i],
+            a2a_recv.at[0, i], peers[i],
+        )
+        copy.start()
+        parts.append(copy)
+    heads_in[tensor] = attn[:, mine]
+    z, side_of_chip = me // 2, tensor % 2
+    beside = (me + 1 - 2 * side, tensor)
+    token_parts = []
+
+    def give_tokens(src, dst, i, device):
+        copy = remote(src, dst, own_send.at[i], own_recv.at[i], device)
+        copy.start()
+        token_parts.append(copy)
+
+    def half_block(b):
+        start = pl.multiple_of(b * tok + side_of_chip * (tok // 2), tok // 2)
+        return pl.ds(start, tok // 2)
+
+    tokens_own[me, side_of_chip] = x[half_block(own)]
+    for k in range(1, 4):
+        peer = lax.rem(z + k, 4)
+        give_tokens(
+            x.at[half_block(peer)], tokens_own.at[me, side_of_chip], k - 1,
+            (2 * peer + side, tensor),
+        )
+    half_own = tokens_own.at[me, side_of_chip]
+    give_tokens(half_own, half_own, 3, beside)
+
+    def pass_tokens():
+        for k in range(1, 4):
+            token_parts[k - 1].wait_recv()
+        for k in range(1, 4):
+            come = tokens_own.at[2 * lax.rem(z + 4 - k, 4) + side, side_of_chip]
+            give_tokens(come, come, 3 + k, beside)
+
+    for copy in loads[5:]:
+        copy.wait()
+    for copy in parts:
+        copy.wait_recv()
+    sent += parts
+    branch = jnp.zeros((tok, width), f32)
+    for t in range(4):
+        branch = branch + dot(heads_in[t, 0], out_whole[t, :LANES])
+        branch = branch + dot(heads_in[t, 1], out_whole[t, LANES:])
+
+    def line(vector):
+        return vector[...].reshape(1, vector.shape[0])
+
+    first_total = x[mine].astype(f32) + (branch + line(out_bias))
+    normal_one, inverse_one = normal_of(first_total)
+    hidden_one = normal_one * line(gain_one) + line(shift_one)
+    hidden[mine] = hidden_one.astype(bf16)
+    ring = (ag_send, ag_recv, sum_send, sum_recv, core_out, core_in, y_out, y_in)
+
+    def up(t):
+        at = block_rows(t, tok)
+        value = dot(hidden[at], up_weight[...]) + line(up_bias)
+        half_erf = 0.5 * (1.0 + lax.erf(value * (0.5**0.5)))
+        density = jnp.exp(-0.5 * value * value) * (0.5 / jnp.pi) ** 0.5
+        slope[at] = half_erf + value * density
+        low = (value * half_erf).astype(bf16)
+        active[at] = low
+        return dot(low, down_weight[...])
+
+    down_sum, copies = gather_and_sum(0, me, tensor, hidden, up, ring, pass_tokens)
+    sent += copies
+    second_total = hidden_one + (down_sum + line(down_bias))
+    normal_two, inverse_two = normal_of(second_total)
+    output[mine] = (normal_two * line(gain_two) + line(shift_two)).astype(bf16)
+    grad_output = out_grad[mine].astype(f32)
+    grad_second = before_norm(grad_output, normal_two, inverse_two, line(gain_two))
+    low = grad_second.astype(bf16)
+    down_in[mine] = low
+
+    def down(t):
+        at = block_rows(t, tok)
+        low = (dot(down_in[at], down_weight[...], NT) * slope[at]).astype(bf16)
+        up_in[at] = low
+        return dot(low, up_weight[...], NT)
+
+    def fill():
+        source_down[...] = dot(down_in[...], active[...], TN).astype(bf16)
+        job_down.first()
+        source_up[...] = dot(hidden[...], up_in[...], TN).astype(bf16)
+        early[0:1] = total_of(grad_output * normal_two)
+        early[1:2] = total_of(grad_output)
+        early[2:3] = total_of(low.astype(f32))
+        early[6:7] = dot(jnp.ones((8, rows), bf16), up_in[...])[0:1]
+
+    for copy in token_parts[3:7]:
+        copy.wait_recv()
+    half_all = tokens_own.at[:, side_of_chip]
+    give_tokens(half_all, half_all, 7, core)
+    up_sum, copies = gather_and_sum(1, me, tensor, down_in, down, ring, fill)
+    sent += copies
+    grad_hidden = grad_second + up_sum
+    grad_first = before_norm(grad_hidden, normal_one, inverse_one, line(gain_one))
+    low_out = grad_first.astype(bf16)
+    out_in[mine] = low_out
+    parts = []
+    for i in (2, 1, 0):
+        t = peers[i][1]
+        heads_out[i, 0] = dot(low_out, out_whole[t, :LANES], NT).astype(bf16)
+        heads_out[i, 1] = turn(dot(low_out, out_whole[t, LANES:], NT), heads_out[i, 0])
+        copy = remote(
+            heads_out.at[i], grad_attn.at[:, mine], a2a_send.at[1, i], a2a_recv.at[1, i], peers[i]
+        )
+        copy.start()
+        parts.append(copy)
+    own_first = dot(low_out, out_whole[tensor, :LANES], NT).astype(bf16)
+    grad_attn[0, mine] = own_first
+    grad_attn[1, mine] = turn(dot(low_out, out_whole[tensor, LANES:], NT), own_first)
+    sent += parts
+    early[3:4] = total_of(grad_hidden * normal_one)
+    early[4:5] = total_of(grad_hidden)
+    early[5:6] = total_of(low_out.astype(f32))
+    early_tensor[tensor] = early[...]
+    for copy in parts:
+        copy.wait_recv()
+
+    here = pl.ds(pl.multiple_of(half + me * tok, 16), tok)
+    parts = []
+    for d in range(1, n):
+        peer = lax.rem(me + d, n)
+        copy = remote(
+            grad_attn.at[peer % 2, block_rows(peer // 2, tok)], gs.at[here], grad_send.at[d - 1],
+            grad_recv.at[d - 1], (peer, tensor),
+        )
+        copy.start()
+        parts.append(copy)
+    gs[here] = grad_attn[side, block_rows(own, tok)]
+    shares = []
+    for i, held in enumerate((out_in, output)):
+        for j, device in enumerate((across, core)):
+            copy = remote(
+                held.at[mine], held.at[mine], share_send.at[i, j], share_recv.at[i, j], device
+            )
+            copy.start()
+            shares.append(copy)
+    smalls = []
+    for i, device in enumerate(peers):
+        copy = remote(
+            early, early_tensor.at[tensor], small_send.at[0, i], small_recv.at[0, i], device
+        )
+        copy.start()
+        smalls.append(copy)
+    job_up.first(range(2))
+
+    members = member_columns(length, total)
+    outs = []
+
+    def give(i, block):
+        low = block.astype(bf16)
+        blocks = low.reshape(n, 2, tok // 2, LANES)
+        back_stage[i] = low.reshape(n, tok, LANES)
+        back_single[i] = jnp.concatenate(
+            [blocks[:, 0, :, :HEAD_DIM], blocks[:, 1, :, :HEAD_DIM]], axis=2
+        )
+        part = []
+        for d in range(1, n):
+            peer = lax.rem(me + d, n)
+            source, target = (back_stage, come_pair) if d % 2 == 0 else (back_single, come_single)
+            copy = remote(
+                source.at[i, peer], target.at[i, own], back_send.at[i, d - 1],
+                back_recv.at[i, d - 1], (peer, tensor),
+            )
+            copy.start()
+            part.append(copy)
+        come_pair[i, own] = back_stage[i, me]
+        outs.append(part)
+        return low
+
+    job_down.second()
+    for copy in parts:
+        copy.wait_recv()
+    sent += parts
+    job_up.first(range(2, 4))
+    grad = gs[half : half + total]
+    kernel_one = k1[...]
+    grad_carried = jnp.where(same_head, fine(kernel_one, grad, TN), 0.0)
+    grad_third = fine(inverse, grad_carried, TN)
+    grad_inverse = fine(grad_carried, third_out, NT)
+    third_prob = p3[...]
+    convolved = jnp.concatenate(
+        [conv_block(reverse, gs[m * tok : (m + 2) * tok]) for m in range(n)], axis=0
+    )
+    grad_values = fine(third_prob, grad_third) + convolved
+    value_in = give(2, jnp.where(iota(grad_values.shape, 0) < length, grad_values, 0.0))
+
+
+    kernel_back = jnp.zeros((LANES, LANES), f32)
+    grad_state = grad_inverse
+    for step in reversed(range(NS_ITERS)):
+        state, product, inner_one, inner_two = [newton[4 * step + i] for i in range(4)]
+        grad_next = 0.25 * fine(grad_state, 13.0 * identity - inner_two, NT)
+        grad_two = -0.25 * fine(state, grad_state, TN)
+        grad_product = fine(grad_two, 15.0 * identity - inner_one, NT)
+        grad_one = -fine(product, grad_two, TN)
+        grad_product = (
+            grad_product
+            + fine(grad_one, 7.0 * identity - product, NT)
+            - fine(product, grad_one, TN)
+        )
+        grad_state = grad_next + fine(kernel_two, grad_product, TN)
+        kernel_back = kernel_back + fine(grad_product, state, NT)
+    squares = block_sums(kernel_two * kernel_two, same_head)
+    spread_sum = jnp.where(same_head, block_sums(grad_state * newton[0], same_head), 0.0)
+    kernel_back = kernel_back + (grad_state.T - 2.0 * kernel_two * spread_sum) / squares
+    grad_scores = scale * kernel_two * (
+        kernel_back - jnp.sum(kernel_two * kernel_back, axis=1, keepdims=True)
+    )
+    query_two = fine(grad_scores, key_marks)
+    key_two = fine(grad_scores, query_marks, TN)
+
+    grad_one = fine(grad, carried, NT)
+    both = kernel_one * grad_one
+    first_scores = scale * (both - kernel_one * fine(both, ones))
+    key_one = jnp.where(same_head, fine(first_scores, queries, TN), 0.0)
+    delta = fine(jnp.ones((8, LANES), bf16), grad_third * third_out, NT)[0:1]
+    third_scores = scale * third_prob * (fine(values, grad_third, NT) - delta)
+    query_three = jnp.where(same_head, fine(third_scores, keys, TN), 0.0)
+    key_in = give(0, fine(third_scores, query_marks) + fine(members, (key_one + key_two) / counts))
+    query_in = give(1, fine(first_scores, key_marks) + fine(members, (query_two + query_three) / counts))
+
+    for i, held in enumerate((out_in, output)):
+        shares[2 * i].wait_recv()
+        block = held.at[block_rows(across[1], tok)]
+        copy = remote(block, block, share_send.at[i, 2], share_recv.at[i, 2], core)
+        copy.start()
+        shares.append(copy)
+    for copy in smalls:
+        copy.wait_recv()
+    by_tensor = early_tensor[0] + early_tensor[1] + early_tensor[2] + early_tensor[3]
+    early_seq[me] = jnp.where(iota(by_tensor.shape, 0) == 6, early[...], by_tensor)
+    smalls_early = []
+    for d, device in enumerate(ring_peers):
+        copy = remote(
+            early_seq.at[me], early_seq.at[me], small_send.at[1, d], small_recv.at[1, d], device
+        )
+        copy.start()
+        smalls_early.append(copy)
+    position = iota((tok, tok), 0) + iota((tok, tok), 1)
+    upside = jnp.where(position == tok - 1, 1.0, 0.0).astype(bf16)
+    lane = iota((tok, LANES), 1)
+    conv_rows = []
+    for h in range(2):
+        inner = (lane < HEAD_DIM) if h == 0 else (lane >= HEAD_DIM)
+        table = jnp.zeros((tok, 2 * tok), f32)
+        for m in range(n):
+            block = gs[half + m * tok : half + (m + 1) * tok]
+            block = jnp.where(inner, block, jnp.zeros_like(block))
+            table = table + dot(block, vs[m * tok : (m + 2) * tok], NT)
+        table = pltpu.roll(fine(upside, table), 0, 1, stride=1, stride_axis=0)
+        row = jnp.sum(table, axis=0, keepdims=True)
+        row = pltpu.roll(jnp.broadcast_to(row, (8, 2 * tok)), tok + 1, 1)
+        conv_rows.append(row[0:1, :LANES])
+    shares[1].wait_recv()
+    shares[4].wait_recv()
+    attention = jnp.concatenate([attn[0], attn[1, :, :HEAD_DIM]], axis=1)
+    source_out[...] = dot(out_in[...], attention, TN).astype(bf16)
+    job_out.first()
+    token_parts[7].wait_recv()
+    sent += token_parts
+    tokens_all = tokens_own[...].reshape(total, width)
+    source_v[...] = dot(tokens_all, value_in, TN).astype(bf16)
+    source_kq[:, :LANES] = dot(tokens_all, key_in, TN).astype(bf16)
+    source_kq[:, LANES:] = dot(tokens_all, query_in, TN).astype(bf16)
+    job_v.first()
+    job_kq.first()
+    late = late_seq.at[me]
+    late[...] = jnp.zeros(late.shape, f32)
+    column = jnp.ones((8, total), bf16)
+    for row, v in ((0, query_in), (1, value_in)):
+        v = dot(column, v)[0:1]
+        late[row : row + 1, 0:LANES] = jnp.where(even, v, 0.0)
+        late[row : row + 1, LANES:local] = jnp.where(even, 0.0, v[:, :HEAD_DIM])
+    late[2:3, 0:LANES] = jnp.where(even, conv_rows[0], 0.0)
+    late[3:4, 0:LANES] = jnp.where(even, conv_rows[1], 0.0)
+    late[4:5, 0:LANES] = jnp.where(even, 0.0, conv_rows[0])
+    smalls_late = []
+    for d, device in enumerate(ring_peers):
+        copy = remote(late, late, small_send.at[2, d], small_recv.at[2, d], device)
+        copy.start()
+        smalls_late.append(copy)
+    job_up.second()
+    job_down.third()
+
+    for part in outs:
+        for copy in part:
+            copy.wait_recv()
+    singles = []
+    for i in range(3):
+        tokens_low[:, i * LANES : (i + 1) * LANES] = come_pair[i].reshape(rows, LANES)
+        packed = come_single[i]
+        single = jnp.concatenate([packed[:, :, :HEAD_DIM], packed[:, :, HEAD_DIM:]], axis=1)
+        singles.append(single.reshape(rows, HEAD_DIM))
+    tokens_low[:, 3 * LANES :] = jnp.concatenate(singles, axis=1)
+
+    def input_part(t):
+        return dot(tokens_low[block_rows(t, tok)], weight_in[...])
+
+    def pass_sum(k, value, device):
+        core_out[2, k] = value.astype(bf16)
+        copy = remote(
+            core_out.at[2, k], core_in.at[2, k], sum_send.at[2, k], sum_recv.at[2, k], device
+        )
+        copy.start()
+        sent.append(copy)
+        return copy
+
+    middle = pass_sum(1, input_part(far[1]), core)
+    near = pass_sum(0, input_part(core[1]), core)
+    part = input_part(across[1])
+    middle.wait_recv()
+    y_out[2] = (part + core_in[2, 1].astype(f32)).astype(bf16)
+    final = remote(y_out.at[2], y_in.at[2], sum_send.at[2, 2], sum_recv.at[2, 2], across)
+    final.start()
+    sent.append(final)
+    result = input_part(tensor) + grad_first
+    job_out.second()
+    job_v.second()
+    near.wait_recv()
+    final.wait_recv()
+    result = result + core_in[2, 0].astype(f32) + y_in[2].astype(f32)
+    tokens_whole[mine] = result.astype(bf16)
+    ends = []
+    for j, device in enumerate((across, core)):
+        copy = remote(
+            tokens_whole.at[mine], tokens_whole.at[mine], share_send.at[2, j], share_recv.at[2, j],
+            device,
+        )
+        copy.start()
+        ends.append(copy)
+    job_up.third()
+    job_kq.second()
+    job_out.third()
+    job_v.third()
+    grad_down[...] = job_down.last()
+    done(14)
+    for copy in smalls_early + smalls_late:
+        copy.wait_recv()
+    by_seq = functools.reduce(lambda a, b: a + b, [early_seq[i] for i in range(n)])
+    for ref, row in (
+        (second_gain, 0), (second_shift, 1), (down_bias_grad, 2), (first_gain, 3),
+        (first_shift, 4), (out_bias_grad, 5), (up_bias_grad, 6),
+    ):
+        ref[...] = by_seq[row]
+    proxy[...] = by_seq[7:8, 0:1]
+    by_seq = functools.reduce(lambda a, b: a + b, [late_seq[i] for i in range(n)])
+    query_bias[...] = by_seq[0, :local]
+    value_bias[...] = by_seq[1, :local]
+    conv[...] = by_seq[2:5, :CONV]
+    shares[3].wait_recv()
+    shares[5].wait_recv()
+    done(0, 3, 6, 7, 9, 10, 11, 13, 15, 16, 17, 18)
+    ends[0].wait_recv()
+    block = tokens_whole.at[block_rows(across[1], tok)]
+    copy = remote(block, block, share_send.at[2, 2], share_recv.at[2, 2], core)
+    copy.start()
+    ends.append(copy)
+    job_kq.third()
+    grad_up[...] = job_up.last()
+    done(12)
+    grad_out[...] = job_out.last().T
+    done(8)
+
+    def heads(job, *refs):
+        kept, come = job.swapped()
+        pair, single = jnp.where(even, kept, come), jnp.where(even, come, kept)
+        for i, ref in enumerate(refs):
+            ref[:, :LANES] = pair[:, i * LANES : (i + 1) * LANES].astype(f32)
+            ref[:, LANES:] = single[:, i * LANES : i * LANES + HEAD_DIM].astype(f32)
+
+    heads(job_v, grad_value)
+    done(5)
+    ends[1].wait_recv()
+    ends[2].wait_recv()
+    grad_tokens[...] = tokens_whole[...].astype(f32)
+    done(1)
+    heads(job_kq, grad_key, grad_query)
+    done(2, 4)
+    for copy in sent + shares + smalls + smalls_early + smalls_late + ends:
+        copy.wait_send()
+    for part in outs:
+        for copy in part:
+            copy.wait_send()
+    for job in jobs:
+        job.finish()
+    for copy in stores:
+        copy.wait()
+
+
+def finish_kernel(*refs):
+    come, go, held = [refs[i * RESULTS : (i + 1) * RESULTS] for i in range(3)]
+    loads, stores = refs[3 * RESULTS :]
+    copies = [
+        pltpu.make_async_copy(come[i], held[i], loads.at[i]) for i in range(RESULTS)
+    ]
+    for copy in copies:
+        copy.start()
+    outs = []
+    for i in range(RESULTS):
+        copies[i].wait()
+        copy = pltpu.make_async_copy(held[i], go[i], stores.at[i])
+        copy.start()
+        outs.append(copy)
+    for copy in outs:
+        copy.wait()
+
+
+def whole(shape, dtype):
+    return jax.ShapeDtypeStruct(shape, dtype)
+
+
+VMEM = pl.BlockSpec(memory_space=pltpu.VMEM)
+SMEM = pl.BlockSpec(memory_space=pltpu.SMEM)
+HBM = pl.BlockSpec(memory_space=pl.ANY)
+
+
+def dma(*shape):
+    return pltpu.SemaphoreType.DMA(shape)
+
+
+def gathered_plan(
+    n, tokens, lengths, query_weight, query_bias, key_weight, value_weight, value_bias,
+    conv_kernel, out_weight, out_bias, first_gain, first_shift, up_weight, up_bias, down_weight,
+    down_bias, second_gain, second_shift, out_grad,
+):
+    batch, tok, width = tokens.shape
+    rows = batch * tok
+    local = query_weight.shape[1]
+    hidden = up_weight.shape[1]
+    total = n * tok
+    block = width // n
+
+    def low(*shape):
+        return pltpu.VMEM(shape, bf16)
+
+    def wide(*shape):
+        return pltpu.VMEM(shape, f32)
+
+    results = (
+        whole((rows, width), bf16),
+        whole((rows, width), f32),
+        whole((block, local), f32),
+        whole((local,), f32),
+        whole((block, local), f32),
+        whole((block, local), f32),
+        whole((local,), f32),
+        whole(conv_kernel.shape, f32),
+        whole((local, block), f32),
+        whole((width,), f32),
+        whole((width,), f32),
+        whole((width,), f32),
+        whole((block, hidden), f32),
+        whole((hidden,), f32),
+        whole((block, hidden), f32),
+        whole((width,), f32),
+        whole((width,), f32),
+        whole((width,), f32),
+        whole((1, 1), f32),
+    )
+    outs = pl.pallas_call(
+        functools.partial(layer_kernel, n),
+        out_shape=results,
+        in_specs=[SMEM, HBM, HBM, VMEM, HBM, HBM, VMEM, VMEM, HBM, VMEM, VMEM, VMEM, HBM, VMEM, HBM,
+                  VMEM, VMEM, VMEM, HBM],
+        out_specs=(HBM,) * RESULTS,
+        scratch_shapes=[pltpu.VMEM(r.shape, r.dtype) for r in results]
+        + [
+            low(rows, width), low(local, width), low(local, width), low(local, width),
+            low(width, hidden), low(hidden, width), low(rows, width), low(4, 2 * LANES, width),
+            low(3, 2, rows, LANES), low(total, LANES), low(total, LANES), low(total + tok, LANES),
+            wide(total, LANES), wide(total, LANES), wide(4 * NS_ITERS, LANES, LANES),
+            low(n - 1, tok, LANES), low(2, rows, LANES),
+            low(4, 2, tok, LANES), low(3, 2, tok, LANES), low(2, rows, LANES), low(rows, width),
+            wide(rows, hidden), low(rows, hidden), low(rows, width), low(rows, hidden),
+            low(3, 2, tok, width), low(3, 2, tok, width), low(3, tok, width), low(3, tok, width),
+            low(total + tok, LANES), low(3, n, tok, LANES), low(3, n, tok // 2, LANES),
+            low(3, batch, tok, LANES), low(3, batch, tok // 2, LANES), low(3 * local, width),
+            low(rows, width), wide(8, width), wide(4, 8, width), low(n, 2, tok // 2, width),
+            low(rows, 3 * local), low(width, hidden), low(width, hidden), low(width, local),
+            low(width, LANES), low(width, 2 * LANES), wide(n, 8, width), wide(n, 8, width),
+            low(rows, width),
+        ]
+        + [
+            b
+            for w in (hidden, hidden, local, LANES, 2 * LANES)
+            for b in scatter_buffers(w, block)
+        ]
+        + [
+            dma(8), dma(3, n - 1), dma(3, n - 1), dma(n - 1), dma(n - 1), dma(3), dma(3),
+            dma(2, 3), dma(2, 3), dma(2, 3), dma(2, 3), dma(3, 3), dma(3, 3), dma(n - 1),
+            dma(n - 1), dma(3, n - 1), dma(3, n - 1), dma(3, 3), dma(3, 3), dma(3, n - 1),
+            dma(3, n - 1), dma(JOBS, 7), dma(JOBS, 7), dma(8), dma(8), dma(RESULTS),
+        ],
+        compiler_params=pltpu.CompilerParams(
+            collective_id=0, has_side_effects=True, vmem_limit_bytes=56 * 2**20
+        ),
+        name="layer",
+    )(
+        lengths, tokens.reshape(rows, width), query_weight.T, query_bias, key_weight.T,
+        value_weight.T, value_bias, conv_kernel, out_weight, out_bias, first_gain, first_shift,
+        up_weight, up_bias, down_weight, down_bias, second_gain, second_shift,
+        out_grad.reshape(rows, width),
+    )
+    outs = pl.pallas_call(
+        finish_kernel,
+        out_shape=results,
+        in_specs=[HBM] * RESULTS,
+        out_specs=(HBM,) * RESULTS,
+        scratch_shapes=[pltpu.VMEM(r.shape, r.dtype) for r in results]
+        + [dma(RESULTS), dma(RESULTS)],
+        compiler_params=pltpu.CompilerParams(vmem_limit_bytes=60 * 2**20),
+        name="finish",
+    )(*outs)
+    return (
+        outs[0].reshape(tokens.shape),
+        outs[1].reshape(tokens.shape),
+        *outs[2:14],
+        outs[14].T,
+        *outs[15:18],
+        outs[18].reshape(()),
+    )
+
+
+def per_device(seq, tensor, *args):
+    batch, tok, width = args[0].shape
+    heads = args[7].shape[0]
+    if seq == 8 and tensor == 4 and batch == 4 and heads == 3 and tok == 128:
+        return gathered_plan(seq, *args)
+    return general_plan(*args)
+
+
 def solution(mesh):
     return jax.shard_map(
-        per_device,
+        functools.partial(per_device, mesh.shape["seq"], mesh.shape["tensor"]),
         mesh=mesh,
         in_specs=(
             P(None, "seq", None),

time: 1060 us -> 152 us (0.14)
  the two profiles are of different devices: /device:TPU:0 before, /device:TPU:10 now
where the time goes in v3:
time: 152 us
  Pallas kernels  151 us (99%)
    pallas_call x1, Pallas kernels, gathered_plan(): pl.pallas_call(functools.partial(layer_kernel, n), out_shape=results, in_...  147 us
    pallas_call x1, Pallas kernels, gathered_plan(): pl.pallas_call(finish_kernel, out_shape=results, in_specs=[HBM] * RESULTS...  4.06 us

profile of v3, /device:TPU:10, one launch (start us, length us, event | category | flops | bytes accessed | tf_op | source)
XLA Modules:
  0.0 152.1 jit_solution(5554558964031897242)
XLA Ops:
  0.7 147.2 %layer.1 = (bf16[512,768]{1,0:T(8,128)(2,1)}, f32[512,768]{1,0:T(8,128)}, f32[96,192]{1,0:T(8,128)}, f32[192]{0:T(256)}, f32[96,192]{1,0:T(8,128)}, /*index=5*/f...) custom-call(s32[4]{0:T(128)} %lengths.1, ...), custom_call_target="tpu_custom_call" | custom-call | tf_op jit(solution)/shard_map/layer/pallas_call | solution.py:1340
  147.9 4.1 %finish.1 = (bf16[512,768]{1,0:T(8,128)(2,1)}, f32[512,768]{1,0:T(8,128)}, f32[96,192]{1,0:T(8,128)}, f32[192]{0:T(256)}, f32[96,192]{1,0:T(8,128)}, /*index=5*/...) custom-call(bf16[512,768]{1,0:T(8,128)(2,1)} %get-tuple-element.57.r, ...), custom_call_target="tpu_custom_call" | custom-call | tf_op jit(solution)/shard_map/finish/pallas_call | solution.py:1384

commit v4 on v3

--- a/solution.py
+++ b/solution.py
@@ -520,52 +520,10 @@
     return pl.ds(pl.multiple_of(t * tok, tok), tok)
 
 
-def gather_and_sum(phase, me, tensor, held, work, ring, filler):
-    tok = held.shape[0] // 4
-    ag_send, ag_recv, sum_send, sum_recv, core_out, core_in, y_out, y_in = ring
-    core, across, far = others(me, tensor)
-    mine = held.at[block_rows(tensor, tok)]
-    to_y = remote(mine, mine, ag_send.at[phase, 0], ag_recv.at[phase, 0], across)
-    to_y.start()
-    to_core = remote(mine, mine, ag_send.at[phase, 1], ag_recv.at[phase, 1], core)
-    to_core.start()
-    total = work(tensor)
-    to_core.wait_recv()
-    core_out[phase, 0] = work(core[1]).astype(bf16)
-    near = remote(
-        core_out.at[phase, 0], core_in.at[phase, 0], sum_send.at[phase, 0], sum_recv.at[phase, 0],
-        core,
-    )
-    near.start()
-    to_y.wait_recv()
-    other = held.at[block_rows(across[1], tok)]
-    pass_on = remote(other, other, ag_send.at[phase, 2], ag_recv.at[phase, 2], core)
-    pass_on.start()
-    part = work(across[1])
-    pass_on.wait_recv()
-    core_out[phase, 1] = work(far[1]).astype(bf16)
-    middle = remote(
-        core_out.at[phase, 1], core_in.at[phase, 1], sum_send.at[phase, 1], sum_recv.at[phase, 1],
-        core,
-    )
-    middle.start()
-    middle.wait_recv()
-    y_out[phase] = (part + core_in[phase, 1].astype(f32)).astype(bf16)
-    last = remote(
-        y_out.at[phase], y_in.at[phase], sum_send.at[phase, 2], sum_recv.at[phase, 2], across
-    )
-    last.start()
-    filler()
-    near.wait_recv()
-    last.wait_recv()
-    total = total + core_in[phase, 0].astype(f32) + y_in[phase].astype(f32)
-    return total, [to_y, to_core, pass_on, near, middle, last]
-
-
 class Scatter:
-    def __init__(self, index, me, tensor, source, buffers, send, recv, order=(0, 1, 2)):
-        self.index, self.source = index, source
-        self.first_in, self.held, self.second_in, self.pair, self.last_in = buffers
+    def __init__(self, index, me, tensor, source, columns, buffers, send, recv, order):
+        self.index, self.source, self.columns = index, source, pl.ds(*columns)
+        self.first_in, self.held, self.second_in, self.pair, self.last_in, self.cross_in = buffers
         self.block = source.shape[0] // 8
         self.weights = [2**bit for bit in order]
         self.bits = [(me // weight) % 2 for weight in self.weights]
@@ -589,16 +547,19 @@
 
     def first(self, slots=range(4)):
         for slot in slots:
-            self.copy(self.source.at[self.rows(slot, 1 - self.bits[0])], self.first_in.at[slot], slot, 0)
+            self.copy(self.source.at[self.rows(slot, 1 - self.bits[0]), self.columns], self.first_in.at[slot], slot, 0)
 
     def second(self):
         for slot in range(4):
             self.copies[slot].wait_recv()
         for slot in range(4):
-            both = self.source[self.rows(slot, self.bits[0])].astype(f32)
-            self.held[slot] = (both + self.first_in[slot].astype(f32)).astype(bf16)
+            mine = self.source[self.rows(slot, self.bits[0]), self.columns]
+            self.held[slot] = self.joined(mine, self.first_in[slot])
         for k in range(2):
             self.copy(self.held.at[2 * k + 1 - self.bits[1]], self.second_in.at[k], 4 + k, 1)
+
+    def joined(self, mine, come):
+        return (mine.astype(f32) + come.astype(f32)).astype(bf16)
 
     def third(self):
         for k in range(2):
@@ -608,26 +569,118 @@
             self.pair[k] = both.astype(bf16)
         self.copy(self.pair.at[1 - self.bits[2]], self.last_in, 6, 2)
 
-    def last(self):
-        kept, come = self.swapped()
-        return kept.astype(f32) + come.astype(f32)
-
-    def swapped(self):
+    def last(self, write):
         self.copies[6].wait_recv()
-        return self.pair[self.bits[2]], self.last_in[...]
+        write(self.pair[self.bits[2]].astype(f32) + self.last_in[...].astype(f32))
 
     def finish(self):
         for copy in self.copies:
             copy.wait_send()
 
 
-def scatter_buffers(width, block):
+class Line(Scatter):
+    def __init__(self, *args):
+        super().__init__(*args)
+        z = self.bits[1] + 2 * self.bits[2]
+        right = z // 2
+        self.end = self.bits[1] == right
+        self.inner = self.bits[1] != right
+        self.slots = [k * (1 - right) + (3 - k) * right for k in range(4)]
+        self.partners[2] = (2 * (3 - z) + self.bits[0], self.partners[0][1])
+        self.own = {}
+
+    def step(self, src, dst, k, stage):
+        copy = remote(
+            src, dst, self.send.at[self.index, k], self.recv.at[self.index, k],
+            self.partners[stage],
+        )
+        self.own[k] = copy
+        return copy
+
+    def second(self):
+        for slot in range(4):
+            self.copies[slot].wait_recv()
+        for slot in range(4):
+            mine = self.source[self.rows(slot, self.bits[0]), self.columns]
+            self.held[slot] = self.joined(mine, self.first_in[slot])
+        come = (self.second_in.at[0], self.second_in.at[1], self.last_in)
+        sends = [
+            self.step(self.held.at[self.slots[3 - k]], come[k], 4 + k, 1) for k in range(3)
+        ]
+
+        @pl.when(self.end)
+        def _():
+            for copy in sends:
+                copy.start()
+
+    def third(self):
+        sends = [
+            self.step(self.pair.at[k], self.cross_in.at[k], 7 + k, 2) for k in range(2)
+        ]
+
+        @pl.when(self.inner)
+        def _():
+            for k in range(2):
+                self.own[4 + k].wait_recv()
+                self.pair[k] = self.joined(self.held[self.slots[3 - k]], self.second_in[k])
+                sends[k].start()
+
+    def fourth(self):
+        back = self.step(self.first_in.at[2], self.first_in.at[3], 9, 1)
+
+        @pl.when(self.inner)
+        def _():
+            self.own[7].wait_recv()
+            self.first_in[2] = self.joined(self.held[self.slots[0]], self.cross_in[0])
+            back.start()
+
+    def last(self, write):
+        @pl.when(self.inner)
+        def _():
+            self.own[6].wait_recv()
+            self.own[8].wait_recv()
+            write(
+                self.held[self.slots[1]].astype(f32)
+                + self.last_in[...].astype(f32)
+                + self.cross_in[1].astype(f32)
+            )
+
+        @pl.when(self.end)
+        def _():
+            self.own[9].wait_recv()
+            write(self.held[self.slots[0]].astype(f32) + self.first_in[3].astype(f32))
+
+    def finish(self):
+        super().finish()
+
+        @pl.when(self.end)
+        def _():
+            for k in range(4, 7):
+                self.own[k].wait_send()
+
+        @pl.when(self.inner)
+        def _():
+            for k in range(7, 10):
+                self.own[k].wait_send()
+
+
+class Heads(Scatter):
+    def joined(self, mine, come):
+        even = self.bits[0] == 0
+        pair, other = jnp.where(even, mine, come), jnp.where(even, come, mine)
+        return jnp.concatenate(
+            [pair] + [other[:, k : k + HEAD_DIM] for k in range(0, other.shape[1], LANES)], axis=1
+        )
+
+
+def scatter_buffers(first, width, block):
     return [
-        pltpu.VMEM((4, block, width), bf16),
+        pltpu.VMEM((4, block, first), bf16),
         pltpu.VMEM((4, block, width), bf16),
         pltpu.VMEM((2, block, width), bf16),
         pltpu.VMEM((2, block, width), bf16),
         pltpu.VMEM((block, width), bf16),
+        pltpu.VMEM((2, block, width), bf16),
     ]
 
 
@@ -635,12 +688,82 @@
     return jnp.sum(v, axis=0, keepdims=True)
 
 
-def turn(second, first):
-    low = second.astype(bf16)
-    return jnp.where(iota(low.shape, 1) < HEAD_DIM, low, first)
-
-
-JOBS = 5
+def packed(block):
+    middle = block.shape[-2] // 2
+    first, second = block[..., :middle, :HEAD_DIM], block[..., middle:, :HEAD_DIM]
+    return jnp.concatenate([first, second], axis=-1)
+
+
+def unpacked(block):
+    return jnp.concatenate([block[..., :HEAD_DIM], block[..., HEAD_DIM:]], axis=-2)
+
+
+class Ring:
+    def __init__(
+        self, tensor, peers, parts, core_out, core_in, y_out, y_in, ag_send, ag_recv, sum_send,
+        sum_recv,
+    ):
+        self.tensor, self.place = tensor, tensor % 2
+        self.core, self.across, self.far = peers
+        self.near_pair = tensor - self.place
+        self.far_pair = lax.rem(self.near_pair + 2, 4)
+        self.parts, self.core_out, self.core_in = parts, core_out, core_in
+        self.y_out, self.y_in = y_out, y_in
+        self.ag, self.sums = (ag_send, ag_recv), (sum_send, sum_recv)
+        self.copies = {}
+
+    def send(self, name, src, dst, sems, at, device):
+        copy = remote(src, dst, sems[0].at[at], sems[1].at[at], device)
+        copy.start()
+        self.copies[name] = copy
+
+    def share(self, phase, c, held):
+        mine = held.at[c, self.tensor]
+        self.send((phase, c, "y"), mine, mine, self.ag, (phase, c, 0), self.across)
+        self.send((phase, c, "core"), mine, mine, self.ag, (phase, c, 1), self.core)
+
+    def work(self, phase, c, side, value):
+        self.parts[phase, c, side] = value.reshape(2, -1, value.shape[1])
+        self.core_out[phase, c, side] = self.parts[phase, c, side, 1 - self.place].astype(bf16)
+        self.send(
+            (phase, c, side), self.core_out.at[phase, c, side], self.core_in.at[phase, c, side],
+            self.sums, (phase, c, side), self.core,
+        )
+
+    def run(self, phase, held, work):
+        for c in range(2):
+            self.copies[phase, c, "core"].wait_recv()
+            self.work(phase, c, 0, work(c, self.near_pair))
+        for c in range(2):
+            self.copies[phase, c, "y"].wait_recv()
+            other = held.at[c, self.across[1]]
+            self.send((phase, c, "pass"), other, other, self.ag, (phase, c, 2), self.core)
+            if c == 1:
+                self.cross(phase, 0)
+            self.copies[phase, c, "pass"].wait_recv()
+            self.work(phase, c, 1, work(c, self.far_pair))
+        self.cross(phase, 1)
+
+    def cross(self, phase, c):
+        self.copies[phase, c, 1].wait_recv()
+        both = self.parts[phase, c, 1, self.place] + self.core_in[phase, c, 1].astype(f32)
+        self.y_out[phase, c] = both.astype(bf16)
+        self.send(
+            (phase, c, "sum"), self.y_out.at[phase, c], self.y_in.at[phase, c], self.sums,
+            (phase, c, 2), self.across,
+        )
+
+    def total(self, phase, c):
+        self.copies[phase, c, 0].wait_recv()
+        self.copies[phase, c, "sum"].wait_recv()
+        return (
+            self.parts[phase, c, 0, self.place]
+            + self.core_in[phase, c, 0].astype(f32)
+            + self.y_in[phase, c].astype(f32)
+        )
+
+
+JOBS = 7
 RESULTS = 19
 
 
@@ -661,18 +784,20 @@
 def layer_body(
     n, lengths, x_far, wq_far, qb, wk_far, wv_far, vb, taps, out_far, out_bias, gain_one,
     shift_one, up_far, up_bias, down_far, down_bias, gain_two, shift_two, grad_far, results, ready,
-    x, wk, wq, wv, up_weight, down_weight, out_grad, out_whole,
-    stage, ks, qs, vs, k1, p3, newton, out_stage, attn,
-    heads_in, heads_out, grad_attn, hidden, slope, active, down_in, up_in,
-    core_out, core_in, y_out, y_in,
+    x, wk, wq, wv, up_weight, down_weight, out_grad, out_weight, out_whole,
+    stage, ks, qs, vs, k1, p3, newton, out_stage, out_single, attn_pair, attn_single,
+    pairs_in, singles_in, heads_out, grad_attn, hidden, slope, active, down_in, up_in,
+    core_out, core_in, y_out, y_in, core_last, y_last,
     gs, back_stage, back_single, come_pair, come_single, weight_in, out_in, early, early_tensor, tokens_own, tokens_low, source_up,
-    source_down, source_out, source_v, source_kq, early_seq, late_seq, tokens_whole,
+    source_down, source_out, source_v, source_kq, early_out, early_in, late_seq, tokens_whole,
+    parts_held,
     *rest,
 ):
-    buffers, sems = rest[: 5 * JOBS], rest[5 * JOBS :]
+    buffers, sems = rest[: 6 * JOBS], rest[6 * JOBS :]
     (load, send, recv, out_send, out_recv, whole_send, whole_recv, a2a_send, a2a_recv, ag_send,
      ag_recv, sum_send, sum_recv, grad_send, grad_recv, back_send, back_recv, share_send,
-     share_recv, small_send, small_recv, job_send, job_recv, own_send, own_recv, store) = sems
+     share_recv, small_send, small_recv, job_send, job_recv, own_send, own_recv, last_send, last_recv,
+     store) = sems
     (output, grad_tokens, grad_query, query_bias, grad_key, grad_value, value_bias, conv, grad_out,
      out_bias_grad, first_gain, first_shift, grad_up, up_bias_grad, grad_down, down_bias_grad,
      second_gain, second_shift, proxy) = ready
@@ -702,20 +827,28 @@
     loads = []
     for i, (source, target) in enumerate((
         (x_far, x), (wk_far, wk), (wq_far, wq), (wv_far, wv),
-        (out_far, out_whole.at[tensor, pl.ds(0, local)]), (up_far, up_weight),
+        (out_far, out_weight), (up_far, up_weight),
         (down_far, down_weight), (grad_far, out_grad),
     )):
         copy = pltpu.make_async_copy(source, target, load.at[i])
         copy.start()
         loads.append(copy)
+    hidden_width = up_weight.shape[1]
+    span = hidden_width // 2
     jobs = [
-        Scatter(i, me, tensor, source, buffers[5 * i : 5 * i + 5], job_send, job_recv, order)
-        for i, (source, order) in enumerate((
-            (source_down, (0, 1, 2)), (source_up, (0, 1, 2)), (source_out, (0, 1, 2)),
-            (source_v, (1, 2, 0)), (source_kq, (1, 2, 0)),
+        kind(i, me, tensor, source, columns, buffers[6 * i : 6 * i + 6], job_send, job_recv, order)
+        for i, (kind, source, columns, order) in enumerate((
+            (Line, source_down, (0, span), (0, 1, 2)),
+            (Scatter, source_down, (span, span), (1, 0, 2)),
+            (Line, source_up, (0, span), (0, 1, 2)),
+            (Line, source_up, (span, span), (0, 1, 2)),
+            (Scatter, source_out, (0, local), (0, 1, 2)),
+            (Heads, source_v, (0, LANES), (0, 1, 2)),
+            (Heads, source_kq, (0, 2 * LANES), (0, 1, 2)),
         ))
     ]
-    job_down, job_up, job_out, job_v, job_kq = jobs
+    job_down, job_up = jobs[0:2], jobs[2:4]
+    job_out, job_v, job_kq = jobs[4:]
     sent = []
 
     owned = (ks, qs, vs)
@@ -723,8 +856,7 @@
     for padded in (vs, gs):
         padded[0:half] = jnp.zeros((half, LANES), bf16)
         padded[half + total : total + tok] = jnp.zeros((tok - half, LANES), bf16)
-    for t in range(4):
-        out_whole[t, local:] = jnp.zeros((2 * LANES - local, width), bf16)
+    even = side == 0
 
     arrivals = [[], [], []]
 
@@ -765,11 +897,19 @@
     stage[2, 0], stage[2, 1] = paired(y.astype(bf16))
     loads[4].wait()
     whole_parts = []
+    pair_rows = block_rows(tensor, LANES)
+    single_rows = pl.ds(pl.multiple_of(4 * LANES + tensor * HEAD_DIM, HEAD_DIM), HEAD_DIM)
+    first, single = out_weight[:LANES], out_weight[LANES:]
+    out_whole[pair_rows] = jnp.where(
+        even, first, jnp.concatenate([single, first[HEAD_DIM:]], axis=0)
+    )
+    out_whole[single_rows] = jnp.where(even, single, first[:HEAD_DIM])
     for i, device in enumerate(peers):
-        part = out_whole.at[tensor, pl.ds(0, local)]
-        copy = remote(part, part, whole_send.at[i], whole_recv.at[i], device)
-        copy.start()
-        whole_parts.append(copy)
+        for j, at in enumerate((pair_rows, single_rows)):
+            part = out_whole.at[at]
+            copy = remote(part, part, whole_send.at[i, j], whole_recv.at[i, j], device)
+            copy.start()
+            whole_parts.append(copy)
 
     length = lengths[own]
     same_head = block_mask()
@@ -787,7 +927,6 @@
         )
         for h in (2 * side, 1)
     ]
-    even = side == 0
     for i, w in enumerate((wk, wq, wv)):
         pair, single = w[:LANES], w[LANES:]
         weight_in[i * LANES : (i + 1) * LANES] = jnp.where(
@@ -849,7 +988,6 @@
     third_out = jnp.where(same_head, fine(third_prob, values, TN), 0.0)
     carried = fine(inverse, third_out)
 
-    there = block_rows(own, tok)
     attn_parts = []
     for d in range(1, n + 1):
         peer = lax.rem(me + d, n)
@@ -858,28 +996,32 @@
         convolved = conv_block(matrices, vs[pl.ds(start, 2 * tok)])
         low = (nystrom + convolved).astype(bf16)
         if d == n:
-            attn[side, there] = low
+            attn_pair[own] = low
+            continue
+        if d % 2 == 0:
+            source, target = out_stage.at[d - 1], attn_pair.at[own]
+            source[...] = low
         else:
-            out_stage[d - 1] = low
-            copy = remote(
-                out_stage.at[d - 1], attn.at[side, there], out_send.at[d - 1], out_recv.at[d - 1],
-                (peer, tensor),
-            )
-            copy.start()
-            attn_parts.append(copy)
+            source, target = out_single.at[d - 1], attn_single.at[own]
+            source[...] = packed(low)
+        copy = remote(source, target, out_send.at[d - 1], out_recv.at[d - 1], (peer, tensor))
+        copy.start()
+        attn_parts.append(copy)
     for copy in whole_parts + attn_parts:
         copy.wait_recv()
     sent += whole_parts + attn_parts
 
     parts = []
     for i in (2, 1, 0):
-        copy = remote(
-            attn.at[:, block_rows(peers[i][1], tok)], heads_in.at[tensor], a2a_send.at[0, i],
-            a2a_recv.at[0, i], peers[i],
-        )
-        copy.start()
-        parts.append(copy)
-    heads_in[tensor] = attn[:, mine]
+        t = peers[i][1]
+        for j, (held, come) in enumerate(((attn_pair, pairs_in), (attn_single, singles_in))):
+            copy = remote(
+                held.at[t], come.at[tensor], a2a_send.at[0, i, j], a2a_recv.at[0, i, j], peers[i]
+            )
+            copy.start()
+            parts.append(copy)
+    pairs_in[tensor] = attn_pair[tensor]
+    singles_in[tensor] = attn_single[tensor]
     z, side_of_chip = me // 2, tensor % 2
     beside = (me + 1 - 2 * side, tensor)
     token_parts = []
@@ -915,82 +1057,116 @@
     for copy in parts:
         copy.wait_recv()
     sent += parts
-    branch = jnp.zeros((tok, width), f32)
-    for t in range(4):
-        branch = branch + dot(heads_in[t, 0], out_whole[t, :LANES])
-        branch = branch + dot(heads_in[t, 1], out_whole[t, LANES:])
-
     def line(vector):
         return vector[...].reshape(1, vector.shape[0])
 
-    first_total = x[mine].astype(f32) + (branch + line(out_bias))
-    normal_one, inverse_one = normal_of(first_total)
-    hidden_one = normal_one * line(gain_one) + line(shift_one)
-    hidden[mine] = hidden_one.astype(bf16)
-    ring = (ag_send, ag_recv, sum_send, sum_recv, core_out, core_in, y_out, y_in)
-
-    def up(t):
-        at = block_rows(t, tok)
-        value = dot(hidden[at], up_weight[...]) + line(up_bias)
+    piece = tok // 2
+    chunks = range(2)
+    ring = Ring(
+        tensor, peers, parts_held, core_out, core_in, y_out, y_in, ag_send, ag_recv, sum_send,
+        sum_recv,
+    )
+
+    def rows_of(c):
+        return pl.ds(pl.multiple_of(tensor * tok + c * piece, piece), piece)
+
+    def normed(c):
+        at = slice(c * piece, (c + 1) * piece)
+        lanes = slice(c * HEAD_DIM, (c + 1) * HEAD_DIM)
+        heads = jnp.concatenate(
+            [pairs_in[t, at] for t in range(4)] + [singles_in[t, :, lanes] for t in range(4)],
+            axis=1,
+        )
+        branch = dot(heads, out_whole[...])
+        first_total = x[rows_of(c)].astype(f32) + (branch + line(out_bias))
+        normal, inverse_std = normal_of(first_total)
+        whole_row = normal * line(gain_one) + line(shift_one)
+        hidden[c, tensor] = whole_row.astype(bf16)
+        ring.share(0, c, hidden)
+        return normal, inverse_std, whole_row
+
+    def up(c, t):
+        at = pl.ds(t, 2)
+        value = dot(hidden[c, at].reshape(tok, width), up_weight[...]) + line(up_bias)
         half_erf = 0.5 * (1.0 + lax.erf(value * (0.5**0.5)))
         density = jnp.exp(-0.5 * value * value) * (0.5 / jnp.pi) ** 0.5
-        slope[at] = half_erf + value * density
+        slope[c, at] = (half_erf + value * density).reshape(2, piece, hidden_width)
         low = (value * half_erf).astype(bf16)
-        active[at] = low
+        active[c, at] = low.reshape(2, piece, hidden_width)
         return dot(low, down_weight[...])
 
-    down_sum, copies = gather_and_sum(0, me, tensor, hidden, up, ring, pass_tokens)
-    sent += copies
-    second_total = hidden_one + (down_sum + line(down_bias))
-    normal_two, inverse_two = normal_of(second_total)
-    output[mine] = (normal_two * line(gain_two) + line(shift_two)).astype(bf16)
-    grad_output = out_grad[mine].astype(f32)
-    grad_second = before_norm(grad_output, normal_two, inverse_two, line(gain_two))
-    low = grad_second.astype(bf16)
-    down_in[mine] = low
-
-    def down(t):
-        at = block_rows(t, tok)
-        low = (dot(down_in[at], down_weight[...], NT) * slope[at]).astype(bf16)
-        up_in[at] = low
+    def down(c, t):
+        at = pl.ds(t, 2)
+        grad = dot(down_in[c, at].reshape(tok, width), down_weight[...], NT)
+        low = (grad * slope[c, at].reshape(tok, hidden_width)).astype(bf16)
+        up_in[c, at] = low.reshape(2, piece, hidden_width)
         return dot(low, up_weight[...], NT)
 
-    def fill():
-        source_down[...] = dot(down_in[...], active[...], TN).astype(bf16)
-        job_down.first()
-        source_up[...] = dot(hidden[...], up_in[...], TN).astype(bf16)
-        early[0:1] = total_of(grad_output * normal_two)
-        early[1:2] = total_of(grad_output)
-        early[2:3] = total_of(low.astype(f32))
-        early[6:7] = dot(jnp.ones((8, rows), bf16), up_in[...])[0:1]
-
-    for copy in token_parts[3:7]:
-        copy.wait_recv()
-    half_all = tokens_own.at[:, side_of_chip]
-    give_tokens(half_all, half_all, 7, core)
-    up_sum, copies = gather_and_sum(1, me, tensor, down_in, down, ring, fill)
-    sent += copies
-    grad_hidden = grad_second + up_sum
-    grad_first = before_norm(grad_hidden, normal_one, inverse_one, line(gain_one))
-    low_out = grad_first.astype(bf16)
-    out_in[mine] = low_out
+    after_norm_one = [normed(c) for c in chunks]
+    ring.run(0, hidden, up)
+    pass_tokens()
+
+    grads_second, sums_second = [], []
+    for c in chunks:
+        hidden_one = after_norm_one[c][2]
+        second_total = hidden_one + (ring.total(0, c) + line(down_bias))
+        normal, inverse_std = normal_of(second_total)
+        output[rows_of(c)] = (normal * line(gain_two) + line(shift_two)).astype(bf16)
+        grad_output = out_grad[rows_of(c)].astype(f32)
+        grad_second = before_norm(grad_output, normal, inverse_std, line(gain_two))
+        low = grad_second.astype(bf16)
+        down_in[c, tensor] = low
+        ring.share(1, c, down_in)
+        grads_second.append(grad_second)
+        sums_second.append(
+            (total_of(grad_output * normal), total_of(grad_output), total_of(low.astype(f32)))
+        )
+    ring.run(1, down_in, down)
+    everything = (rows, width)
+    every_hidden = (rows, hidden_width)
+    source_down[...] = dot(
+        down_in[...].reshape(everything), active[...].reshape(every_hidden), TN
+    ).astype(bf16)
+    for job in job_down:
+        job.first()
+
+    grads_first, sums_first = [], []
     parts = []
-    for i in (2, 1, 0):
-        t = peers[i][1]
-        heads_out[i, 0] = dot(low_out, out_whole[t, :LANES], NT).astype(bf16)
-        heads_out[i, 1] = turn(dot(low_out, out_whole[t, LANES:], NT), heads_out[i, 0])
-        copy = remote(
-            heads_out.at[i], grad_attn.at[:, mine], a2a_send.at[1, i], a2a_recv.at[1, i], peers[i]
-        )
-        copy.start()
-        parts.append(copy)
-    own_first = dot(low_out, out_whole[tensor, :LANES], NT).astype(bf16)
-    grad_attn[0, mine] = own_first
-    grad_attn[1, mine] = turn(dot(low_out, out_whole[tensor, LANES:], NT), own_first)
+    for c in chunks:
+        normal, inverse_std, _ = after_norm_one[c]
+        grad_hidden = grads_second[c] + ring.total(1, c)
+        grad_first = before_norm(grad_hidden, normal, inverse_std, line(gain_one))
+        low = grad_first.astype(bf16)
+        out_in[rows_of(c)] = low
+        heads = dot(low, out_whole[...], NT).astype(bf16)
+        at = slice(c * piece, (c + 1) * piece)
+        for t in range(4):
+            start = 4 * LANES + t * HEAD_DIM
+            pair = heads[:, t * LANES : (t + 1) * LANES]
+            heads_out[t, 0, at] = pair
+            heads_out[t, 1, at] = jnp.concatenate(
+                [heads[:, start : start + HEAD_DIM], pair[:, HEAD_DIM:]], axis=1
+            )
+        for i in (2, 1, 0):
+            copy = remote(
+                heads_out.at[peers[i][1], :, pl.ds(c * piece, piece)],
+                grad_attn.at[:, rows_of(c)], a2a_send.at[1, i, c], a2a_recv.at[1, i, c], peers[i],
+            )
+            copy.start()
+            parts.append(copy)
+        grads_first.append(grad_first)
+        sums_first.append(
+            (total_of(grad_hidden * normal), total_of(grad_hidden), total_of(low.astype(f32)))
+        )
+    grad_attn[:, mine] = heads_out[tensor]
     sent += parts
-    early[3:4] = total_of(grad_hidden * normal_one)
-    early[4:5] = total_of(grad_hidden)
-    early[5:6] = total_of(low_out.astype(f32))
+    source_up[...] = dot(
+        hidden[...].reshape(everything), up_in[...].reshape(every_hidden), TN
+    ).astype(bf16)
+    for i in range(3):
+        early[i : i + 1] = sums_second[0][i] + sums_second[1][i]
+        early[i + 3 : i + 4] = sums_first[0][i] + sums_first[1][i]
+    early[6:7] = dot(jnp.ones((8, rows), bf16), up_in[...].reshape(every_hidden))[0:1]
     early_tensor[tensor] = early[...]
     for copy in parts:
         copy.wait_recv()
@@ -1000,12 +1176,19 @@
     for d in range(1, n):
         peer = lax.rem(me + d, n)
         copy = remote(
-            grad_attn.at[peer % 2, block_rows(peer // 2, tok)], gs.at[here], grad_send.at[d - 1],
+            grad_attn.at[d % 2, block_rows(peer // 2, tok)], gs.at[here], grad_send.at[d - 1],
             grad_recv.at[d - 1], (peer, tensor),
         )
         copy.start()
         parts.append(copy)
-    gs[here] = grad_attn[side, block_rows(own, tok)]
+    gs[here] = grad_attn[0, block_rows(own, tok)]
+    smalls = []
+    for i, device in enumerate(peers):
+        copy = remote(
+            early, early_tensor.at[tensor], small_send.at[0, i], small_recv.at[0, i], device
+        )
+        copy.start()
+        smalls.append(copy)
     shares = []
     for i, held in enumerate((out_in, output)):
         for j, device in enumerate((across, core)):
@@ -1014,25 +1197,22 @@
             )
             copy.start()
             shares.append(copy)
-    smalls = []
-    for i, device in enumerate(peers):
-        copy = remote(
-            early, early_tensor.at[tensor], small_send.at[0, i], small_recv.at[0, i], device
-        )
-        copy.start()
-        smalls.append(copy)
-    job_up.first(range(2))
+    for job in job_down:
+        job.second()
+    for job in job_up:
+        job.first()
+    for copy in token_parts[3:7]:
+        copy.wait_recv()
+    half_all = tokens_own.at[:, side_of_chip]
+    give_tokens(half_all, half_all, 7, core)
 
     members = member_columns(length, total)
     outs = []
 
     def give(i, block):
         low = block.astype(bf16)
-        blocks = low.reshape(n, 2, tok // 2, LANES)
         back_stage[i] = low.reshape(n, tok, LANES)
-        back_single[i] = jnp.concatenate(
-            [blocks[:, 0, :, :HEAD_DIM], blocks[:, 1, :, :HEAD_DIM]], axis=2
-        )
+        back_single[i] = packed(low.reshape(n, tok, LANES))
         part = []
         for d in range(1, n):
             peer = lax.rem(me + d, n)
@@ -1047,11 +1227,9 @@
         outs.append(part)
         return low
 
-    job_down.second()
     for copy in parts:
         copy.wait_recv()
     sent += parts
-    job_up.first(range(2, 4))
     grad = gs[half : half + total]
     kernel_one = k1[...]
     grad_carried = jnp.where(same_head, fine(kernel_one, grad, TN), 0.0)
@@ -1065,6 +1243,11 @@
     value_in = give(2, jnp.where(iota(grad_values.shape, 0) < length, grad_values, 0.0))
 
 
+    job_down[0].third()
+    token_parts[7].wait_recv()
+    sent += token_parts
+    tokens_all = tokens_own[...].reshape(total, width)
+    source_v[...] = dot(tokens_all, value_in, TN).astype(bf16)
     kernel_back = jnp.zeros((LANES, LANES), f32)
     grad_state = grad_inverse
     for step in reversed(range(NS_ITERS)):
@@ -1096,6 +1279,7 @@
     delta = fine(jnp.ones((8, LANES), bf16), grad_third * third_out, NT)[0:1]
     third_scores = scale * third_prob * (fine(values, grad_third, NT) - delta)
     query_three = jnp.where(same_head, fine(third_scores, keys, TN), 0.0)
+    job_v.first()
     key_in = give(0, fine(third_scores, query_marks) + fine(members, (key_one + key_two) / counts))
     query_in = give(1, fine(first_scores, key_marks) + fine(members, (query_two + query_three) / counts))
 
@@ -1105,17 +1289,41 @@
         copy = remote(block, block, share_send.at[i, 2], share_recv.at[i, 2], core)
         copy.start()
         shares.append(copy)
+    source_kq[:, :LANES] = dot(tokens_all, key_in, TN).astype(bf16)
+    source_kq[:, LANES:] = dot(tokens_all, query_in, TN).astype(bf16)
+    job_kq.first()
     for copy in smalls:
         copy.wait_recv()
     by_tensor = early_tensor[0] + early_tensor[1] + early_tensor[2] + early_tensor[3]
-    early_seq[me] = jnp.where(iota(by_tensor.shape, 0) == 6, early[...], by_tensor)
+    early_out[0] = jnp.where(iota(by_tensor.shape, 0) == 6, early[...], by_tensor)
     smalls_early = []
-    for d, device in enumerate(ring_peers):
-        copy = remote(
-            early_seq.at[me], early_seq.at[me], small_send.at[1, d], small_recv.at[1, d], device
-        )
-        copy.start()
-        smalls_early.append(copy)
+
+    def early_next(k):
+        if k > 0:
+            smalls_early[k - 1].wait_recv()
+            early_out[k] = early_out[k - 1] + early_in[k - 1]
+        if k < 3:
+            copy = remote(
+                early_out.at[k], early_in.at[k], small_send.at[1, k], small_recv.at[1, k],
+                job_out.partners[k],
+            )
+            copy.start()
+            smalls_early.append(copy)
+
+    early_next(0)
+    shares[1].wait_recv()
+    shares[4].wait_recv()
+    pair, single = attn_pair[...].reshape(rows, LANES), unpacked(attn_single[...])
+    single = single.reshape(rows, HEAD_DIM)
+    attention = jnp.concatenate(
+        [
+            jnp.where(even, pair, jnp.concatenate([single, pair[:, HEAD_DIM:]], axis=1)),
+            jnp.where(even, single, pair[:, :HEAD_DIM]),
+        ],
+        axis=1,
+    )
+    source_out[...] = dot(out_in[...], attention, TN).astype(bf16)
+    job_out.first()
     position = iota((tok, tok), 0) + iota((tok, tok), 1)
     upside = jnp.where(position == tok - 1, 1.0, 0.0).astype(bf16)
     lane = iota((tok, LANES), 1)
@@ -1131,19 +1339,6 @@
         row = jnp.sum(table, axis=0, keepdims=True)
         row = pltpu.roll(jnp.broadcast_to(row, (8, 2 * tok)), tok + 1, 1)
         conv_rows.append(row[0:1, :LANES])
-    shares[1].wait_recv()
-    shares[4].wait_recv()
-    attention = jnp.concatenate([attn[0], attn[1, :, :HEAD_DIM]], axis=1)
-    source_out[...] = dot(out_in[...], attention, TN).astype(bf16)
-    job_out.first()
-    token_parts[7].wait_recv()
-    sent += token_parts
-    tokens_all = tokens_own[...].reshape(total, width)
-    source_v[...] = dot(tokens_all, value_in, TN).astype(bf16)
-    source_kq[:, :LANES] = dot(tokens_all, key_in, TN).astype(bf16)
-    source_kq[:, LANES:] = dot(tokens_all, query_in, TN).astype(bf16)
-    job_v.first()
-    job_kq.first()
     late = late_seq.at[me]
     late[...] = jnp.zeros(late.shape, f32)
     column = jnp.ones((8, total), bf16)
@@ -1159,27 +1354,25 @@
         copy = remote(late, late, small_send.at[2, d], small_recv.at[2, d], device)
         copy.start()
         smalls_late.append(copy)
-    job_up.second()
-    job_down.third()
-
+    job_down[1].third()
+    job_down[0].fourth()
+    job_up[0].second()
     for part in outs:
         for copy in part:
             copy.wait_recv()
     singles = []
     for i in range(3):
         tokens_low[:, i * LANES : (i + 1) * LANES] = come_pair[i].reshape(rows, LANES)
-        packed = come_single[i]
-        single = jnp.concatenate([packed[:, :, :HEAD_DIM], packed[:, :, HEAD_DIM:]], axis=1)
-        singles.append(single.reshape(rows, HEAD_DIM))
+        singles.append(unpacked(come_single[i]).reshape(rows, HEAD_DIM))
     tokens_low[:, 3 * LANES :] = jnp.concatenate(singles, axis=1)
 
     def input_part(t):
         return dot(tokens_low[block_rows(t, tok)], weight_in[...])
 
     def pass_sum(k, value, device):
-        core_out[2, k] = value.astype(bf16)
+        core_last[0, k] = value.astype(bf16)
         copy = remote(
-            core_out.at[2, k], core_in.at[2, k], sum_send.at[2, k], sum_recv.at[2, k], device
+            core_last.at[0, k], core_last.at[1, k], last_send.at[k], last_recv.at[k], device
         )
         copy.start()
         sent.append(copy)
@@ -1187,18 +1380,19 @@
 
     middle = pass_sum(1, input_part(far[1]), core)
     near = pass_sum(0, input_part(core[1]), core)
-    part = input_part(across[1])
+    crossing = input_part(across[1])
     middle.wait_recv()
-    y_out[2] = (part + core_in[2, 1].astype(f32)).astype(bf16)
-    final = remote(y_out.at[2], y_in.at[2], sum_send.at[2, 2], sum_recv.at[2, 2], across)
+    y_last[0] = (crossing + core_last[1, 1].astype(f32)).astype(bf16)
+    final = remote(y_last.at[0], y_last.at[1], last_send.at[2], last_recv.at[2], across)
     final.start()
     sent.append(final)
-    result = input_part(tensor) + grad_first
-    job_out.second()
+    result = input_part(tensor) + jnp.concatenate(grads_first, axis=0)
     job_v.second()
+    job_up[1].second()
+    job_up[0].third()
     near.wait_recv()
     final.wait_recv()
-    result = result + core_in[2, 0].astype(f32) + y_in[2].astype(f32)
+    result = result + core_last[1, 0].astype(f32) + y_last[1].astype(f32)
     tokens_whole[mine] = result.astype(bf16)
     ends = []
     for j, device in enumerate((across, core)):
@@ -1208,15 +1402,39 @@
         )
         copy.start()
         ends.append(copy)
-    job_up.third()
+    early_next(1)
     job_kq.second()
+    job_out.second()
+    job_up[0].fourth()
+    job_up[1].third()
+    early_next(2)
+    job_v.third()
+
+    def into(ref, k):
+        def write(value):
+            ref[:, k * span : (k + 1) * span] = value
+
+        return write
+
+    for k, job in enumerate(job_down):
+        job.last(into(grad_down, k))
+    done(14)
+    ends[0].wait_recv()
+    block = tokens_whole.at[block_rows(across[1], tok)]
+    copy = remote(block, block, share_send.at[2, 2], share_recv.at[2, 2], core)
+    copy.start()
+    ends.append(copy)
+    job_kq.third()
+    job_up[1].fourth()
     job_out.third()
-    job_v.third()
-    grad_down[...] = job_down.last()
-    done(14)
-    for copy in smalls_early + smalls_late:
+    ends[1].wait_recv()
+    ends[2].wait_recv()
+    grad_tokens[...] = tokens_whole[...].astype(f32)
+    done(1)
+    for copy in smalls_late:
         copy.wait_recv()
-    by_seq = functools.reduce(lambda a, b: a + b, [early_seq[i] for i in range(n)])
+    early_next(3)
+    by_seq = early_out[3]
     for ref, row in (
         (second_gain, 0), (second_shift, 1), (down_bias_grad, 2), (first_gain, 3),
         (first_shift, 4), (out_bias_grad, 5), (up_bias_grad, 6),
@@ -1230,33 +1448,30 @@
     shares[3].wait_recv()
     shares[5].wait_recv()
     done(0, 3, 6, 7, 9, 10, 11, 13, 15, 16, 17, 18)
-    ends[0].wait_recv()
-    block = tokens_whole.at[block_rows(across[1], tok)]
-    copy = remote(block, block, share_send.at[2, 2], share_recv.at[2, 2], core)
-    copy.start()
-    ends.append(copy)
-    job_kq.third()
-    grad_up[...] = job_up.last()
-    done(12)
-    grad_out[...] = job_out.last().T
-    done(8)
 
     def heads(job, *refs):
-        kept, come = job.swapped()
-        pair, single = jnp.where(even, kept, come), jnp.where(even, come, kept)
-        for i, ref in enumerate(refs):
-            ref[:, :LANES] = pair[:, i * LANES : (i + 1) * LANES].astype(f32)
-            ref[:, LANES:] = single[:, i * LANES : i * LANES + HEAD_DIM].astype(f32)
+        def write(result):
+            for i, ref in enumerate(refs):
+                start = len(refs) * LANES + i * HEAD_DIM
+                ref[:, :LANES] = result[:, i * LANES : (i + 1) * LANES]
+                ref[:, LANES:] = result[:, start : start + HEAD_DIM]
+
+        job.last(write)
 
     heads(job_v, grad_value)
     done(5)
-    ends[1].wait_recv()
-    ends[2].wait_recv()
-    grad_tokens[...] = tokens_whole[...].astype(f32)
-    done(1)
+    for k, job in enumerate(job_up):
+        job.last(into(grad_up, k))
+    done(12)
     heads(job_kq, grad_key, grad_query)
     done(2, 4)
-    for copy in sent + shares + smalls + smalls_early + smalls_late + ends:
+
+    def write_out(value):
+        grad_out[...] = value.T
+
+    job_out.last(write_out)
+    done(8)
+    for copy in list(ring.copies.values()) + sent + shares + smalls + smalls_early + smalls_late + ends:
         copy.wait_send()
     for part in outs:
         for copy in part:
@@ -1309,6 +1524,7 @@
     hidden = up_weight.shape[1]
     total = n * tok
     block = width // n
+    piece = tok // 2
 
     def low(*shape):
         return pltpu.VMEM(shape, bf16)
@@ -1346,30 +1562,37 @@
         scratch_shapes=[pltpu.VMEM(r.shape, r.dtype) for r in results]
         + [
             low(rows, width), low(local, width), low(local, width), low(local, width),
-            low(width, hidden), low(hidden, width), low(rows, width), low(4, 2 * LANES, width),
+            low(width, hidden), low(hidden, width), low(rows, width), low(local, width),
+            low(width, width),
             low(3, 2, rows, LANES), low(total, LANES), low(total, LANES), low(total + tok, LANES),
             wide(total, LANES), wide(total, LANES), wide(4 * NS_ITERS, LANES, LANES),
-            low(n - 1, tok, LANES), low(2, rows, LANES),
-            low(4, 2, tok, LANES), low(3, 2, tok, LANES), low(2, rows, LANES), low(rows, width),
-            wide(rows, hidden), low(rows, hidden), low(rows, width), low(rows, hidden),
-            low(3, 2, tok, width), low(3, 2, tok, width), low(3, tok, width), low(3, tok, width),
+            low(n - 1, tok, LANES), low(n - 1, piece, LANES), low(batch, tok, LANES),
+            low(batch, piece, LANES),
+            low(4, tok, LANES), low(4, piece, LANES), low(4, 2, tok, LANES),
+            low(2, rows, LANES), low(2, 4, piece, width), wide(2, 4, piece, hidden),
+            low(2, 4, piece, hidden), low(2, 4, piece, width), low(2, 4, piece, hidden),
+            low(2, 2, 2, piece, width), low(2, 2, 2, piece, width), low(2, 2, piece, width),
+            low(2, 2, piece, width), low(2, 2, tok, width), low(2, tok, width),
             low(total + tok, LANES), low(3, n, tok, LANES), low(3, n, tok // 2, LANES),
             low(3, batch, tok, LANES), low(3, batch, tok // 2, LANES), low(3 * local, width),
             low(rows, width), wide(8, width), wide(4, 8, width), low(n, 2, tok // 2, width),
             low(rows, 3 * local), low(width, hidden), low(width, hidden), low(width, local),
-            low(width, LANES), low(width, 2 * LANES), wide(n, 8, width), wide(n, 8, width),
-            low(rows, width),
+            low(width, LANES), low(width, 2 * LANES), wide(4, 8, width), wide(3, 8, width),
+            wide(n, 8, 2 * LANES), low(rows, width), wide(2, 2, 2, 2, piece, width),
         ]
         + [
             b
-            for w in (hidden, hidden, local, LANES, 2 * LANES)
-            for b in scatter_buffers(w, block)
+            for first, w in (
+                *((hidden // 2, hidden // 2),) * 4, (local, local), (LANES, local), (2 * LANES, 2 * local)
+            )
+            for b in scatter_buffers(first, w, block)
         ]
         + [
-            dma(8), dma(3, n - 1), dma(3, n - 1), dma(n - 1), dma(n - 1), dma(3), dma(3),
-            dma(2, 3), dma(2, 3), dma(2, 3), dma(2, 3), dma(3, 3), dma(3, 3), dma(n - 1),
+            dma(8), dma(3, n - 1), dma(3, n - 1), dma(n - 1), dma(n - 1), dma(3, 2),
+            dma(3, 2), dma(2, 3, 2), dma(2, 3, 2), dma(2, 2, 3), dma(2, 2, 3), dma(2, 2, 3),
+            dma(2, 2, 3), dma(n - 1),
             dma(n - 1), dma(3, n - 1), dma(3, n - 1), dma(3, 3), dma(3, 3), dma(3, n - 1),
-            dma(3, n - 1), dma(JOBS, 7), dma(JOBS, 7), dma(8), dma(8), dma(RESULTS),
+            dma(3, n - 1), dma(JOBS, 10), dma(JOBS, 10), dma(8), dma(8), dma(3), dma(3), dma(RESULTS),
         ],
         compiler_params=pltpu.CompilerParams(
             collective_id=0, has_side_effects=True, vmem_limit_bytes=56 * 2**20

time: 152 us -> 134 us (0.88)
  the two profiles are of different devices: /device:TPU:10 before, /device:TPU:0 now
where the time goes in v4:
time: 134 us
  Pallas kernels  133 us (99%)
    pallas_call x1, Pallas kernels, gathered_plan(): pl.pallas_call(functools.partial(layer_kernel, n), out_shape=results, in_...  129 us
    pallas_call x1, Pallas kernels, gathered_plan(): pl.pallas_call(finish_kernel, out_shape=results, in_specs=[HBM] * RESULTS...  4.06 us

profile of v4, /device:TPU:0, one launch (start us, length us, event | category | flops | bytes accessed | tf_op | source)
XLA Modules:
  0.0 134.0 jit_solution(9207405781373513948)
XLA Ops:
  0.7 129.1 %layer.1 = (bf16[512,768]{1,0:T(8,128)(2,1)}, f32[512,768]{1,0:T(8,128)}, f32[96,192]{1,0:T(8,128)}, f32[192]{0:T(256)}, f32[96,192]{1,0:T(8,128)}, /*index=5*/f...) custom-call(s32[4]{0:T(128)} %lengths.1, ...), custom_call_target="tpu_custom_call" | custom-call | tf_op jit(solution)/shard_map/layer/pallas_call | solution.py:1556
  129.8 4.1 %finish.1 = (bf16[512,768]{1,0:T(8,128)(2,1)}, f32[512,768]{1,0:T(8,128)}, f32[96,192]{1,0:T(8,128)}, f32[192]{0:T(256)}, f32[96,192]{1,0:T(8,128)}, /*index=5*/...) custom-call(bf16[512,768]{1,0:T(8,128)(2,1)} %get-tuple-element.57.r, ...), custom_call_target="tpu_custom_call" | custom-call | tf_op jit(solution)/shard_map/finish/pallas_call | solution.py:1607

commit v5 on v4

--- a/solution.py
+++ b/solution.py
@@ -520,6 +520,10 @@
     return pl.ds(pl.multiple_of(t * tok, tok), tok)
 
 
+def settle(ref, sem):
+    pltpu.make_async_copy(ref, ref, sem).wait()
+
+
 class Scatter:
     def __init__(self, index, me, tensor, source, columns, buffers, send, recv, order):
         self.index, self.source, self.columns = index, source, pl.ds(*columns)
@@ -531,51 +535,50 @@
             (me + weight * (1 - 2 * bit), tensor) for weight, bit in zip(self.weights, self.bits)
         ]
         self.send, self.recv = send, recv
-        self.copies = []
 
     def rows(self, slot, bit):
         index = (slot // 2) * self.weights[2] + (slot % 2) * self.weights[1] + bit * self.weights[0]
         return pl.ds(pl.multiple_of(index * self.block, 16), self.block)
 
     def copy(self, src, dst, k, stage):
-        copy = remote(
-            src, dst, self.send.at[self.index, k], self.recv.at[self.index, k],
+        return remote(
+            src, dst, self.send.at[self.index, min(k, 1)], self.recv.at[self.index, k],
             self.partners[stage],
         )
-        copy.start()
-        self.copies.append(copy)
+
+    def arrived(self, ref, k):
+        settle(ref, self.recv.at[self.index, k])
 
     def first(self, slots=range(4)):
         for slot in slots:
-            self.copy(self.source.at[self.rows(slot, 1 - self.bits[0]), self.columns], self.first_in.at[slot], slot, 0)
+            source = self.source.at[self.rows(slot, 1 - self.bits[0]), self.columns]
+            self.copy(source, self.first_in.at[slot], 0, 0).start()
 
     def second(self):
-        for slot in range(4):
-            self.copies[slot].wait_recv()
+        self.arrived(self.first_in, 0)
         for slot in range(4):
             mine = self.source[self.rows(slot, self.bits[0]), self.columns]
             self.held[slot] = self.joined(mine, self.first_in[slot])
         for k in range(2):
-            self.copy(self.held.at[2 * k + 1 - self.bits[1]], self.second_in.at[k], 4 + k, 1)
+            self.copy(self.held.at[2 * k + 1 - self.bits[1]], self.second_in.at[k], 1, 1).start()
 
     def joined(self, mine, come):
         return (mine.astype(f32) + come.astype(f32)).astype(bf16)
 
     def third(self):
-        for k in range(2):
-            self.copies[4 + k].wait_recv()
+        self.arrived(self.second_in, 1)
         for k in range(2):
             both = self.held[2 * k + self.bits[1]].astype(f32) + self.second_in[k].astype(f32)
             self.pair[k] = both.astype(bf16)
-        self.copy(self.pair.at[1 - self.bits[2]], self.last_in, 6, 2)
+        self.copy(self.pair.at[1 - self.bits[2]], self.last_in, 2, 2).start()
 
     def last(self, write):
-        self.copies[6].wait_recv()
+        self.arrived(self.last_in, 2)
         write(self.pair[self.bits[2]].astype(f32) + self.last_in[...].astype(f32))
 
     def finish(self):
-        for copy in self.copies:
-            copy.wait_send()
+        settle(self.first_in, self.send.at[self.index, 0])
+        settle(self.held.at[pl.ds(0, 3)], self.send.at[self.index, 1])
 
 
 class Line(Scatter):
@@ -587,25 +590,16 @@
         self.inner = self.bits[1] != right
         self.slots = [k * (1 - right) + (3 - k) * right for k in range(4)]
         self.partners[2] = (2 * (3 - z) + self.bits[0], self.partners[0][1])
-        self.own = {}
-
-    def step(self, src, dst, k, stage):
-        copy = remote(
-            src, dst, self.send.at[self.index, k], self.recv.at[self.index, k],
-            self.partners[stage],
-        )
-        self.own[k] = copy
-        return copy
 
     def second(self):
-        for slot in range(4):
-            self.copies[slot].wait_recv()
+        self.arrived(self.first_in, 0)
         for slot in range(4):
             mine = self.source[self.rows(slot, self.bits[0]), self.columns]
             self.held[slot] = self.joined(mine, self.first_in[slot])
         come = (self.second_in.at[0], self.second_in.at[1], self.last_in)
         sends = [
-            self.step(self.held.at[self.slots[3 - k]], come[k], 4 + k, 1) for k in range(3)
+            self.copy(self.held.at[self.slots[3 - k]], come[k], (1, 1, 2)[k], 1)
+            for k in range(3)
         ]
 
         @pl.when(self.end)
@@ -615,30 +609,29 @@
 
     def third(self):
         sends = [
-            self.step(self.pair.at[k], self.cross_in.at[k], 7 + k, 2) for k in range(2)
+            self.copy(self.pair.at[k], self.cross_in.at[k], 3, 2) for k in range(2)
         ]
 
         @pl.when(self.inner)
         def _():
+            self.arrived(self.second_in, 1)
             for k in range(2):
-                self.own[4 + k].wait_recv()
                 self.pair[k] = self.joined(self.held[self.slots[3 - k]], self.second_in[k])
                 sends[k].start()
 
     def fourth(self):
-        back = self.step(self.first_in.at[2], self.first_in.at[3], 9, 1)
+        back = self.copy(self.first_in.at[2], self.first_in.at[3], 4, 1)
 
         @pl.when(self.inner)
         def _():
-            self.own[7].wait_recv()
+            self.arrived(self.cross_in, 3)
             self.first_in[2] = self.joined(self.held[self.slots[0]], self.cross_in[0])
             back.start()
 
     def last(self, write):
         @pl.when(self.inner)
         def _():
-            self.own[6].wait_recv()
-            self.own[8].wait_recv()
+            self.arrived(self.last_in, 2)
             write(
                 self.held[self.slots[1]].astype(f32)
                 + self.last_in[...].astype(f32)
@@ -647,21 +640,8 @@
 
         @pl.when(self.end)
         def _():
-            self.own[9].wait_recv()
+            self.arrived(self.first_in.at[3], 4)
             write(self.held[self.slots[0]].astype(f32) + self.first_in[3].astype(f32))
-
-    def finish(self):
-        super().finish()
-
-        @pl.when(self.end)
-        def _():
-            for k in range(4, 7):
-                self.own[k].wait_send()
-
-        @pl.when(self.inner)
-        def _():
-            for k in range(7, 10):
-                self.own[k].wait_send()
 
 
 class Heads(Scatter):
@@ -671,6 +651,19 @@
         return jnp.concatenate(
             [pair] + [other[:, k : k + HEAD_DIM] for k in range(0, other.shape[1], LANES)], axis=1
         )
+
+
+class Pairs(Scatter):
+    def second(self):
+        self.arrived(self.first_in, 0)
+        width = self.first_in.shape[2]
+        for slot in range(4):
+            at = self.rows(slot, self.bits[0])
+            self.held[slot, :, :width] = self.source[at]
+            self.held[slot, :, width : 2 * width] = self.shared[at]
+            self.held[slot, :, 2 * width :] = self.first_in[slot]
+        for k in range(2):
+            self.copy(self.held.at[2 * k + 1 - self.bits[1]], self.second_in.at[k], 1, 1).start()
 
 
 def scatter_buffers(first, width, block):
@@ -713,7 +706,7 @@
         self.copies = {}
 
     def send(self, name, src, dst, sems, at, device):
-        copy = remote(src, dst, sems[0].at[at], sems[1].at[at], device)
+        copy = remote(src, dst, sems[0].at[0], sems[1].at[at], device)
         copy.start()
         self.copies[name] = copy
 
@@ -789,7 +782,7 @@
     pairs_in, singles_in, heads_out, grad_attn, hidden, slope, active, down_in, up_in,
     core_out, core_in, y_out, y_in, core_last, y_last,
     gs, back_stage, back_single, come_pair, come_single, weight_in, out_in, early, early_tensor, tokens_own, tokens_low, source_up,
-    source_down, source_out, source_v, source_kq, early_out, early_in, late_seq, tokens_whole,
+    source_down, source_out, source_v, source_kq, shared_kq, early_out, early_in, late_out, late_in, tokens_whole,
     parts_held,
     *rest,
 ):
@@ -844,12 +837,12 @@
             (Line, source_up, (span, span), (0, 1, 2)),
             (Scatter, source_out, (0, local), (0, 1, 2)),
             (Heads, source_v, (0, LANES), (0, 1, 2)),
-            (Heads, source_kq, (0, 2 * LANES), (0, 1, 2)),
+            (Pairs, source_kq, (0, LANES), (0, 1, 2)),
         ))
     ]
     job_down, job_up = jobs[0:2], jobs[2:4]
     job_out, job_v, job_kq = jobs[4:]
-    sent = []
+    job_kq.shared = shared_kq
 
     owned = (ks, qs, vs)
     offsets = (0, 0, half)
@@ -858,7 +851,7 @@
         padded[half + total : total + tok] = jnp.zeros((tok - half, LANES), bf16)
     even = side == 0
 
-    arrivals = [[], [], []]
+    seven = pl.ds(0, (n - 1) * tok)
 
     def spread(i):
         here = pl.ds(pl.multiple_of(offsets[i] + me * tok, 16), tok)
@@ -866,12 +859,9 @@
             peer = lax.rem(me + d, n)
             copy = remote(
                 stage.at[i, peer % 2, block_rows(peer // 2, tok)], owned[i].at[here],
-                send.at[i, d - 1], recv.at[i, d - 1], (peer, tensor),
+                send.at[i], recv.at[i], (peer, tensor),
             )
             copy.start()
-            arrivals[i].append(copy)
-            if i != 1:
-                sent.append(copy)
         owned[i][here] = stage[i, side, block_rows(own, tok)]
 
     loads[0].wait()
@@ -896,7 +886,6 @@
     )
     stage[2, 0], stage[2, 1] = paired(y.astype(bf16))
     loads[4].wait()
-    whole_parts = []
     pair_rows = block_rows(tensor, LANES)
     single_rows = pl.ds(pl.multiple_of(4 * LANES + tensor * HEAD_DIM, HEAD_DIM), HEAD_DIM)
     first, single = out_weight[:LANES], out_weight[LANES:]
@@ -905,11 +894,9 @@
     )
     out_whole[single_rows] = jnp.where(even, single, first[:HEAD_DIM])
     for i, device in enumerate(peers):
-        for j, at in enumerate((pair_rows, single_rows)):
+        for at in (pair_rows, single_rows):
             part = out_whole.at[at]
-            copy = remote(part, part, whole_send.at[i, j], whole_recv.at[i, j], device)
-            copy.start()
-            whole_parts.append(copy)
+            remote(part, part, whole_send.at[0], whole_recv.at[0], device).start()
 
     length = lengths[own]
     same_head = block_mask()
@@ -934,15 +921,12 @@
         )
         start = 3 * LANES + i * HEAD_DIM
         weight_in[start : start + HEAD_DIM] = jnp.where(even, single, pair[:HEAD_DIM])
-    for copy in arrivals[0]:
-        copy.wait_recv()
+    settle(ks.at[seven], recv.at[0])
     keys = ks[...]
     key_marks = jnp.where(same_head, dot(members, keys) / counts, 0.0)
-    for copy in arrivals[1]:
-        copy.wait_send()
+    settle(qs.at[seven], send.at[1])
     spread(2)
-    for copy in arrivals[1]:
-        copy.wait_recv()
+    settle(qs.at[seven], recv.at[1])
     queries = qs[...]
     query_marks = jnp.where(same_head, dot(members, queries) / counts, 0.0)
     scores = jnp.where(same_head, fine(query_marks, key_marks, NT) * scale, negative)
@@ -951,17 +935,19 @@
     inverse = jnp.where(
         same_head, kernel_two.T / block_sums(kernel_two * kernel_two, same_head), 0.0
     )
+    product = fine(kernel_two, inverse)
     for step in range(NS_ITERS):
-        product = fine(kernel_two, inverse)
-        inner_one = fine(product, 7.0 * identity - product)
-        inner_two = fine(product, 15.0 * identity - inner_one)
-        newton[4 * step] = inverse
-        newton[4 * step + 1] = product
-        newton[4 * step + 2] = inner_one
-        newton[4 * step + 3] = inner_two
-        inverse = 0.25 * fine(inverse, 13.0 * identity - inner_two)
-
-    deviation = identity - fine(kernel_two, inverse)
+        inner = fine(product, 7.0 * identity - product)
+        outer = 13.0 * identity - fine(product, 15.0 * identity - inner)
+        newton[5 * step] = inverse
+        newton[5 * step + 1] = product
+        newton[5 * step + 2] = inner
+        newton[5 * step + 3] = outer
+        newton[5 * step + 4] = fine(product, kernel_two)
+        inverse = 0.25 * fine(inverse, outer)
+        product = 0.25 * fine(product, outer)
+
+    deviation = identity - product
     norms = jnp.sqrt(block_sums(deviation * deviation, same_head))
     first, second = norms[0:1, 0:1], norms[LANES - 1 :, LANES - 1 :]
     norm_sum = jnp.where(side == 0, first + second, first) / (batch * HEADS)
@@ -982,13 +968,11 @@
     third_prob = weights / jnp.sum(weights, axis=0, keepdims=True)
     p3[...] = third_prob
 
-    for copy in arrivals[2]:
-        copy.wait_recv()
+    settle(vs.at[seven], recv.at[2])
     values = vs[half : half + total]
     third_out = jnp.where(same_head, fine(third_prob, values, TN), 0.0)
     carried = fine(inverse, third_out)
 
-    attn_parts = []
     for d in range(1, n + 1):
         peer = lax.rem(me + d, n)
         start = pl.multiple_of(peer * tok, tok)
@@ -1004,32 +988,24 @@
         else:
             source, target = out_single.at[d - 1], attn_single.at[own]
             source[...] = packed(low)
-        copy = remote(source, target, out_send.at[d - 1], out_recv.at[d - 1], (peer, tensor))
-        copy.start()
-        attn_parts.append(copy)
-    for copy in whole_parts + attn_parts:
-        copy.wait_recv()
-    sent += whole_parts + attn_parts
-
-    parts = []
+        remote(source, target, out_send.at[d % 2], out_recv.at[d % 2], (peer, tensor)).start()
+    three = pl.ds(0, 3)
+    settle(attn_pair.at[three], out_recv.at[0])
+    settle(attn_single, out_recv.at[1])
+    settle(out_whole.at[pl.ds(0, 3 * local)], whole_recv.at[0])
+
     for i in (2, 1, 0):
         t = peers[i][1]
         for j, (held, come) in enumerate(((attn_pair, pairs_in), (attn_single, singles_in))):
-            copy = remote(
-                held.at[t], come.at[tensor], a2a_send.at[0, i, j], a2a_recv.at[0, i, j], peers[i]
-            )
-            copy.start()
-            parts.append(copy)
+            remote(
+                held.at[t], come.at[tensor], a2a_send.at[j], a2a_recv.at[j], peers[i]
+            ).start()
     pairs_in[tensor] = attn_pair[tensor]
     singles_in[tensor] = attn_single[tensor]
     z, side_of_chip = me // 2, tensor % 2
     beside = (me + 1 - 2 * side, tensor)
-    token_parts = []
-
     def give_tokens(src, dst, i, device):
-        copy = remote(src, dst, own_send.at[i], own_recv.at[i], device)
-        copy.start()
-        token_parts.append(copy)
+        remote(src, dst, own_send.at[i // 2], own_recv.at[i], device).start()
 
     def half_block(b):
         start = pl.multiple_of(b * tok + side_of_chip * (tok // 2), tok // 2)
@@ -1039,24 +1015,21 @@
     for k in range(1, 4):
         peer = lax.rem(z + k, 4)
         give_tokens(
-            x.at[half_block(peer)], tokens_own.at[me, side_of_chip], k - 1,
-            (2 * peer + side, tensor),
+            x.at[half_block(peer)], tokens_own.at[me, side_of_chip], 0, (2 * peer + side, tensor)
         )
     half_own = tokens_own.at[me, side_of_chip]
-    give_tokens(half_own, half_own, 3, beside)
+    give_tokens(half_own, half_own, 1, beside)
 
     def pass_tokens():
-        for k in range(1, 4):
-            token_parts[k - 1].wait_recv()
+        settle(tokens_own.at[pl.ds(0, 3), 0], own_recv.at[0])
         for k in range(1, 4):
             come = tokens_own.at[2 * lax.rem(z + 4 - k, 4) + side, side_of_chip]
-            give_tokens(come, come, 3 + k, beside)
+            give_tokens(come, come, 1, beside)
 
     for copy in loads[5:]:
         copy.wait()
-    for copy in parts:
-        copy.wait_recv()
-    sent += parts
+    settle(pairs_in.at[three], a2a_recv.at[0])
+    settle(singles_in.at[three], a2a_recv.at[1])
     def line(vector):
         return vector[...].reshape(1, vector.shape[0])
 
@@ -1131,7 +1104,6 @@
         job.first()
 
     grads_first, sums_first = [], []
-    parts = []
     for c in chunks:
         normal, inverse_std, _ = after_norm_one[c]
         grad_hidden = grads_second[c] + ring.total(1, c)
@@ -1148,18 +1120,15 @@
                 [heads[:, start : start + HEAD_DIM], pair[:, HEAD_DIM:]], axis=1
             )
         for i in (2, 1, 0):
-            copy = remote(
+            remote(
                 heads_out.at[peers[i][1], :, pl.ds(c * piece, piece)],
-                grad_attn.at[:, rows_of(c)], a2a_send.at[1, i, c], a2a_recv.at[1, i, c], peers[i],
-            )
-            copy.start()
-            parts.append(copy)
+                grad_attn.at[:, rows_of(c)], a2a_send.at[2], a2a_recv.at[2], peers[i],
+            ).start()
         grads_first.append(grad_first)
         sums_first.append(
             (total_of(grad_hidden * normal), total_of(grad_hidden), total_of(low.astype(f32)))
         )
     grad_attn[:, mine] = heads_out[tensor]
-    sent += parts
     source_up[...] = dot(
         hidden[...].reshape(everything), up_in[...].reshape(every_hidden), TN
     ).astype(bf16)
@@ -1168,68 +1137,54 @@
         early[i + 3 : i + 4] = sums_first[0][i] + sums_first[1][i]
     early[6:7] = dot(jnp.ones((8, rows), bf16), up_in[...].reshape(every_hidden))[0:1]
     early_tensor[tensor] = early[...]
-    for copy in parts:
-        copy.wait_recv()
+    job_up[0].first(range(2))
+    three_blocks = grad_attn.at[:, pl.ds(0, 3 * tok)]
+    settle(three_blocks, a2a_recv.at[2])
 
     here = pl.ds(pl.multiple_of(half + me * tok, 16), tok)
-    parts = []
     for d in range(1, n):
         peer = lax.rem(me + d, n)
-        copy = remote(
-            grad_attn.at[d % 2, block_rows(peer // 2, tok)], gs.at[here], grad_send.at[d - 1],
-            grad_recv.at[d - 1], (peer, tensor),
-        )
-        copy.start()
-        parts.append(copy)
+        remote(
+            grad_attn.at[d % 2, block_rows(peer // 2, tok)], gs.at[here], grad_send.at[0],
+            grad_recv.at[0], (peer, tensor),
+        ).start()
     gs[here] = grad_attn[0, block_rows(own, tok)]
-    smalls = []
     for i, device in enumerate(peers):
-        copy = remote(
-            early, early_tensor.at[tensor], small_send.at[0, i], small_recv.at[0, i], device
-        )
-        copy.start()
-        smalls.append(copy)
+        remote(
+            early, early_tensor.at[tensor], small_send.at[0], small_recv.at[0], device
+        ).start()
     shares = []
     for i, held in enumerate((out_in, output)):
         for j, device in enumerate((across, core)):
             copy = remote(
-                held.at[mine], held.at[mine], share_send.at[i, j], share_recv.at[i, j], device
+                held.at[mine], held.at[mine], share_send.at[i], share_recv.at[i, j], device
             )
             copy.start()
             shares.append(copy)
-    for job in job_down:
-        job.second()
-    for job in job_up:
-        job.first()
-    for copy in token_parts[3:7]:
-        copy.wait_recv()
+    job_down[0].second()
+    job_up[0].first(range(2, 4))
+    job_down[1].second()
+    job_up[1].first()
+    settle(tokens_own.at[pl.ds(0, 4), 0], own_recv.at[1])
     half_all = tokens_own.at[:, side_of_chip]
-    give_tokens(half_all, half_all, 7, core)
+    give_tokens(half_all, half_all, 2, core)
 
     members = member_columns(length, total)
-    outs = []
-
     def give(i, block):
         low = block.astype(bf16)
         back_stage[i] = low.reshape(n, tok, LANES)
         back_single[i] = packed(low.reshape(n, tok, LANES))
-        part = []
         for d in range(1, n):
             peer = lax.rem(me + d, n)
             source, target = (back_stage, come_pair) if d % 2 == 0 else (back_single, come_single)
-            copy = remote(
-                source.at[i, peer], target.at[i, own], back_send.at[i, d - 1],
-                back_recv.at[i, d - 1], (peer, tensor),
-            )
-            copy.start()
-            part.append(copy)
+            remote(
+                source.at[i, peer], target.at[i, own], back_send.at[d % 2],
+                back_recv.at[d % 2], (peer, tensor),
+            ).start()
         come_pair[i, own] = back_stage[i, me]
-        outs.append(part)
         return low
 
-    for copy in parts:
-        copy.wait_recv()
-    sent += parts
+    settle(gs.at[seven], grad_recv.at[0])
     grad = gs[half : half + total]
     kernel_one = k1[...]
     grad_carried = jnp.where(same_head, fine(kernel_one, grad, TN), 0.0)
@@ -1243,26 +1198,45 @@
     value_in = give(2, jnp.where(iota(grad_values.shape, 0) < length, grad_values, 0.0))
 
 
+    settle(early_tensor.at[three], small_recv.at[0])
+    by_tensor = early_tensor[0] + early_tensor[1] + early_tensor[2] + early_tensor[3]
+    early_out[0] = jnp.where(iota(by_tensor.shape, 0) == 6, early[...], by_tensor)
+    smalls_early = []
+
+    def early_next(k):
+        if k > 0:
+            smalls_early[k - 1].wait_recv()
+            early_out[k] = early_out[k - 1] + early_in[k - 1]
+        if k < 3:
+            copy = remote(
+                early_out.at[k], early_in.at[k], small_send.at[1], small_recv.at[1 + k],
+                job_out.partners[(k + 1) % 3],
+            )
+            copy.start()
+            smalls_early.append(copy)
+
+    early_next(0)
     job_down[0].third()
-    token_parts[7].wait_recv()
-    sent += token_parts
+    settle(half_all, own_recv.at[2])
     tokens_all = tokens_own[...].reshape(total, width)
     source_v[...] = dot(tokens_all, value_in, TN).astype(bf16)
     kernel_back = jnp.zeros((LANES, LANES), f32)
     grad_state = grad_inverse
     for step in reversed(range(NS_ITERS)):
-        state, product, inner_one, inner_two = [newton[4 * step + i] for i in range(4)]
-        grad_next = 0.25 * fine(grad_state, 13.0 * identity - inner_two, NT)
-        grad_two = -0.25 * fine(state, grad_state, TN)
-        grad_product = fine(grad_two, 15.0 * identity - inner_one, NT)
-        grad_one = -fine(product, grad_two, TN)
-        grad_product = (
-            grad_product
-            + fine(grad_one, 7.0 * identity - product, NT)
-            - fine(product, grad_one, TN)
-        )
-        grad_state = grad_next + fine(kernel_two, grad_product, TN)
-        kernel_back = kernel_back + fine(grad_product, state, NT)
+        state, product, inner, outer, shifted = [newton[5 * step + i] for i in range(5)]
+        grad_outer = 0.25 * fine(state, grad_state, TN)
+        partial = (
+            fine(grad_outer, inner, NT)
+            - 15.0 * grad_outer
+            - fine(7.0 * product - inner, grad_outer, TN)
+        )
+        rest_part = 7.0 * grad_outer - fine(grad_outer, product, NT)
+        grad_state = (
+            0.25 * fine(grad_state, outer, NT)
+            + fine(kernel_two, partial, TN)
+            + fine(shifted, rest_part, TN)
+        )
+        kernel_back = kernel_back + fine(partial + fine(product, rest_part, TN), state, NT)
     squares = block_sums(kernel_two * kernel_two, same_head)
     spread_sum = jnp.where(same_head, block_sums(grad_state * newton[0], same_head), 0.0)
     kernel_back = kernel_back + (grad_state.T - 2.0 * kernel_two * spread_sum) / squares
@@ -1272,6 +1246,7 @@
     query_two = fine(grad_scores, key_marks)
     key_two = fine(grad_scores, query_marks, TN)
 
+    job_up[0].second()
     grad_one = fine(grad, carried, NT)
     both = kernel_one * grad_one
     first_scores = scale * (both - kernel_one * fine(both, ones))
@@ -1286,31 +1261,15 @@
     for i, held in enumerate((out_in, output)):
         shares[2 * i].wait_recv()
         block = held.at[block_rows(across[1], tok)]
-        copy = remote(block, block, share_send.at[i, 2], share_recv.at[i, 2], core)
+        copy = remote(block, block, share_send.at[i], share_recv.at[i, 2], core)
         copy.start()
         shares.append(copy)
-    source_kq[:, :LANES] = dot(tokens_all, key_in, TN).astype(bf16)
-    source_kq[:, LANES:] = dot(tokens_all, query_in, TN).astype(bf16)
+    lanes_own, lanes_both = slice(0, HEAD_DIM), slice(HEAD_DIM, LANES)
+    for ref, at in ((source_kq, lanes_own), (shared_kq, lanes_both)):
+        ref[...] = dot(
+            tokens_all, jnp.concatenate([key_in[:, at], query_in[:, at]], axis=1), TN
+        ).astype(bf16)
     job_kq.first()
-    for copy in smalls:
-        copy.wait_recv()
-    by_tensor = early_tensor[0] + early_tensor[1] + early_tensor[2] + early_tensor[3]
-    early_out[0] = jnp.where(iota(by_tensor.shape, 0) == 6, early[...], by_tensor)
-    smalls_early = []
-
-    def early_next(k):
-        if k > 0:
-            smalls_early[k - 1].wait_recv()
-            early_out[k] = early_out[k - 1] + early_in[k - 1]
-        if k < 3:
-            copy = remote(
-                early_out.at[k], early_in.at[k], small_send.at[1, k], small_recv.at[1, k],
-                job_out.partners[k],
-            )
-            copy.start()
-            smalls_early.append(copy)
-
-    early_next(0)
     shares[1].wait_recv()
     shares[4].wait_recv()
     pair, single = attn_pair[...].reshape(rows, LANES), unpacked(attn_single[...])
@@ -1339,7 +1298,7 @@
         row = jnp.sum(table, axis=0, keepdims=True)
         row = pltpu.roll(jnp.broadcast_to(row, (8, 2 * tok)), tok + 1, 1)
         conv_rows.append(row[0:1, :LANES])
-    late = late_seq.at[me]
+    late = late_out.at[0]
     late[...] = jnp.zeros(late.shape, f32)
     column = jnp.ones((8, total), bf16)
     for row, v in ((0, query_in), (1, value_in)):
@@ -1350,16 +1309,28 @@
     late[3:4, 0:LANES] = jnp.where(even, conv_rows[1], 0.0)
     late[4:5, 0:LANES] = jnp.where(even, 0.0, conv_rows[0])
     smalls_late = []
-    for d, device in enumerate(ring_peers):
-        copy = remote(late, late, small_send.at[2, d], small_recv.at[2, d], device)
-        copy.start()
-        smalls_late.append(copy)
+
+    def late_next(k):
+        if k > 0:
+            smalls_late[k - 1].wait_recv()
+            late_out[k] = late_out[k - 1] + late_in[k - 1]
+        if k < 3:
+            copy = remote(
+                late_out.at[k], late_in.at[k], small_send.at[2], small_recv.at[4 + k],
+                job_out.partners[(k + 1) % 3],
+            )
+            copy.start()
+            smalls_late.append(copy)
+
+    late_next(0)
+    early_next(1)
     job_down[1].third()
     job_down[0].fourth()
-    job_up[0].second()
-    for part in outs:
-        for copy in part:
-            copy.wait_recv()
+    job_up[0].third()
+    job_up[1].second()
+    job_v.second()
+    settle(come_pair.at[:, three], back_recv.at[0])
+    settle(come_single, back_recv.at[1])
     singles = []
     for i in range(3):
         tokens_low[:, i * LANES : (i + 1) * LANES] = come_pair[i].reshape(rows, LANES)
@@ -1372,10 +1343,9 @@
     def pass_sum(k, value, device):
         core_last[0, k] = value.astype(bf16)
         copy = remote(
-            core_last.at[0, k], core_last.at[1, k], last_send.at[k], last_recv.at[k], device
+            core_last.at[0, k], core_last.at[1, k], last_send.at[0], last_recv.at[k], device
         )
         copy.start()
-        sent.append(copy)
         return copy
 
     middle = pass_sum(1, input_part(far[1]), core)
@@ -1383,13 +1353,13 @@
     crossing = input_part(across[1])
     middle.wait_recv()
     y_last[0] = (crossing + core_last[1, 1].astype(f32)).astype(bf16)
-    final = remote(y_last.at[0], y_last.at[1], last_send.at[2], last_recv.at[2], across)
+    final = remote(y_last.at[0], y_last.at[1], last_send.at[0], last_recv.at[2], across)
     final.start()
-    sent.append(final)
     result = input_part(tensor) + jnp.concatenate(grads_first, axis=0)
-    job_v.second()
-    job_up[1].second()
-    job_up[0].third()
+    late_next(1)
+    job_kq.second()
+    early_next(2)
+    job_v.third()
     near.wait_recv()
     final.wait_recv()
     result = result + core_last[1, 0].astype(f32) + y_last[1].astype(f32)
@@ -1397,18 +1367,15 @@
     ends = []
     for j, device in enumerate((across, core)):
         copy = remote(
-            tokens_whole.at[mine], tokens_whole.at[mine], share_send.at[2, j], share_recv.at[2, j],
+            tokens_whole.at[mine], tokens_whole.at[mine], share_send.at[2], share_recv.at[2, j],
             device,
         )
         copy.start()
         ends.append(copy)
-    early_next(1)
-    job_kq.second()
     job_out.second()
     job_up[0].fourth()
     job_up[1].third()
-    early_next(2)
-    job_v.third()
+    late_next(2)
 
     def into(ref, k):
         def write(value):
@@ -1419,21 +1386,20 @@
     for k, job in enumerate(job_down):
         job.last(into(grad_down, k))
     done(14)
+    job_kq.third()
+    job_up[1].fourth()
     ends[0].wait_recv()
     block = tokens_whole.at[block_rows(across[1], tok)]
-    copy = remote(block, block, share_send.at[2, 2], share_recv.at[2, 2], core)
+    copy = remote(block, block, share_send.at[2], share_recv.at[2, 2], core)
     copy.start()
     ends.append(copy)
-    job_kq.third()
-    job_up[1].fourth()
     job_out.third()
     ends[1].wait_recv()
     ends[2].wait_recv()
     grad_tokens[...] = tokens_whole[...].astype(f32)
     done(1)
-    for copy in smalls_late:
-        copy.wait_recv()
     early_next(3)
+    late_next(3)
     by_seq = early_out[3]
     for ref, row in (
         (second_gain, 0), (second_shift, 1), (down_bias_grad, 2), (first_gain, 3),
@@ -1441,7 +1407,7 @@
     ):
         ref[...] = by_seq[row]
     proxy[...] = by_seq[7:8, 0:1]
-    by_seq = functools.reduce(lambda a, b: a + b, [late_seq[i] for i in range(n)])
+    by_seq = late_out[3]
     query_bias[...] = by_seq[0, :local]
     value_bias[...] = by_seq[1, :local]
     conv[...] = by_seq[2:5, :CONV]
@@ -1463,7 +1429,14 @@
     for k, job in enumerate(job_up):
         job.last(into(grad_up, k))
     done(12)
-    heads(job_kq, grad_key, grad_query)
+    def write_kq(result):
+        mine, both, come = [result[:, i * LANES : (i + 1) * LANES] for i in range(3)]
+        first, third = jnp.where(even, mine, come), jnp.where(even, come, mine)
+        for ref, at in ((grad_key, lanes_own), (grad_query, lanes_both)):
+            ref[:, :LANES] = jnp.concatenate([first[:, at], both[:, at]], axis=1)
+            ref[:, LANES:] = third[:, at]
+
+    job_kq.last(write_kq)
     done(2, 4)
 
     def write_out(value):
@@ -1471,11 +1444,21 @@
 
     job_out.last(write_out)
     done(8)
-    for copy in list(ring.copies.values()) + sent + shares + smalls + smalls_early + smalls_late + ends:
-        copy.wait_send()
-    for part in outs:
-        for copy in part:
-            copy.wait_send()
+    three_rows = x.at[pl.ds(0, 3 * tok)]
+    for ref, sem in (
+        (ks.at[seven], send.at[0]), (vs.at[seven], send.at[2]),
+        (attn_pair.at[three], out_send.at[0]), (attn_single, out_send.at[1]),
+        (out_whole.at[pl.ds(0, 3 * local)], whole_send.at[0]),
+        (pairs_in.at[three], a2a_send.at[0]), (singles_in.at[three], a2a_send.at[1]),
+        (three_blocks, a2a_send.at[2]), (out_whole, ag_send.at[0]), (out_whole, sum_send.at[0]),
+        (gs.at[seven], grad_send.at[0]), (come_pair.at[:, three], back_send.at[0]),
+        (come_single, back_send.at[1]), (three_rows, share_send.at[0]),
+        (three_rows, share_send.at[1]), (three_rows, share_send.at[2]),
+        (early_tensor.at[three], small_send.at[0]), (early_in, small_send.at[1]),
+        (late_in, small_send.at[2]), (tokens_own.at[pl.ds(0, n - 1), 0], own_send.at[0]),
+        (half_all, own_send.at[1]), (three_rows, last_send.at[0]),
+    ):
+        settle(ref, sem)
     for job in jobs:
         job.finish()
     for copy in stores:
@@ -1565,7 +1548,7 @@
             low(width, hidden), low(hidden, width), low(rows, width), low(local, width),
             low(width, width),
             low(3, 2, rows, LANES), low(total, LANES), low(total, LANES), low(total + tok, LANES),
-            wide(total, LANES), wide(total, LANES), wide(4 * NS_ITERS, LANES, LANES),
+            wide(total, LANES), wide(total, LANES), wide(5 * NS_ITERS, LANES, LANES),
             low(n - 1, tok, LANES), low(n - 1, piece, LANES), low(batch, tok, LANES),
             low(batch, piece, LANES),
             low(4, tok, LANES), low(4, piece, LANES), low(4, 2, tok, LANES),
@@ -1577,22 +1560,21 @@
             low(3, batch, tok, LANES), low(3, batch, tok // 2, LANES), low(3 * local, width),
             low(rows, width), wide(8, width), wide(4, 8, width), low(n, 2, tok // 2, width),
             low(rows, 3 * local), low(width, hidden), low(width, hidden), low(width, local),
-            low(width, LANES), low(width, 2 * LANES), wide(4, 8, width), wide(3, 8, width),
-            wide(n, 8, 2 * LANES), low(rows, width), wide(2, 2, 2, 2, piece, width),
+            low(width, LANES), low(width, LANES), low(width, LANES), wide(4, 8, width), wide(3, 8, width),
+            wide(4, 8, 2 * LANES), wide(3, 8, 2 * LANES), low(rows, width), wide(2, 2, 2, 2, piece, width),
         ]
         + [
             b
             for first, w in (
-                *((hidden // 2, hidden // 2),) * 4, (local, local), (LANES, local), (2 * LANES, 2 * local)
+                *((hidden // 2, hidden // 2),) * 4, (local, local), (LANES, local), (LANES, 2 * local)
             )
             for b in scatter_buffers(first, w, block)
         ]
         + [
-            dma(8), dma(3, n - 1), dma(3, n - 1), dma(n - 1), dma(n - 1), dma(3, 2),
-            dma(3, 2), dma(2, 3, 2), dma(2, 3, 2), dma(2, 2, 3), dma(2, 2, 3), dma(2, 2, 3),
-            dma(2, 2, 3), dma(n - 1),
-            dma(n - 1), dma(3, n - 1), dma(3, n - 1), dma(3, 3), dma(3, 3), dma(3, n - 1),
-            dma(3, n - 1), dma(JOBS, 10), dma(JOBS, 10), dma(8), dma(8), dma(3), dma(3), dma(RESULTS),
+            dma(8), dma(3), dma(3), dma(2), dma(2), dma(1), dma(1), dma(3), dma(3), dma(1),
+            dma(2, 2, 3), dma(1), dma(2, 2, 3), dma(1), dma(1), dma(2), dma(2), dma(3), dma(3, 3),
+            dma(3), dma(7), dma(JOBS, 2), dma(JOBS, 5), dma(2), dma(3), dma(1), dma(3),
+            dma(RESULTS),
         ],
         compiler_params=pltpu.CompilerParams(
             collective_id=0, has_side_effects=True, vmem_limit_bytes=56 * 2**20

time: 134 us -> 128 us (0.955)
  Pallas kernels: 133 us -> 127 us
    pallas_call x1, Pallas kernels: 129 us -> 123 us  [gathered_plan(): pl.pallas_call(functools.partial(layer_kernel, n), out_shape=results, in_...]
where the time goes in v5:
time: 128 us
  Pallas kernels  127 us (99%)
    pallas_call x1, Pallas kernels, gathered_plan(): pl.pallas_call(functools.partial(layer_kernel, n), out_shape=results, in_...  123 us
    pallas_call x1, Pallas kernels, gathered_plan(): pl.pallas_call(finish_kernel, out_shape=results, in_specs=[HBM] * RESULTS...  4.06 us

profile of v5, /device:TPU:0, one launch (start us, length us, event | category | flops | bytes accessed | tf_op | source)
XLA Modules:
  0.0 128.2 jit_solution(2845165550993979808)
XLA Ops:
  0.7 123.3 %layer.1 = (bf16[512,768]{1,0:T(8,128)(2,1)}, f32[512,768]{1,0:T(8,128)}, f32[96,192]{1,0:T(8,128)}, f32[192]{0:T(256)}, f32[96,192]{1,0:T(8,128)}, /*index=5*/f...) custom-call(s32[4]{0:T(128)} %lengths.1, ...), custom_call_target="tpu_custom_call" | custom-call | tf_op jit(solution)/shard_map/layer/pallas_call | solution.py:1539
  124.0 4.1 %finish.1 = (bf16[512,768]{1,0:T(8,128)(2,1)}, f32[512,768]{1,0:T(8,128)}, f32[96,192]{1,0:T(8,128)}, f32[192]{0:T(256)}, f32[96,192]{1,0:T(8,128)}, /*index=5*/...) custom-call(bf16[512,768]{1,0:T(8,128)(2,1)} %get-tuple-element.57.r, ...), custom_call_target="tpu_custom_call" | custom-call | tf_op jit(solution)/shard_map/finish/pallas_call | solution.py:1589

commit v6 on v5

--- a/solution.py
+++ b/solution.py
@@ -644,15 +644,6 @@
             write(self.held[self.slots[0]].astype(f32) + self.first_in[3].astype(f32))
 
 
-class Heads(Scatter):
-    def joined(self, mine, come):
-        even = self.bits[0] == 0
-        pair, other = jnp.where(even, mine, come), jnp.where(even, come, mine)
-        return jnp.concatenate(
-            [pair] + [other[:, k : k + HEAD_DIM] for k in range(0, other.shape[1], LANES)], axis=1
-        )
-
-
 class Pairs(Scatter):
     def second(self):
         self.arrived(self.first_in, 0)
@@ -756,7 +747,7 @@
         )
 
 
-JOBS = 7
+JOBS = 6
 RESULTS = 19
 
 
@@ -778,16 +769,16 @@
     n, lengths, x_far, wq_far, qb, wk_far, wv_far, vb, taps, out_far, out_bias, gain_one,
     shift_one, up_far, up_bias, down_far, down_bias, gain_two, shift_two, grad_far, results, ready,
     x, wk, wq, wv, up_weight, down_weight, out_grad, out_weight, out_whole,
-    stage, ks, qs, vs, k1, p3, newton, out_stage, out_single, attn_pair, attn_single,
-    pairs_in, singles_in, heads_out, grad_attn, hidden, slope, active, down_in, up_in,
+    up_turned, down_turned, stage, ks, qs, vs, k1, p3, newton, out_stage, out_single, attn_pair, attn_single,
+    pairs_in, singles_in, heads_out, hidden, slope, active, down_in, up_in,
     core_out, core_in, y_out, y_in, core_last, y_last,
     gs, back_stage, back_single, come_pair, come_single, weight_in, out_in, early, early_tensor, tokens_own, tokens_low, source_up,
-    source_down, source_out, source_v, source_kq, shared_kq, early_out, early_in, late_out, late_in, tokens_whole,
+    source_down, source_out, source_own, source_both, early_out, early_in, late_out, late_in, tokens_whole,
     parts_held,
     *rest,
 ):
     buffers, sems = rest[: 6 * JOBS], rest[6 * JOBS :]
-    (load, send, recv, out_send, out_recv, whole_send, whole_recv, a2a_send, a2a_recv, ag_send,
+    (load, send, recv, out_send, out_recv, whole_send, whole_recv, copy_send, copy_recv, ag_send,
      ag_recv, sum_send, sum_recv, grad_send, grad_recv, back_send, back_recv, share_send,
      share_recv, small_send, small_recv, job_send, job_recv, own_send, own_recv, last_send, last_recv,
      store) = sems
@@ -814,7 +805,16 @@
     ring_peers = around(n, me, tensor)
     peers = others(me, tensor)
     core, across, far = peers
-    mine = block_rows(tensor, tok)
+
+    def batch_of(t):
+        return lax.rem(t - me + 8, 4)
+
+    def rows_at(t):
+        return block_rows(batch_of(t), tok)
+
+    mine = rows_at(tensor)
+    at_home = batch_of(tensor) == own
+    away = batch_of(tensor) != own
     local = wk.shape[0]
     barrier = greet(ring_peers + peers)
     loads = []
@@ -836,13 +836,12 @@
             (Line, source_up, (0, span), (0, 1, 2)),
             (Line, source_up, (span, span), (0, 1, 2)),
             (Scatter, source_out, (0, local), (0, 1, 2)),
-            (Heads, source_v, (0, LANES), (0, 1, 2)),
-            (Pairs, source_kq, (0, LANES), (0, 1, 2)),
+            (Pairs, source_own, (0, local), (0, 1, 2)),
         ))
     ]
     job_down, job_up = jobs[0:2], jobs[2:4]
-    job_out, job_v, job_kq = jobs[4:]
-    job_kq.shared = shared_kq
+    job_out, job_heads = jobs[4:]
+    job_heads.shared = source_both
 
     owned = (ks, qs, vs)
     offsets = (0, 0, half)
@@ -921,6 +920,10 @@
         )
         start = 3 * LANES + i * HEAD_DIM
         weight_in[start : start + HEAD_DIM] = jnp.where(even, single, pair[:HEAD_DIM])
+    for copy in loads[5:]:
+        copy.wait()
+    up_turned[...] = up_weight[...].T
+    down_turned[...] = down_weight[...].T
     settle(ks.at[seven], recv.at[0])
     keys = ks[...]
     key_marks = jnp.where(same_head, dot(members, keys) / counts, 0.0)
@@ -935,8 +938,31 @@
     inverse = jnp.where(
         same_head, kernel_two.T / block_sums(kernel_two * kernel_two, same_head), 0.0
     )
+    def scores_one():
+        values = fine(queries, key_marks, NT) * scale
+        left = iota(values.shape, 1) < HEAD_DIM
+        top_left = jnp.max(jnp.where(left, values, negative), axis=1, keepdims=True)
+        top_right = jnp.max(jnp.where(left, negative, values), axis=1, keepdims=True)
+        return jnp.exp(values - jnp.where(left, top_left, top_right))
+
+    def scores_three():
+        values = fine(keys, query_marks, NT) * scale
+        alive = iota(values.shape, 0) < length
+        values = jnp.where(alive, values, negative)
+        weights = jnp.exp(values - jnp.max(values, axis=0, keepdims=True))
+        return jnp.where(alive, weights, 0.0)
+
     product = fine(kernel_two, inverse)
     for step in range(NS_ITERS):
+        if step == 0:
+            weights_one = scores_one()
+        if step == 1:
+            k1[...] = weights_one / fine(weights_one, ones)
+        if step == 2:
+            weights_three = scores_three()
+        if step == 3:
+            third_prob = weights_three / jnp.sum(weights_three, axis=0, keepdims=True)
+            p3[...] = third_prob
         inner = fine(product, 7.0 * identity - product)
         outer = 13.0 * identity - fine(product, 15.0 * identity - inner)
         newton[5 * step] = inverse
@@ -953,21 +979,6 @@
     norm_sum = jnp.where(side == 0, first + second, first) / (batch * HEADS)
     early[7:8] = jnp.broadcast_to(norm_sum, (1, width))
 
-    first_scores = fine(queries, key_marks, NT) * scale
-    left = iota(first_scores.shape, 1) < HEAD_DIM
-    top_left = jnp.max(jnp.where(left, first_scores, negative), axis=1, keepdims=True)
-    top_right = jnp.max(jnp.where(left, negative, first_scores), axis=1, keepdims=True)
-    weights = jnp.exp(first_scores - jnp.where(left, top_left, top_right))
-    k1[...] = weights / fine(weights, ones)
-
-    third_scores = fine(keys, query_marks, NT) * scale
-    alive = iota(third_scores.shape, 0) < length
-    third_scores = jnp.where(alive, third_scores, negative)
-    weights = jnp.exp(third_scores - jnp.max(third_scores, axis=0, keepdims=True))
-    weights = jnp.where(alive, weights, 0.0)
-    third_prob = weights / jnp.sum(weights, axis=0, keepdims=True)
-    p3[...] = third_prob
-
     settle(vs.at[seven], recv.at[2])
     values = vs[half : half + total]
     third_out = jnp.where(same_head, fine(third_prob, values, TN), 0.0)
@@ -979,29 +990,33 @@
         nystrom = fine(k1[pl.ds(start, tok)], carried)
         convolved = conv_block(matrices, vs[pl.ds(start, 2 * tok)])
         low = (nystrom + convolved).astype(bf16)
-        if d == n:
-            attn_pair[own] = low
-            continue
+        device = (peer, lax.rem(own + peer, 4))
         if d % 2 == 0:
-            source, target = out_stage.at[d - 1], attn_pair.at[own]
+            source, target = out_stage.at[d - 1], pairs_in.at[tensor]
             source[...] = low
         else:
-            source, target = out_single.at[d - 1], attn_single.at[own]
+            source, target = out_single.at[d - 1], singles_in.at[tensor]
             source[...] = packed(low)
-        remote(source, target, out_send.at[d % 2], out_recv.at[d % 2], (peer, tensor)).start()
+        copy = remote(source, target, out_send.at[d % 2], out_recv.at[d % 2], device)
+        if d < n:
+            copy.start()
+            continue
+        attn_pair[own] = low
+        pl.when(away)(copy.start)
+
+        @pl.when(at_home)
+        def _():
+            pairs_in[tensor] = low
+
     three = pl.ds(0, 3)
-    settle(attn_pair.at[three], out_recv.at[0])
-    settle(attn_single, out_recv.at[1])
+
+    def settle_home(ref, some, sem):
+        pl.when(away)(lambda: settle(ref, sem))
+        pl.when(at_home)(lambda: settle(ref.at[some], sem))
+
+    settle_home(pairs_in, three, out_recv.at[0])
+    settle(singles_in, out_recv.at[1])
     settle(out_whole.at[pl.ds(0, 3 * local)], whole_recv.at[0])
-
-    for i in (2, 1, 0):
-        t = peers[i][1]
-        for j, (held, come) in enumerate(((attn_pair, pairs_in), (attn_single, singles_in))):
-            remote(
-                held.at[t], come.at[tensor], a2a_send.at[j], a2a_recv.at[j], peers[i]
-            ).start()
-    pairs_in[tensor] = attn_pair[tensor]
-    singles_in[tensor] = attn_single[tensor]
     z, side_of_chip = me // 2, tensor % 2
     beside = (me + 1 - 2 * side, tensor)
     def give_tokens(src, dst, i, device):
@@ -1026,10 +1041,6 @@
             come = tokens_own.at[2 * lax.rem(z + 4 - k, 4) + side, side_of_chip]
             give_tokens(come, come, 1, beside)
 
-    for copy in loads[5:]:
-        copy.wait()
-    settle(pairs_in.at[three], a2a_recv.at[0])
-    settle(singles_in.at[three], a2a_recv.at[1])
     def line(vector):
         return vector[...].reshape(1, vector.shape[0])
 
@@ -1041,7 +1052,7 @@
     )
 
     def rows_of(c):
-        return pl.ds(pl.multiple_of(tensor * tok + c * piece, piece), piece)
+        return pl.ds(pl.multiple_of(batch_of(tensor) * tok + c * piece, piece), piece)
 
     def normed(c):
         at = slice(c * piece, (c + 1) * piece)
@@ -1070,14 +1081,23 @@
 
     def down(c, t):
         at = pl.ds(t, 2)
-        grad = dot(down_in[c, at].reshape(tok, width), down_weight[...], NT)
+        grad = dot(down_in[c, at].reshape(tok, width), down_turned[...])
         low = (grad * slope[c, at].reshape(tok, hidden_width)).astype(bf16)
         up_in[c, at] = low.reshape(2, piece, hidden_width)
-        return dot(low, up_weight[...], NT)
+        return dot(low, up_turned[...])
 
     after_norm_one = [normed(c) for c in chunks]
     ring.run(0, hidden, up)
     pass_tokens()
+    for d in range(1, n):
+        if d % 2 == 0:
+            source, target = out_stage.at[d - 1], attn_pair.at[own]
+        else:
+            source, target = out_single.at[d - 1], attn_single.at[own]
+        remote(
+            source, target, copy_send.at[d % 2], copy_recv.at[d % 2],
+            (lax.rem(me + d, n), tensor),
+        ).start()
 
     grads_second, sums_second = [], []
     for c in chunks:
@@ -1119,16 +1139,28 @@
             heads_out[t, 1, at] = jnp.concatenate(
                 [heads[:, start : start + HEAD_DIM], pair[:, HEAD_DIM:]], axis=1
             )
-        for i in (2, 1, 0):
-            remote(
-                heads_out.at[peers[i][1], :, pl.ds(c * piece, piece)],
-                grad_attn.at[:, rows_of(c)], a2a_send.at[2], a2a_recv.at[2], peers[i],
-            ).start()
+        b = batch_of(tensor)
+        there = pl.ds(pl.multiple_of(half + me * tok + c * piece, 16), piece)
+        for t in range(4):
+            for k, device in enumerate(((2 * b + side, t), (2 * b + 1 - side, t))):
+                copy = remote(
+                    heads_out.at[t, k, pl.ds(c * piece, piece)], gs.at[there], grad_send.at[0],
+                    grad_recv.at[0], device,
+                )
+                if k == 1:
+                    copy.start()
+                else:
+                    pl.when((batch_of(tensor) != own) | (tensor != t))(copy.start)
         grads_first.append(grad_first)
         sums_first.append(
             (total_of(grad_hidden * normal), total_of(grad_hidden), total_of(low.astype(f32)))
         )
-    grad_attn[:, mine] = heads_out[tensor]
+
+    @pl.when(at_home)
+    def _():
+        here = pl.ds(pl.multiple_of(half + me * tok, 16), tok)
+        gs[here] = heads_out[tensor, 0]
+
     source_up[...] = dot(
         hidden[...].reshape(everything), up_in[...].reshape(every_hidden), TN
     ).astype(bf16)
@@ -1138,17 +1170,6 @@
     early[6:7] = dot(jnp.ones((8, rows), bf16), up_in[...].reshape(every_hidden))[0:1]
     early_tensor[tensor] = early[...]
     job_up[0].first(range(2))
-    three_blocks = grad_attn.at[:, pl.ds(0, 3 * tok)]
-    settle(three_blocks, a2a_recv.at[2])
-
-    here = pl.ds(pl.multiple_of(half + me * tok, 16), tok)
-    for d in range(1, n):
-        peer = lax.rem(me + d, n)
-        remote(
-            grad_attn.at[d % 2, block_rows(peer // 2, tok)], gs.at[here], grad_send.at[0],
-            grad_recv.at[0], (peer, tensor),
-        ).start()
-    gs[here] = grad_attn[0, block_rows(own, tok)]
     for i, device in enumerate(peers):
         remote(
             early, early_tensor.at[tensor], small_send.at[0], small_recv.at[0], device
@@ -1163,7 +1184,6 @@
             shares.append(copy)
     job_down[0].second()
     job_up[0].first(range(2, 4))
-    job_down[1].second()
     job_up[1].first()
     settle(tokens_own.at[pl.ds(0, 4), 0], own_recv.at[1])
     half_all = tokens_own.at[:, side_of_chip]
@@ -1184,20 +1204,13 @@
         come_pair[i, own] = back_stage[i, me]
         return low
 
-    settle(gs.at[seven], grad_recv.at[0])
+    eight = gs.at[pl.ds(0, total)]
+    settle_home(eight, seven, grad_recv.at[0])
     grad = gs[half : half + total]
     kernel_one = k1[...]
     grad_carried = jnp.where(same_head, fine(kernel_one, grad, TN), 0.0)
     grad_third = fine(inverse, grad_carried, TN)
     grad_inverse = fine(grad_carried, third_out, NT)
-    third_prob = p3[...]
-    convolved = jnp.concatenate(
-        [conv_block(reverse, gs[m * tok : (m + 2) * tok]) for m in range(n)], axis=0
-    )
-    grad_values = fine(third_prob, grad_third) + convolved
-    value_in = give(2, jnp.where(iota(grad_values.shape, 0) < length, grad_values, 0.0))
-
-
     settle(early_tensor.at[three], small_recv.at[0])
     by_tensor = early_tensor[0] + early_tensor[1] + early_tensor[2] + early_tensor[3]
     early_out[0] = jnp.where(iota(by_tensor.shape, 0) == 6, early[...], by_tensor)
@@ -1217,9 +1230,6 @@
 
     early_next(0)
     job_down[0].third()
-    settle(half_all, own_recv.at[2])
-    tokens_all = tokens_own[...].reshape(total, width)
-    source_v[...] = dot(tokens_all, value_in, TN).astype(bf16)
     kernel_back = jnp.zeros((LANES, LANES), f32)
     grad_state = grad_inverse
     for step in reversed(range(NS_ITERS)):
@@ -1237,6 +1247,27 @@
             + fine(shifted, rest_part, TN)
         )
         kernel_back = kernel_back + fine(partial + fine(product, rest_part, TN), state, NT)
+        if step == NS_ITERS - 1:
+            third_prob = p3[...]
+            convolved = jnp.concatenate(
+                [conv_block(reverse, gs[m * tok : (m + 2) * tok]) for m in range(n)], axis=0
+            )
+            grad_values = fine(third_prob, grad_third) + convolved
+            value_in = give(
+                2, jnp.where(iota(grad_values.shape, 0) < length, grad_values, 0.0)
+            )
+        if step == NS_ITERS - 2:
+            grad_one = fine(grad, carried, NT)
+            both = kernel_one * grad_one
+            first_scores = scale * (both - kernel_one * fine(both, ones))
+        if step == NS_ITERS - 3:
+            key_one = jnp.where(same_head, fine(first_scores, queries, TN), 0.0)
+            delta = fine(jnp.ones((8, LANES), bf16), grad_third * third_out, NT)[0:1]
+            third_scores = scale * third_prob * (fine(values, grad_third, NT) - delta)
+        if step == NS_ITERS - 4:
+            query_three = jnp.where(same_head, fine(third_scores, keys, TN), 0.0)
+            key_part = fine(third_scores, query_marks)
+            query_part = fine(first_scores, key_marks)
     squares = block_sums(kernel_two * kernel_two, same_head)
     spread_sum = jnp.where(same_head, block_sums(grad_state * newton[0], same_head), 0.0)
     kernel_back = kernel_back + (grad_state.T - 2.0 * kernel_two * spread_sum) / squares
@@ -1246,32 +1277,28 @@
     query_two = fine(grad_scores, key_marks)
     key_two = fine(grad_scores, query_marks, TN)
 
-    job_up[0].second()
-    grad_one = fine(grad, carried, NT)
-    both = kernel_one * grad_one
-    first_scores = scale * (both - kernel_one * fine(both, ones))
-    key_one = jnp.where(same_head, fine(first_scores, queries, TN), 0.0)
-    delta = fine(jnp.ones((8, LANES), bf16), grad_third * third_out, NT)[0:1]
-    third_scores = scale * third_prob * (fine(values, grad_third, NT) - delta)
-    query_three = jnp.where(same_head, fine(third_scores, keys, TN), 0.0)
-    job_v.first()
-    key_in = give(0, fine(third_scores, query_marks) + fine(members, (key_one + key_two) / counts))
-    query_in = give(1, fine(first_scores, key_marks) + fine(members, (query_two + query_three) / counts))
+    key_in = give(0, key_part + fine(members, (key_one + key_two) / counts))
+    query_in = give(1, query_part + fine(members, (query_two + query_three) / counts))
 
     for i, held in enumerate((out_in, output)):
         shares[2 * i].wait_recv()
-        block = held.at[block_rows(across[1], tok)]
+        block = held.at[rows_at(across[1])]
         copy = remote(block, block, share_send.at[i], share_recv.at[i, 2], core)
         copy.start()
         shares.append(copy)
+    job_up[0].second()
+    job_down[1].second()
+    settle(half_all, own_recv.at[2])
+    tokens_all = tokens_own[...].reshape(total, width)
     lanes_own, lanes_both = slice(0, HEAD_DIM), slice(HEAD_DIM, LANES)
-    for ref, at in ((source_kq, lanes_own), (shared_kq, lanes_both)):
-        ref[...] = dot(
-            tokens_all, jnp.concatenate([key_in[:, at], query_in[:, at]], axis=1), TN
-        ).astype(bf16)
-    job_kq.first()
+    for ref, at in ((source_own, lanes_own), (source_both, lanes_both)):
+        grads = jnp.concatenate([key_in[:, at], query_in[:, at], value_in[:, at]], axis=1)
+        ref[...] = dot(tokens_all, grads, TN).astype(bf16)
+    job_heads.first()
     shares[1].wait_recv()
     shares[4].wait_recv()
+    settle(attn_pair.at[three], copy_recv.at[0])
+    settle(attn_single, copy_recv.at[1])
     pair, single = attn_pair[...].reshape(rows, LANES), unpacked(attn_single[...])
     single = single.reshape(rows, HEAD_DIM)
     attention = jnp.concatenate(
@@ -1326,9 +1353,7 @@
     early_next(1)
     job_down[1].third()
     job_down[0].fourth()
-    job_up[0].third()
     job_up[1].second()
-    job_v.second()
     settle(come_pair.at[:, three], back_recv.at[0])
     settle(come_single, back_recv.at[1])
     singles = []
@@ -1338,7 +1363,7 @@
     tokens_low[:, 3 * LANES :] = jnp.concatenate(singles, axis=1)
 
     def input_part(t):
-        return dot(tokens_low[block_rows(t, tok)], weight_in[...])
+        return dot(tokens_low[rows_at(t)], weight_in[...])
 
     def pass_sum(k, value, device):
         core_last[0, k] = value.astype(bf16)
@@ -1357,9 +1382,11 @@
     final.start()
     result = input_part(tensor) + jnp.concatenate(grads_first, axis=0)
     late_next(1)
-    job_kq.second()
+    job_up[0].third()
+    job_heads.second()
     early_next(2)
-    job_v.third()
+    job_up[1].third()
+    job_up[0].fourth()
     near.wait_recv()
     final.wait_recv()
     result = result + core_last[1, 0].astype(f32) + y_last[1].astype(f32)
@@ -1373,8 +1400,6 @@
         copy.start()
         ends.append(copy)
     job_out.second()
-    job_up[0].fourth()
-    job_up[1].third()
     late_next(2)
 
     def into(ref, k):
@@ -1386,10 +1411,10 @@
     for k, job in enumerate(job_down):
         job.last(into(grad_down, k))
     done(14)
-    job_kq.third()
+    job_heads.third()
     job_up[1].fourth()
     ends[0].wait_recv()
-    block = tokens_whole.at[block_rows(across[1], tok)]
+    block = tokens_whole.at[rows_at(across[1])]
     copy = remote(block, block, share_send.at[2], share_recv.at[2, 2], core)
     copy.start()
     ends.append(copy)
@@ -1414,30 +1439,22 @@
     shares[3].wait_recv()
     shares[5].wait_recv()
     done(0, 3, 6, 7, 9, 10, 11, 13, 15, 16, 17, 18)
-
-    def heads(job, *refs):
-        def write(result):
-            for i, ref in enumerate(refs):
-                start = len(refs) * LANES + i * HEAD_DIM
-                ref[:, :LANES] = result[:, i * LANES : (i + 1) * LANES]
-                ref[:, LANES:] = result[:, start : start + HEAD_DIM]
-
-        job.last(write)
-
-    heads(job_v, grad_value)
-    done(5)
     for k, job in enumerate(job_up):
         job.last(into(grad_up, k))
     done(12)
-    def write_kq(result):
-        mine, both, come = [result[:, i * LANES : (i + 1) * LANES] for i in range(3)]
-        first, third = jnp.where(even, mine, come), jnp.where(even, come, mine)
-        for ref, at in ((grad_key, lanes_own), (grad_query, lanes_both)):
-            ref[:, :LANES] = jnp.concatenate([first[:, at], both[:, at]], axis=1)
-            ref[:, LANES:] = third[:, at]
-
-    job_kq.last(write_kq)
-    done(2, 4)
+
+    def write_heads(result):
+        for i, ref in enumerate((grad_key, grad_query, grad_value)):
+            mine, both, come = [
+                result[:, k * local + i * HEAD_DIM : k * local + (i + 1) * HEAD_DIM]
+                for k in range(3)
+            ]
+            ref[:, :HEAD_DIM] = jnp.where(even, mine, come)
+            ref[:, HEAD_DIM:LANES] = both
+            ref[:, LANES:] = jnp.where(even, come, mine)
+
+    job_heads.last(write_heads)
+    done(2, 4, 5)
 
     def write_out(value):
         grad_out[...] = value.T
@@ -1445,13 +1462,15 @@
     job_out.last(write_out)
     done(8)
     three_rows = x.at[pl.ds(0, 3 * tok)]
+    settle_home(pairs_in, three, out_send.at[0])
+    settle_home(eight, seven, grad_send.at[0])
     for ref, sem in (
         (ks.at[seven], send.at[0]), (vs.at[seven], send.at[2]),
-        (attn_pair.at[three], out_send.at[0]), (attn_single, out_send.at[1]),
+        (singles_in, out_send.at[1]), (attn_pair.at[three], copy_send.at[0]),
+        (attn_single, copy_send.at[1]),
         (out_whole.at[pl.ds(0, 3 * local)], whole_send.at[0]),
-        (pairs_in.at[three], a2a_send.at[0]), (singles_in.at[three], a2a_send.at[1]),
-        (three_blocks, a2a_send.at[2]), (out_whole, ag_send.at[0]), (out_whole, sum_send.at[0]),
-        (gs.at[seven], grad_send.at[0]), (come_pair.at[:, three], back_send.at[0]),
+        (out_whole, ag_send.at[0]), (out_whole, sum_send.at[0]),
+        (come_pair.at[:, three], back_send.at[0]),
         (come_single, back_send.at[1]), (three_rows, share_send.at[0]),
         (three_rows, share_send.at[1]), (three_rows, share_send.at[2]),
         (early_tensor.at[three], small_send.at[0]), (early_in, small_send.at[1]),
@@ -1546,13 +1565,13 @@
         + [
             low(rows, width), low(local, width), low(local, width), low(local, width),
             low(width, hidden), low(hidden, width), low(rows, width), low(local, width),
-            low(width, width),
+            low(width, width), low(hidden, width), low(width, hidden),
             low(3, 2, rows, LANES), low(total, LANES), low(total, LANES), low(total + tok, LANES),
             wide(total, LANES), wide(total, LANES), wide(5 * NS_ITERS, LANES, LANES),
-            low(n - 1, tok, LANES), low(n - 1, piece, LANES), low(batch, tok, LANES),
+            low(n, tok, LANES), low(n, piece, LANES), low(batch, tok, LANES),
             low(batch, piece, LANES),
             low(4, tok, LANES), low(4, piece, LANES), low(4, 2, tok, LANES),
-            low(2, rows, LANES), low(2, 4, piece, width), wide(2, 4, piece, hidden),
+            low(2, 4, piece, width), wide(2, 4, piece, hidden),
             low(2, 4, piece, hidden), low(2, 4, piece, width), low(2, 4, piece, hidden),
             low(2, 2, 2, piece, width), low(2, 2, 2, piece, width), low(2, 2, piece, width),
             low(2, 2, piece, width), low(2, 2, tok, width), low(2, tok, width),
@@ -1560,18 +1579,18 @@
             low(3, batch, tok, LANES), low(3, batch, tok // 2, LANES), low(3 * local, width),
             low(rows, width), wide(8, width), wide(4, 8, width), low(n, 2, tok // 2, width),
             low(rows, 3 * local), low(width, hidden), low(width, hidden), low(width, local),
-            low(width, LANES), low(width, LANES), low(width, LANES), wide(4, 8, width), wide(3, 8, width),
+            low(width, local), low(width, local), wide(4, 8, width), wide(3, 8, width),
             wide(4, 8, 2 * LANES), wide(3, 8, 2 * LANES), low(rows, width), wide(2, 2, 2, 2, piece, width),
         ]
         + [
             b
             for first, w in (
-                *((hidden // 2, hidden // 2),) * 4, (local, local), (LANES, local), (LANES, 2 * local)
+                *((hidden // 2, hidden // 2),) * 4, (local, local), (local, 3 * local)
             )
             for b in scatter_buffers(first, w, block)
         ]
         + [
-            dma(8), dma(3), dma(3), dma(2), dma(2), dma(1), dma(1), dma(3), dma(3), dma(1),
+            dma(8), dma(3), dma(3), dma(2), dma(2), dma(1), dma(1), dma(2), dma(2), dma(1),
             dma(2, 2, 3), dma(1), dma(2, 2, 3), dma(1), dma(1), dma(2), dma(2), dma(3), dma(3, 3),
             dma(3), dma(7), dma(JOBS, 2), dma(JOBS, 5), dma(2), dma(3), dma(1), dma(3),
             dma(RESULTS),

time: 128 us -> 120 us (0.938)
  Pallas kernels: 127 us -> 119 us
    pallas_call x1, Pallas kernels: 123 us -> 115 us  [gathered_plan(): pl.pallas_call(functools.partial(layer_kernel, n), out_shape=results, in_...]
where the time goes in v6:
time: 120 us
  Pallas kernels  119 us (99%)
    pallas_call x1, Pallas kernels, gathered_plan(): pl.pallas_call(functools.partial(layer_kernel, n), out_shape=results, in_...  115 us
    pallas_call x1, Pallas kernels, gathered_plan(): pl.pallas_call(finish_kernel, out_shape=results, in_specs=[HBM] * RESULTS...  4.06 us

profile of v6, /device:TPU:0, one launch (start us, length us, event | category | flops | bytes accessed | tf_op | source)
XLA Modules:
  0.0 119.9 jit_solution(9012118355207622331)
XLA Ops:
  0.7 115.0 %layer.1 = (bf16[512,768]{1,0:T(8,128)(2,1)}, f32[512,768]{1,0:T(8,128)}, f32[96,192]{1,0:T(8,128)}, f32[192]{0:T(256)}, f32[96,192]{1,0:T(8,128)}, /*index=5*/f...) custom-call(s32[4]{0:T(128)} %lengths.1, ...), custom_call_target="tpu_custom_call" | custom-call | tf_op jit(solution)/shard_map/layer/pallas_call | solution.py:1558
  115.6 4.1 %finish.1 = (bf16[512,768]{1,0:T(8,128)(2,1)}, f32[512,768]{1,0:T(8,128)}, f32[96,192]{1,0:T(8,128)}, f32[192]{0:T(256)}, f32[96,192]{1,0:T(8,128)}, /*index=5*/...) custom-call(bf16[512,768]{1,0:T(8,128)(2,1)} %get-tuple-element.57.r, ...), custom_call_target="tpu_custom_call" | custom-call | tf_op jit(solution)/shard_map/finish/pallas_call | solution.py:1608

commit v7 on v6

--- a/solution.py
+++ b/solution.py
@@ -748,7 +748,9 @@
 
 
 JOBS = 6
-RESULTS = 19
+MATRICES = 8
+RESULTS = MATRICES + 2
+OUTPUTS = 19
 
 
 def layer_kernel(
@@ -757,7 +759,7 @@
     *rest,
 ):
     results, rest = rest[:RESULTS], rest[RESULTS:]
-    ready, rest = rest[:RESULTS], rest[RESULTS:]
+    ready, rest = rest[:MATRICES], rest[MATRICES:]
     layer_body(
         n, lengths, x_far, wq_far, qb, wk_far, wv_far, vb, taps, out_far, out_bias, gain_one,
         shift_one, up_far, up_bias, down_far, down_bias, gain_two, shift_two, grad_far, results,
@@ -782,9 +784,8 @@
      ag_recv, sum_send, sum_recv, grad_send, grad_recv, back_send, back_recv, share_send,
      share_recv, small_send, small_recv, job_send, job_recv, own_send, own_recv, last_send, last_recv,
      store) = sems
-    (output, grad_tokens, grad_query, query_bias, grad_key, grad_value, value_bias, conv, grad_out,
-     out_bias_grad, first_gain, first_shift, grad_up, up_bias_grad, grad_down, down_bias_grad,
-     second_gain, second_shift, proxy) = ready
+    output, grad_tokens, grad_query, grad_key, grad_value, grad_out, grad_up, grad_down = ready
+    ready = (*ready, early_out.at[3], late_out.at[3])
     stores = []
 
     def done(*numbers):
@@ -1410,7 +1411,7 @@
 
     for k, job in enumerate(job_down):
         job.last(into(grad_down, k))
-    done(14)
+    done(7)
     job_heads.third()
     job_up[1].fourth()
     ends[0].wait_recv()
@@ -1425,23 +1426,12 @@
     done(1)
     early_next(3)
     late_next(3)
-    by_seq = early_out[3]
-    for ref, row in (
-        (second_gain, 0), (second_shift, 1), (down_bias_grad, 2), (first_gain, 3),
-        (first_shift, 4), (out_bias_grad, 5), (up_bias_grad, 6),
-    ):
-        ref[...] = by_seq[row]
-    proxy[...] = by_seq[7:8, 0:1]
-    by_seq = late_out[3]
-    query_bias[...] = by_seq[0, :local]
-    value_bias[...] = by_seq[1, :local]
-    conv[...] = by_seq[2:5, :CONV]
     shares[3].wait_recv()
     shares[5].wait_recv()
-    done(0, 3, 6, 7, 9, 10, 11, 13, 15, 16, 17, 18)
+    done(0, 8, 9)
     for k, job in enumerate(job_up):
         job.last(into(grad_up, k))
-    done(12)
+    done(6)
 
     def write_heads(result):
         for i, ref in enumerate((grad_key, grad_query, grad_value)):
@@ -1454,13 +1444,13 @@
             ref[:, LANES:] = jnp.where(even, come, mine)
 
     job_heads.last(write_heads)
-    done(2, 4, 5)
+    done(2, 3, 4)
 
     def write_out(value):
         grad_out[...] = value.T
 
     job_out.last(write_out)
-    done(8)
+    done(5)
     three_rows = x.at[pl.ds(0, 3 * tok)]
     settle_home(pairs_in, three, out_send.at[0])
     settle_home(eight, seven, grad_send.at[0])
@@ -1485,19 +1475,45 @@
 
 
 def finish_kernel(*refs):
-    come, go, held = [refs[i * RESULTS : (i + 1) * RESULTS] for i in range(3)]
-    loads, stores = refs[3 * RESULTS :]
+    come, refs = refs[:RESULTS], refs[RESULTS:]
+    go, refs = refs[:OUTPUTS], refs[OUTPUTS:]
+    held, refs = refs[:RESULTS], refs[RESULTS:]
+    (query_bias, value_bias, conv, out_bias, first_gain, first_shift, up_bias, down_bias,
+     second_gain, second_shift, proxy, loads, stores) = refs
+    early, late = held[MATRICES:]
+    small = (query_bias, value_bias, conv, out_bias, first_gain, first_shift, up_bias, down_bias,
+             second_gain, second_shift, proxy)
+    places = (0, 1, 2, 4, 5, 8, 12, 14)
+    other = [i for i in range(OUTPUTS) if i not in places]
     copies = [
         pltpu.make_async_copy(come[i], held[i], loads.at[i]) for i in range(RESULTS)
     ]
     for copy in copies:
         copy.start()
     outs = []
-    for i in range(RESULTS):
-        copies[i].wait()
-        copy = pltpu.make_async_copy(held[i], go[i], stores.at[i])
+
+    def store(i, source):
+        copy = pltpu.make_async_copy(source, go[i], stores.at[i])
         copy.start()
         outs.append(copy)
+
+    copies[MATRICES].wait()
+    copies[MATRICES + 1].wait()
+    for ref, row in (
+        (second_gain, 0), (second_shift, 1), (down_bias, 2), (first_gain, 3), (first_shift, 4),
+        (out_bias, 5), (up_bias, 6),
+    ):
+        ref[...] = early[row]
+    proxy[...] = early[7:8, 0:1]
+    local = query_bias.shape[0]
+    query_bias[...] = late[0, :local]
+    value_bias[...] = late[1, :local]
+    conv[...] = late[2:5, :CONV]
+    for i, ref in zip(other, small):
+        store(i, ref)
+    for k, i in enumerate(places):
+        copies[k].wait()
+        store(i, held[k])
     for copy in outs:
         copy.wait()
 
@@ -1555,13 +1571,16 @@
         whole((width,), f32),
         whole((1, 1), f32),
     )
+    places = (0, 1, 2, 4, 5, 8, 12, 14)
+    parts = [results[i] for i in places]
+    sums = [whole((8, width), f32), whole((8, 2 * LANES), f32)]
     outs = pl.pallas_call(
         functools.partial(layer_kernel, n),
-        out_shape=results,
+        out_shape=(*parts, *sums),
         in_specs=[SMEM, HBM, HBM, VMEM, HBM, HBM, VMEM, VMEM, HBM, VMEM, VMEM, VMEM, HBM, VMEM, HBM,
                   VMEM, VMEM, VMEM, HBM],
         out_specs=(HBM,) * RESULTS,
-        scratch_shapes=[pltpu.VMEM(r.shape, r.dtype) for r in results]
+        scratch_shapes=[pltpu.VMEM(r.shape, r.dtype) for r in parts]
         + [
             low(rows, width), low(local, width), low(local, width), low(local, width),
             low(width, hidden), low(hidden, width), low(rows, width), low(local, width),
@@ -1609,9 +1628,10 @@
         finish_kernel,
         out_shape=results,
         in_specs=[HBM] * RESULTS,
-        out_specs=(HBM,) * RESULTS,
-        scratch_shapes=[pltpu.VMEM(r.shape, r.dtype) for r in results]
-        + [dma(RESULTS), dma(RESULTS)],
+        out_specs=(HBM,) * OUTPUTS,
+        scratch_shapes=[pltpu.VMEM(r.shape, r.dtype) for r in (*parts, *sums)]
+        + [pltpu.VMEM(results[i].shape, f32) for i in range(OUTPUTS) if i not in places]
+        + [dma(RESULTS), dma(OUTPUTS)],
         compiler_params=pltpu.CompilerParams(vmem_limit_bytes=60 * 2**20),
         name="finish",
     )(*outs)

time: 120 us -> 120 us (level)
  no operation moved by 1% of the time
where the time goes in v7:
time: 120 us; the launch traced here: 119 us
  Pallas kernels  119 us (99%)
    pallas_call x1, Pallas kernels, gathered_plan(): pl.pallas_call(functools.partial(layer_kernel, n), out_shape=(*parts, *su...  115 us
    pallas_call x1, Pallas kernels, gathered_plan(): pl.pallas_call(finish_kernel, out_shape=results, in_specs=[HBM] * RESULTS...  3.78 us

profile of v7, /device:TPU:0, one launch (start us, length us, event | category | flops | bytes accessed | tf_op | source)
XLA Modules:
  0.0 119.4 jit_solution(7121178127073361723)
XLA Ops:
  0.7 114.8 %layer.1 = (bf16[512,768]{1,0:T(8,128)(2,1)}, f32[512,768]{1,0:T(8,128)}, f32[96,192]{1,0:T(8,128)}, f32[96,192]{1,0:T(8,128)}, f32[96,192]{1,0:T(8,128)}, /*ind...) custom-call(s32[4]{0:T(128)} %lengths.1, ...), custom_call_target="tpu_custom_call" | custom-call | tf_op jit(solution)/shard_map/layer/pallas_call | solution.py:1577
  115.4 3.8 %finish.1 = (bf16[512,768]{1,0:T(8,128)(2,1)}, f32[512,768]{1,0:T(8,128)}, f32[96,192]{1,0:T(8,128)}, f32[192]{0:T(256)}, f32[96,192]{1,0:T(8,128)}, /*index=5*/...) custom-call(bf16[512,768]{1,0:T(8,128)(2,1)} %get-tuple-element.48.r, ...), custom_call_target="tpu_custom_call" | custom-call | tf_op jit(solution)/shard_map/finish/pallas_call | solution.py:1627

commit v8 on v7

--- a/solution.py
+++ b/solution.py
@@ -751,6 +751,7 @@
 MATRICES = 8
 RESULTS = MATRICES + 2
 OUTPUTS = 19
+ORDER = (4, 3, 5, 2, 6, 1, 7)
 
 
 def layer_kernel(
@@ -855,7 +856,7 @@
 
     def spread(i):
         here = pl.ds(pl.multiple_of(offsets[i] + me * tok, 16), tok)
-        for d in range(1, n):
+        for d in ORDER:
             peer = lax.rem(me + d, n)
             copy = remote(
                 stage.at[i, peer % 2, block_rows(peer // 2, tok)], owned[i].at[here],
@@ -985,7 +986,7 @@
     third_out = jnp.where(same_head, fine(third_prob, values, TN), 0.0)
     carried = fine(inverse, third_out)
 
-    for d in range(1, n + 1):
+    for d in (*ORDER, n):
         peer = lax.rem(me + d, n)
         start = pl.multiple_of(peer * tok, tok)
         nystrom = fine(k1[pl.ds(start, tok)], carried)
@@ -1195,7 +1196,7 @@
         low = block.astype(bf16)
         back_stage[i] = low.reshape(n, tok, LANES)
         back_single[i] = packed(low.reshape(n, tok, LANES))
-        for d in range(1, n):
+        for d in ORDER:
             peer = lax.rem(me + d, n)
             source, target = (back_stage, come_pair) if d % 2 == 0 else (back_single, come_single)
             remote(

time: 120 us -> 119 us (level)
  Pallas kernels: 119 us -> 117 us
where the time goes in v8:
time: 119 us; the launch traced here: 118 us
  Pallas kernels  117 us (98%)
    pallas_call x1, Pallas kernels, gathered_plan(): pl.pallas_call(functools.partial(layer_kernel, n), out_shape=(*parts, *su...  114 us
    pallas_call x1, Pallas kernels, gathered_plan(): pl.pallas_call(finish_kernel, out_shape=results, in_specs=[HBM] * RESULTS...  3.78 us

profile of v8, /device:TPU:0, one launch (start us, length us, event | category | flops | bytes accessed | tf_op | source)
XLA Modules:
  0.0 118.3 jit_solution(16746450869092868414)
XLA Ops:
  0.7 113.7 %layer.1 = (bf16[512,768]{1,0:T(8,128)(2,1)}, f32[512,768]{1,0:T(8,128)}, f32[96,192]{1,0:T(8,128)}, f32[96,192]{1,0:T(8,128)}, f32[96,192]{1,0:T(8,128)}, /*ind...) custom-call(s32[4]{0:T(128)} %lengths.1, ...), custom_call_target="tpu_custom_call" | custom-call | tf_op jit(solution)/shard_map/layer/pallas_call | solution.py:1578
  114.4 3.8 %finish.1 = (bf16[512,768]{1,0:T(8,128)(2,1)}, f32[512,768]{1,0:T(8,128)}, f32[96,192]{1,0:T(8,128)}, f32[192]{0:T(256)}, f32[96,192]{1,0:T(8,128)}, /*index=5*/...) custom-call(bf16[512,768]{1,0:T(8,128)(2,1)} %get-tuple-element.48.r, ...), custom_call_target="tpu_custom_call" | custom-call | tf_op jit(solution)/shard_map/finish/pallas_call | solution.py:1628

commit v9 on v8

--- a/solution.py
+++ b/solution.py
@@ -826,7 +826,8 @@
         (down_far, down_weight), (grad_far, out_grad),
     )):
         copy = pltpu.make_async_copy(source, target, load.at[i])
-        copy.start()
+        if i < 5:
+            copy.start()
         loads.append(copy)
     hidden_width = up_weight.shape[1]
     span = hidden_width // 2
@@ -871,6 +872,8 @@
     stage[0, 0], stage[0, 1] = paired(y.astype(bf16))
     pl.semaphore_wait(barrier, n + 2)
     spread(0)
+    for copy in loads[5:]:
+        copy.start()
     loads[2].wait()
     y = dot(x[...], wq[...], NT) + qb[...].reshape(1, local)
     stage[1, 0], stage[1, 1] = paired(y.astype(bf16))

time: 119 us -> 119 us (level)
  no operation moved by 1% of the time
where the time goes in v9:
time: 119 us; the launch traced here: 118 us
  Pallas kernels  117 us (98%)
    pallas_call x1, Pallas kernels, gathered_plan(): pl.pallas_call(functools.partial(layer_kernel, n), out_shape=(*parts, *su...  114 us
    pallas_call x1, Pallas kernels, gathered_plan(): pl.pallas_call(finish_kernel, out_shape=results, in_specs=[HBM] * RESULTS...  3.78 us

profile of v9, /device:TPU:0, one launch (start us, length us, event | category | flops | bytes accessed | tf_op | source)
XLA Modules:
  0.0 118.3 jit_solution(13800331225568592444)
XLA Ops:
  0.7 113.7 %layer.1 = (bf16[512,768]{1,0:T(8,128)(2,1)}, f32[512,768]{1,0:T(8,128)}, f32[96,192]{1,0:T(8,128)}, f32[96,192]{1,0:T(8,128)}, f32[96,192]{1,0:T(8,128)}, /*ind...) custom-call(s32[4]{0:T(128)} %lengths.1, ...), custom_call_target="tpu_custom_call" | custom-call | tf_op jit(solution)/shard_map/layer/pallas_call | solution.py:1581
  114.4 3.8 %finish.1 = (bf16[512,768]{1,0:T(8,128)(2,1)}, f32[512,768]{1,0:T(8,128)}, f32[96,192]{1,0:T(8,128)}, f32[192]{0:T(256)}, f32[96,192]{1,0:T(8,128)}, /*index=5*/...) custom-call(bf16[512,768]{1,0:T(8,128)(2,1)} %get-tuple-element.48.r, ...), custom_call_target="tpu_custom_call" | custom-call | tf_op jit(solution)/shard_map/finish/pallas_call | solution.py:1631
